TPU v7x, 32 devices: a whole 2x2x4 slice. The times are simulated.
32 devices in a mesh: parts: 32 (over z, y, x, core).
Axes of the slice: x: 2, y: 2, z: 4, core: 2. Of those that a mesh axis runs over, the one named last changes fastest.
Arguments:
- positions: float32 [3, 16384], P(None, 'parts'), may hold values from -6 to 6
- velocity: float32 [3, 16384], P(None, 'parts'), may hold values from -6 to 6
- inv_mass: float32 [16384], P('parts'), may hold values from 0.5 to 4
- swap_lists: int32 [3, 8192], P(None, 'parts'), may hold values from 0 to 511, as said below
- rim_list: int32 [4096], P('parts'), may hold values from 0 to 511, as said below
- contact_pair: int32 [2, 32768], P(None, 'parts'), may hold values from 0 to 767, as said below
- delassus: float32 [256, 128, 128], P('parts'), as said below
Outputs:
- new_velocity: float32 [3, 16384], P(None, 'parts')
- impulse: float32 [32768], P('parts')
Inputs may be any that keep to these rules, and one draw needn't show every extreme that they name: `swap_lists`: the 256 slots of one part at one level are distinct. `rim_list`: the 128 slots of one part are distinct. `contact_pair`: the first index of a contact is a local grain; the two indices differ. `delassus`: tile diagonals lie between 4 and 8.
All inputs are finite; a program needn't handle non-finite values.
Results may differ from a plain program's by a relative error of at most 0.0003.
Values sent between devices are 32-bit elements; how exact they have to be, the bound alone decides.
No kernel may reach another device: no remote copies, remote signals or barrier semaphores. Data moves between devices by JAX's collectives and lax.ppermute only.
A program may use at most 64 MiB of HBM per device.

v0:
```python
import jax
import jax.numpy as jnp
from jax import lax
from jax.sharding import PartitionSpec as P

TILE = 128
LEVELS = 3
ITERS = 2


def partner(value, axis, apart):
    mask = 2**apart
    pairs = [(source, source ^ mask) for source in range(lax.axis_size(axis))]
    return lax.ppermute(value, axis, pairs)


def with_halo(x, sides, width):
    for axis, dim in sides:
        size, length = (lax.axis_size(axis), x.shape[dim])
        up = [(i, (i + 1) % size) for i in range(size - 1)]
        down = [(j, i) for i, j in up]
        last = lax.slice_in_dim(x, length - width, length, axis=dim)
        first = lax.slice_in_dim(x, 0, width, axis=dim)
        before = lax.ppermute(last, axis, up)
        after = lax.ppermute(first, axis, down)
        x = jnp.concatenate([before, x, after], axis=dim)
    return x


def selector(slots, extent):
    return (slots[:, None] == jnp.arange(extent, dtype=jnp.int32)[None, :]).astype(jnp.float32)


def pick(field, table):
    return lax.dot_general(
        field,
        table,
        (((1,), (1,)), ((), ())),
        precision=lax.Precision.HIGHEST,
        preferred_element_type=jnp.float32,
    )


def spread(values, table):
    return jnp.dot(
        values, table, precision=lax.Precision.HIGHEST, preferred_element_type=jnp.float32
    )


def attach(field, halo_rows, width):
    return jnp.concatenate([field, halo_rows[:, :width], halo_rows[:, 2 * width :]], axis=1)


def body(positions, velocity, inv_mass, swap_lists, rim_list, contact_pair, delassus):
    grains = positions.shape[1]
    width = rim_list.shape[0]
    contacts = contact_pair.shape[1]
    tiles = delassus.shape[0]
    extent = grains + 2 * width
    bits = lax.axis_size("parts").bit_length() - 1
    state = jnp.concatenate([positions, velocity, inv_mass[None]], axis=0)
    for level in range(LEVELS):
        table = selector(swap_lists[level], grains)
        arrived = partner(pick(state, table), "parts", bits - 1 - level)
        keep_mask = 1.0 - jnp.sum(table, axis=0)
        state = state * keep_mask[None] + spread(arrived, table)
    vel = state[3:6]
    mass = state[6]
    rim_table = selector(rim_list, grains)
    first_table = selector(contact_pair[0], extent)
    second_table = selector(contact_pair[1], extent)
    neighbour = with_halo(pick(state[0:6], rim_table), (("parts", 1),), width)
    extended = attach(state[0:6], neighbour, width)
    ends = pick(extended, first_table) - pick(extended, second_table)
    normal = ends[0:3]
    relative = ends[3:6]
    diag = jnp.diagonal(delassus, axis1=1, axis2=2).reshape(contacts)
    lam = jnp.zeros((contacts,), jnp.float32)
    current = vel
    for step in range(ITERS):
        if step > 0:
            fresh = with_halo(pick(current, rim_table), (("parts", 1),), width)
            ext_vel = attach(current, fresh, width)
            relative = pick(ext_vel, first_table) - pick(ext_vel, second_table)
        speed = jnp.sum(normal * relative, axis=0)
        coupled = jnp.einsum(
            "tij,tj->ti", delassus, lam.reshape(tiles, TILE), precision=lax.Precision.HIGHEST
        ).reshape(contacts)
        lam = jnp.maximum(0.0, lam - (coupled + speed) / diag)
        force = normal * lam[None]
        partial_value = spread(force, first_table) - spread(force, second_table)
        shared = with_halo(partial_value[:, grains:], (("parts", 1),), width)
        incoming = shared[:, :width] + shared[:, 3 * width :]
        local = partial_value[:, :grains] + spread(incoming, rim_table)
        current = vel + mass[None] * local
    return (current, lam)


def solution(mesh):
    in_specs = (
        P(None, "parts"),
        P(None, "parts"),
        P("parts"),
        P(None, "parts"),
        P("parts"),
        P(None, "parts"),
        P("parts", None, None),
    )
    out_specs = (P(None, "parts"), P("parts"))
    return jax.shard_map(body, mesh=mesh, in_specs=in_specs, out_specs=out_specs, check_vma=False)
```

profile of v0, /device:TPU:23, one launch (start us, length us, event | category | flops | bytes accessed | tf_op | source)
XLA Modules:
  0.0 73.7 jit_solution(6995765113428559350)
XLA Ops:
  0.6 0.8 %fusion.71 = (s32[1,256]{1,0:T(1,128)S(1)}, s32[1,256]{1,0:T(1,128)S(1)}, s32[1,256]{1,0:T(1,128)S(1)}) fusion(s32[3,256]{1,0:T(4,128)} %param.10), kind=kLoop, calls=%fused_computation.99 | loop fusion | bytes 6144 | tf_op jit(solution)/shard_map/slice | solution.py:63
  1.4 1.1 %fusion.30 = f32[7,256]{1,0:T(8,128)S(1)} fusion(s32[256]{0:T(256)S(1)} %bitcast.52, f32[1,512]{1,0:T(1,128)} %bitcast.67, f32[3,512]{1,0:T(4,128)} %param.8, f32[3,512]{1,0:T(4,128)} %param.7), kind=kOutput, calls=%fused_computation.43 | convolution fusion | flops 11148288 | bytes 22528 | tf_op jit(solution)/shard_map/dot_general | solution.py:35
  2.6 0.1 collective-permute-start
  2.6 0.1 convert_reduce_fusion.2
  2.8 0.8 %fusion.70 = (s32[1,1024]{1,0:T(1,128)S(1)}, s32[1,1024]{1,0:T(1,128)S(1)}) fusion(s32[2,1024]{1,0:T(2,128)} %param.12), kind=kLoop, calls=%fused_computation.98 | loop fusion | bytes 16384 | tf_op jit(solution)/shard_map/slice | solution.py:70
  3.5 0.1 convert_reduce_fusion
  3.7 0.1 convert_reduce_fusion.1
  3.8 2.1 %collective-permute-done = f32[7,256]{1,0:T(8,128)S(1)} collective-permute-done((f32[7,256]{1,0:T(8,128)S(1)}, f32[7,256]{1,0:T(8,128)S(1)}, u32[]{:S(2)}, u32[]{:S(2)}) %collective-permute-start) | collective-permute-done | bytes 7200 | tf_op jit(solution)/shard_map/ppermute | solution.py:14
  6.0 1.1 %convolution_add_fusion = f32[7,512]{1,0:T(8,128)S(1)} fusion(f32[7,256]{1,0:T(8,128)S(1)} %collective-permute-done, s32[256]{0:T(256)S(1)} %bitcast.54, f32[1,512]{1,0:T(1,128)} %bitcast.68, f32[3,512]{1,0:T(4,128)} %param.8, f32[3,512]{1,0:T(4,128)} %param.7, f32[512]{0:T(512)S(1)} %broadcast_subtract_fusion.2), kind=kOutput, calls=%fused_computation.22 | convolution fusion | flops 11155456 | bytes 38912 | tf_op jit(solution)/shard_map/dot_general | solution.py:45
  7.0 0.4 fusion.29
  7.4 1.3 %collective-permute-start.1 = (f32[7,256]{1,0:T(8,128)S(1)}, f32[7,256]{1,0:T(8,128)S(1)}, u32[]{:S(2)}, u32[]{:S(2)}) collective-permute-start(f32[7,256]{1,0:T(8,128)S(1)} %fusion.29), channel_id=1, source_target_pairs={{0,8},{1,9},{2,10},{3,11},{4,12},{5,13},{6,14},{7,15},{8,0},{9,1},... | collective-permute-start | bytes 21512 | tf_op jit(solution)/shard_map/ppermute | solution.py:14
  8.8 1.2 %collective-permute-done.1 = f32[7,256]{1,0:T(8,128)S(1)} collective-permute-done((f32[7,256]{1,0:T(8,128)S(1)}, f32[7,256]{1,0:T(8,128)S(1)}, u32[]{:S(2)}, u32[]{:S(2)}) %collective-permute-start.1) | collective-permute-done | bytes 7200 | tf_op jit(solution)/shard_map/ppermute | solution.py:14
  10.0 0.3 fusion.28
  10.3 0.4 fusion.27
  10.7 0.2 collective-permute-start.2
  10.9 1.2 %multiply_reduce_fusion = f32[8,128]{1,0:T(8,128)S(1)} fusion(f32[8,128,128]{2,1,0:T(8,128)} %param.13), kind=kLoop, calls=%fused_computation.32 | loop fusion | flops 261120 | bytes 528384 | tf_op jit(solution)/shard_map/tij,tj->ti/dot_general | solution.py:86
  12.2 1.0 %collective-permute-done.2 = f32[7,256]{1,0:T(8,128)S(1)} collective-permute-done((f32[7,256]{1,0:T(8,128)S(1)}, f32[7,256]{1,0:T(8,128)S(1)}, u32[]{:S(2)}, u32[]{:S(2)}) %collective-permute-start.2) | collective-permute-done | bytes 7200 | tf_op jit(solution)/shard_map/ppermute | solution.py:14
  13.2 0.3 multiply_add_fusion
  13.5 0.9 %fusion.32 = f32[6,128]{1,0:T(8,128)S(1)} fusion(s32[128]{0:T(128)} %param.11, f32[7,512]{1,0:T(8,128)S(1)} %multiply_add_fusion), kind=kOutput, calls=%fused_computation.46 | convolution fusion | flops 4784128 | bytes 17920 | tf_op jit(solution)/shard_map/dot_general | solution.py:35
  14.4 6.1 %collective-permute-start.4 = (f32[6,128]{1,0:T(8,128)S(1)}, f32[6,128]{1,0:T(8,128)S(1)}, u32[]{:S(2)}, u32[]{:S(2)}) collective-permute-start(f32[6,128]{1,0:T(8,128)S(1)} %fusion.32), channel_id=1, source_target_pairs={{1,0},{2,1},{3,2},{4,3},{5,4},{6,5},{7,6},{8,7},{9,8},{10,9},{11,1... | collective-permute-start | bytes 9224 | tf_op jit(solution)/shard_map/ppermute | solution.py:25
  20.5 3.0 %collective-permute-start.3 = (f32[6,128]{1,0:T(8,128)S(1)}, f32[6,128]{1,0:T(8,128)S(1)}, u32[]{:S(2)}, u32[]{:S(2)}) collective-permute-start(f32[6,128]{1,0:T(8,128)S(1)} %fusion.32), channel_id=1, source_target_pairs={{0,1},{1,2},{2,3},{3,4},{4,5},{5,6},{6,7},{7,8},{8,9},{9,10},{10,1... | collective-permute-start | bytes 9224 | tf_op jit(solution)/shard_map/ppermute | solution.py:24
  23.6 5.9 %copy.15 = f32[8,128,128]{0,2,1:T(8,128)} copy(f32[8,128,128]{2,1,0:T(8,128)} %param.13) | data formatting | bytes 1048576 | tf_op args[6]
  29.4 0.0 copy-start.2
  29.4 0.0 copy-start
  29.4 1.8 %gather_fusion = f32[128,8]{1,0:T(8,128)S(1)} fusion(f32[8,128,128]{0,2,1:T(8,128)} %copy.15, s32[128]{0:T(128)S(1)} %or_bitcast_fusion), kind=kCustom, calls=%fused_computation | custom fusion | bytes 9216 | tf_op jit(solution)/shard_map/jit(diagonal)/gather | solution.py:77
  31.2 0.1 copy.22
  31.4 0.0 collective-permute-done.4
  31.4 0.0 collective-permute-done.3
  31.4 1.5 %fusion.3 = f32[6,1024]{1,0:T(8,128)S(1)} fusion(s32[1024]{0:T(1024)S(1)} %bitcast.59, f32[6,128]{1,0:T(8,128)S(1)} %collective-permute-done.4, f32[6,128]{1,0:T(8,128)S(1)} %collective-permute-done.3, f32[6,512]{1,0:T(8,128)S(1)} %bitcast.65), kind=kOutput, calls=%fused_computation.5 | convolution fusion | flops 57418752 | bytes 47104 | tf_op jit(solution)/shard_map/dot_general | solution.py:35
  32.9 1.6 %fusion.16 = f32[6,1024]{1,0:T(8,128)S(1)} fusion(f32[6,1024]{1,0:T(8,128)S(1)} %fusion.3, s32[1024]{0:T(1024)S(1)} %bitcast.55, f32[6,128]{1,0:T(8,128)S(1)} %collective-permute-done.4, f32[6,128]{1,0:T(8,128)S(1)} %collective-permute-done.3, f32[6,512]{1,0:T(8,128)S(1)} %bitcast.66), kind=kOutput, calls=%fused_computation.19 | convolution fusion | flops 57424896 | bytes 71680 | tf_op jit(solution)/shard_map/dot_general | solution.py:35
  34.5 0.1 copy.17
  34.6 1.1 %fusion.2 = f32[3,768]{1,0:T(4,128)S(1)} fusion(s32[1024]{0:T(1024)S(1)} %bitcast.60, f32[1024]{0:T(1024)S(1)} %fusion.57, f32[6,1024]{1,0:T(8,128)S(1)} %fusion.16), kind=kOutput, calls=%fused_computation.4 | convolution fusion | flops 29101056 | bytes 33792 | tf_op jit(solution)/shard_map/dot_general | solution.py:45
  35.8 1.1 %fusion.19 = f32[3,768]{1,0:T(4,128)S(1)} fusion(f32[3,768]{1,0:T(4,128)S(1)} %fusion.2, s32[1024]{0:T(1024)S(1)} %bitcast.56, f32[1024]{0:T(1024)S(1)} %fusion.57, f32[6,1024]{1,0:T(8,128)S(1)} %fusion.16), kind=kOutput, calls=%fused_computation.23 | convolution fusion | flops 29103360 | bytes 46080 | tf_op jit(solution)/shard_map/dot_general | solution.py:45
  36.9 2.4 %collective-permute-start.5 = (f32[3,128]{1,0:T(4,128)S(1)}, f32[3,128]{1,0:T(4,128)S(1)}, u32[]{:S(2)}, u32[]{:S(2)}) collective-permute-start(f32[3,128]{1,0:T(4,128)S(1)} %get-tuple-element.5), channel_id=1, source_target_pairs={{0,1},{1,2},{2,3},{3,4},{4,5},{5,6},{6,7},{7,8},{8,9},{9,10},{10,1... | collective-permute-start | bytes 4616 | tf_op jit(solution)/shard_map/ppermute | solution.py:24
  39.3 1.9 %collective-permute-start.6 = (f32[3,128]{1,0:T(4,128)S(1)}, f32[3,128]{1,0:T(4,128)S(1)}, u32[]{:S(2)}, u32[]{:S(2)}) collective-permute-start(f32[3,128]{1,0:T(4,128)S(1)} %get-tuple-element.4), channel_id=1, source_target_pairs={{1,0},{2,1},{3,2},{4,3},{5,4},{6,5},{7,6},{8,7},{9,8},{10,9},{11,1... | collective-permute-start | bytes 4616 | tf_op jit(solution)/shard_map/ppermute | solution.py:25
  41.3 0.0 collective-permute-done.5
  41.3 4.7 %collective-permute-done.6 = f32[3,128]{1,0:T(4,128)S(1)} collective-permute-done((f32[3,128]{1,0:T(4,128)S(1)}, f32[3,128]{1,0:T(4,128)S(1)}, u32[]{:S(2)}, u32[]{:S(2)}) %collective-permute-start.6) | collective-permute-done | bytes 1568 | tf_op jit(solution)/shard_map/ppermute | solution.py:25
  46.0 0.0 copy-done.2
  46.0 0.3 fusion.25
  46.3 0.2 fusion.31
  46.5 2.0 %collective-permute-start.8 = (f32[3,128]{1,0:T(4,128)S(1)}, f32[3,128]{1,0:T(4,128)S(1)}, u32[]{:S(2)}, u32[]{:S(2)}) collective-permute-start(f32[3,128]{1,0:T(4,128)S(1)} %fusion.31), channel_id=1, source_target_pairs={{1,0},{2,1},{3,2},{4,3},{5,4},{6,5},{7,6},{8,7},{9,8},{10,9},{11,1... | collective-permute-start | bytes 4616 | tf_op jit(solution)/shard_map/ppermute | solution.py:25
  48.5 5.6 %collective-permute-start.7 = (f32[3,128]{1,0:T(4,128)S(1)}, f32[3,128]{1,0:T(4,128)S(1)}, u32[]{:S(2)}, u32[]{:S(2)}) collective-permute-start(f32[3,128]{1,0:T(4,128)S(1)} %fusion.31), channel_id=1, source_target_pairs={{0,1},{1,2},{2,3},{3,4},{4,5},{5,6},{6,7},{7,8},{8,9},{9,10},{10,1... | collective-permute-start | bytes 4616 | tf_op jit(solution)/shard_map/ppermute | solution.py:24
  54.1 0.0 copy-done
  54.1 0.9 %fusion.72 = f32[8,1,128]{2,1,0:T(1,128)S(1)} fusion(f32[8,128,1]{1,2,0:T(1,128)S(1)} %copy.23, f32[8,128,128]{2,1,0:T(8,128)S(1)} %copy-done), kind=kOutput, calls=%fused_computation.100 | convolution fusion | flops 1572864 | bytes 532480 | tf_op jit(solution)/shard_map/tij,tj->ti/dot_general | solution.py:86
  55.1 0.0 collective-permute-done.8
  55.1 0.0 collective-permute-done.7
  55.1 1.6 %fusion.1 = f32[3,1024]{1,0:T(4,128)S(1)} fusion(s32[1024]{0:T(1024)S(1)} %bitcast.61, f32[3,128]{1,0:T(4,128)S(1)} %collective-permute-done.8, f32[3,128]{1,0:T(4,128)S(1)} %collective-permute-done.7, f32[3,512]{1,0:T(4,128)S(1)} %fusion.25), kind=kOutput, calls=%fused_computation.3 | convolution fusion | flops 29102592 | bytes 25600 | tf_op jit(solution)/shard_map/dot_general | solution.py:35
  56.6 1.6 %fusion.21 = f32[1024]{0:T(1024)S(1)} fusion(f32[3,1024]{1,0:T(4,128)S(1)} %fusion.1, s32[1024]{0:T(1024)S(1)} %bitcast.57, f32[6,1024]{1,0:T(8,128)S(1)} %fusion.16, f32[3,128]{1,0:T(4,128)S(1)} %collective-permute-done.8, f32[3,128]{1,0:T(4,128)S(1)} %collective-permute-done.7, f32[3,512]{1,0:T(4,128)S(1)} %fusion.25), kind=kOutput, calls=%fused_computation.25 | convolution fusion | flops 29110784 | bytes 41984 | tf_op jit(solution)/shard_map/dot_general | solution.py:35
  58.2 0.0 copy-start.1
  58.2 1.1 %fusion = f32[3,768]{1,0:T(4,128)S(1)} fusion(s32[1024]{0:T(1024)S(1)} %bitcast.62, f32[1024]{0:T(1024)S(1)} %fusion.59, f32[6,1024]{1,0:T(8,128)S(1)} %fusion.16), kind=kOutput, calls=%fused_computation.2 | convolution fusion | flops 29101056 | bytes 33792 | tf_op jit(solution)/shard_map/dot_general | solution.py:45
  59.4 1.1 %fusion.20 = f32[3,768]{1,0:T(4,128)S(1)} fusion(f32[3,768]{1,0:T(4,128)S(1)} %fusion, s32[1024]{0:T(1024)S(1)} %bitcast.58, f32[1024]{0:T(1024)S(1)} %fusion.59, f32[6,1024]{1,0:T(8,128)S(1)} %fusion.16), kind=kOutput, calls=%fused_computation.24 | convolution fusion | flops 29103360 | bytes 46080 | tf_op jit(solution)/shard_map/dot_general | solution.py:45
  60.5 5.6 %collective-permute-start.9 = (f32[3,128]{1,0:T(4,128)S(1)}, f32[3,128]{1,0:T(4,128)S(1)}, u32[]{:S(2)}, u32[]{:S(2)}) collective-permute-start(f32[3,128]{1,0:T(4,128)S(1)} %get-tuple-element.3), channel_id=1, source_target_pairs={{0,1},{1,2},{2,3},{3,4},{4,5},{5,6},{6,7},{7,8},{8,9},{9,10},{10,1... | collective-permute-start | bytes 4616 | tf_op jit(solution)/shard_map/ppermute | solution.py:24
  66.1 1.9 %collective-permute-start.10 = (f32[3,128]{1,0:T(4,128)S(1)}, f32[3,128]{1,0:T(4,128)S(1)}, u32[]{:S(2)}, u32[]{:S(2)}) collective-permute-start(f32[3,128]{1,0:T(4,128)S(1)} %get-tuple-element.2), channel_id=1, source_target_pairs={{1,0},{2,1},{3,2},{4,3},{5,4},{6,5},{7,6},{8,7},{9,8},{10,9},{11,1... | collective-permute-start | bytes 4616 | tf_op jit(solution)/shard_map/ppermute | solution.py:25
  68.0 0.0 collective-permute-done.9
  68.0 4.8 %collective-permute-done.10 = f32[3,128]{1,0:T(4,128)S(1)} collective-permute-done((f32[3,128]{1,0:T(4,128)S(1)}, f32[3,128]{1,0:T(4,128)S(1)}, u32[]{:S(2)}, u32[]{:S(2)}) %collective-permute-start.10) | collective-permute-done | bytes 1568 | tf_op jit(solution)/shard_map/ppermute | solution.py:25
  72.8 0.9 %fusion.23 = f32[3,512]{1,0:T(4,128)} fusion(s32[128]{0:T(128)S(1)} %copy-done.2, f32[3,768]{1,0:T(4,128)S(1)} %fusion.20, f32[7,512]{1,0:T(8,128)S(1)} %multiply_add_fusion, f32[512]{0:T(512)S(1)} %bitcast.64, f32[3,128]{1,0:T(4,128)S(1)} %collective-permute-done.9, f32[3,128]{1,0:T(4,128)S(1)} %collective-permute-done.10), kind=kOutput, calls=%fused_computation.28 | convolution fusion | flops 2429824 | bytes 24064 | tf_op jit(solution)/shard_map/dot_general | solution.py:45
  73.7 0.0 copy-done.1
  (13 shorter events, 0.2 us)
Async XLA Ops:
  2.6 3.4 %collective-permute-start = (f32[7,256]{1,0:T(8,128)S(1)}, f32[7,256]{1,0:T(8,128)S(1)}, u32[]{:S(2)}, u32[]{:S(2)}) collective-permute-start(f32[7,256]{1,0:T(8,128)S(1)} %fusion.30), channel_id=1, source_target_pairs={{0,16},{1,17},{2,18},{3,19},{4,20},{5,21},{6,22},{7,23},{8,24},{9,... | collective-permute-start | bytes 21512 | tf_op jit(solution)/shard_map/ppermute | solution.py:14
  7.4 2.5 %collective-permute-start.1 = (f32[7,256]{1,0:T(8,128)S(1)}, f32[7,256]{1,0:T(8,128)S(1)}, u32[]{:S(2)}, u32[]{:S(2)}) collective-permute-start(f32[7,256]{1,0:T(8,128)S(1)} %fusion.29), channel_id=1, source_target_pairs={{0,8},{1,9},{2,10},{3,11},{4,12},{5,13},{6,14},{7,15},{8,0},{9,1},... | collective-permute-start | bytes 21512 | tf_op jit(solution)/shard_map/ppermute | solution.py:14
  10.7 2.5 %collective-permute-start.2 = (f32[7,256]{1,0:T(8,128)S(1)}, f32[7,256]{1,0:T(8,128)S(1)}, u32[]{:S(2)}, u32[]{:S(2)}) collective-permute-start(f32[7,256]{1,0:T(8,128)S(1)} %fusion.27), channel_id=1, source_target_pairs={{0,4},{1,5},{2,6},{3,7},{4,0},{5,1},{6,2},{7,3},{8,12},{9,13},{10,... | collective-permute-start | bytes 21512 | tf_op jit(solution)/shard_map/ppermute | solution.py:14
  14.4 16.9 %collective-permute-start.4 = (f32[6,128]{1,0:T(8,128)S(1)}, f32[6,128]{1,0:T(8,128)S(1)}, u32[]{:S(2)}, u32[]{:S(2)}) collective-permute-start(f32[6,128]{1,0:T(8,128)S(1)} %fusion.32), channel_id=1, source_target_pairs={{1,0},{2,1},{3,2},{4,3},{5,4},{6,5},{7,6},{8,7},{9,8},{10,9},{11,1... | collective-permute-start | bytes 9224 | tf_op jit(solution)/shard_map/ppermute | solution.py:25
  20.5 10.8 %collective-permute-start.3 = (f32[6,128]{1,0:T(8,128)S(1)}, f32[6,128]{1,0:T(8,128)S(1)}, u32[]{:S(2)}, u32[]{:S(2)}) collective-permute-start(f32[6,128]{1,0:T(8,128)S(1)} %fusion.32), channel_id=1, source_target_pairs={{0,1},{1,2},{2,3},{3,4},{4,5},{5,6},{6,7},{7,8},{8,9},{9,10},{10,1... | collective-permute-start | bytes 9224 | tf_op jit(solution)/shard_map/ppermute | solution.py:24
  29.4 16.6 %copy-start.2 = (s32[128]{0:T(128)S(1)}, s32[128]{0:T(128)}, u32[]{:S(2)}) copy-start(s32[128]{0:T(128)} %param.11) | copy-start | bytes 1540
  29.4 24.7 %copy-start = (f32[8,128,128]{2,1,0:T(8,128)S(1)}, f32[8,128,128]{2,1,0:T(8,128)}, u32[]{:S(2)}) copy-start(f32[8,128,128]{2,1,0:T(8,128)} %param.13) | copy-start | bytes 1572868
  36.9 4.4 %collective-permute-start.5 = (f32[3,128]{1,0:T(4,128)S(1)}, f32[3,128]{1,0:T(4,128)S(1)}, u32[]{:S(2)}, u32[]{:S(2)}) collective-permute-start(f32[3,128]{1,0:T(4,128)S(1)} %get-tuple-element.5), channel_id=1, source_target_pairs={{0,1},{1,2},{2,3},{3,4},{4,5},{5,6},{6,7},{7,8},{8,9},{9,10},{10,1... | collective-permute-start | bytes 4616 | tf_op jit(solution)/shard_map/ppermute | solution.py:24
  39.3 6.7 %collective-permute-start.6 = (f32[3,128]{1,0:T(4,128)S(1)}, f32[3,128]{1,0:T(4,128)S(1)}, u32[]{:S(2)}, u32[]{:S(2)}) collective-permute-start(f32[3,128]{1,0:T(4,128)S(1)} %get-tuple-element.4), channel_id=1, source_target_pairs={{1,0},{2,1},{3,2},{4,3},{5,4},{6,5},{7,6},{8,7},{9,8},{10,9},{11,1... | collective-permute-start | bytes 4616 | tf_op jit(solution)/shard_map/ppermute | solution.py:25
  46.5 8.6 %collective-permute-start.8 = (f32[3,128]{1,0:T(4,128)S(1)}, f32[3,128]{1,0:T(4,128)S(1)}, u32[]{:S(2)}, u32[]{:S(2)}) collective-permute-start(f32[3,128]{1,0:T(4,128)S(1)} %fusion.31), channel_id=1, source_target_pairs={{1,0},{2,1},{3,2},{4,3},{5,4},{6,5},{7,6},{8,7},{9,8},{10,9},{11,1... | collective-permute-start | bytes 4616 | tf_op jit(solution)/shard_map/ppermute | solution.py:25
  48.5 6.6 %collective-permute-start.7 = (f32[3,128]{1,0:T(4,128)S(1)}, f32[3,128]{1,0:T(4,128)S(1)}, u32[]{:S(2)}, u32[]{:S(2)}) collective-permute-start(f32[3,128]{1,0:T(4,128)S(1)} %fusion.31), channel_id=1, source_target_pairs={{0,1},{1,2},{2,3},{3,4},{4,5},{5,6},{6,7},{7,8},{8,9},{9,10},{10,1... | collective-permute-start | bytes 4616 | tf_op jit(solution)/shard_map/ppermute | solution.py:24
  58.2 15.4 %copy-start.1 = (f32[1024]{0:T(1024)}, f32[1024]{0:T(1024)S(1)}, u32[]{:S(2)}) copy-start(f32[1024]{0:T(1024)S(1)} %fusion.59) | copy-start | bytes 12292
  60.5 7.5 %collective-permute-start.9 = (f32[3,128]{1,0:T(4,128)S(1)}, f32[3,128]{1,0:T(4,128)S(1)}, u32[]{:S(2)}, u32[]{:S(2)}) collective-permute-start(f32[3,128]{1,0:T(4,128)S(1)} %get-tuple-element.3), channel_id=1, source_target_pairs={{0,1},{1,2},{2,3},{3,4},{4,5},{5,6},{6,7},{7,8},{8,9},{9,10},{10,1... | collective-permute-start | bytes 4616 | tf_op jit(solution)/shard_map/ppermute | solution.py:24
  66.1 6.7 %collective-permute-start.10 = (f32[3,128]{1,0:T(4,128)S(1)}, f32[3,128]{1,0:T(4,128)S(1)}, u32[]{:S(2)}, u32[]{:S(2)}) collective-permute-start(f32[3,128]{1,0:T(4,128)S(1)} %get-tuple-element.2), channel_id=1, source_target_pairs={{1,0},{2,1},{3,2},{4,3},{5,4},{6,5},{7,6},{8,7},{9,8},{10,9},{11,1... | collective-permute-start | bytes 4616 | tf_op jit(solution)/shard_map/ppermute | solution.py:25
where the time goes:
time: 74.3 us; the launch traced here: 73.7 us
  starting transfers between devices  30.2 us (41%)
  matrix products  17.6 us (24%)
  waiting for transfers between devices  13.8 us (19%)
  local copies, waits for them, and re-layouts  9.54 us (13%)
  other arithmetic  1.73 us (2%)
  between operations  0.84 us (1%)
    ppermute x4, starting transfers between devices, with_halo(): before = lax.ppermute(last, axis, up)  16.6 us
    ppermute x4, starting transfers between devices, with_halo(): after = lax.ppermute(first, axis, down)  11.9 us
    ppermute x4, waiting for transfers between devices, with_halo(): after = lax.ppermute(first, axis, down)  9.46 us
    dot_general x9, matrix products, pick(): lax.dot_general(field, table, (((1,), (1,)), ((), ())), precision=lax.Pre...  9.26 us
    dot_general x9, matrix products, spread(): jnp.dot(values, table, precision=lax.Precision.HIGHEST, preferred_element...  7.38 us
    unnamed x7, local copies, waits for them, and re-layouts  5.87 us
    ppermute x3, waiting for transfers between devices, partner(): return lax.ppermute(value, axis, pairs)  4.37 us
    gather x2, local copies, waits for them, and re-layouts, body(): diag = jnp.diagonal(delassus, axis1=1, axis2=2).reshape(contacts)  1.8 us
  transfers between devices with their start and end apart: 11, of which 5 were waited for; matrix products, arithmetic and copies ran while one was open for 15% of the time, Pallas kernels for 0%

commit v1 on v0

v1 whole, which is shorter than its diff:
```python
import functools

import jax
import jax.numpy as jnp
from jax import lax
from jax.experimental import pallas as pl
from jax.experimental.pallas import tpu as pltpu
from jax.sharding import PartitionSpec as P

TILE = 128
LEVELS = 3
GROUP = 2**LEVELS
REACH = 4
FIELDS = 8
CHUNKS = 4
EXT_CHUNKS = 6
RIM_AT = 7
FIRST_AT = 32
SECOND_AT = 40
DIAG_AT = 48
RECORD = 56
LISTS_AT = 32
RAW = 40
FIXED = RECORD - FIRST_AT
BLOCK = 4
PARAMS = pltpu.CompilerParams(vmem_limit_bytes=32 * 2**20)
FROM_HBM = pltpu.CompilerParams(vmem_limit_bytes=63 * 2**20)
NT = (((1,), (1,)), ((), ()))


def rows_iota(shape):
    return lax.broadcasted_iota(jnp.int32, shape, 0)


def lanes_iota(shape):
    return lax.broadcasted_iota(jnp.int32, shape, 1)


def wide(row):
    return jnp.broadcast_to(row, (FIELDS, TILE))


def take(table, lane):
    return jnp.take_along_axis(table, lane, axis=1, mode="promise_in_bounds")


def look_up(rows, index):
    lane, high = index & (TILE - 1), index >> 7
    found = take(wide(rows[0]), lane)
    for h in range(1, len(rows)):
        found = jnp.where(high == h, take(wide(rows[h]), lane), found)
    return found


def one_hot(low_row):
    return (rows_iota((TILE, TILE)) == low_row).astype(jnp.float32).astype(jnp.bfloat16)


def inverse(slot_rows):
    left, right = [], []
    for at, row in enumerate(slot_rows):
        slots = row.astype(jnp.int32)
        place = (lanes_iota((FIELDS, TILE)) + (at * TILE + 1)).astype(jnp.float32)
        heads = jnp.where(wide(slots >> 7) == rows_iota((FIELDS, TILE)), place, 0.0)
        left.append(heads.astype(jnp.bfloat16))
        right.append(one_hot(slots & (TILE - 1)))
    total = lax.dot_general(
        jnp.concatenate(left, axis=1),
        jnp.concatenate(right, axis=1),
        NT,
        preferred_element_type=jnp.float32,
    )
    return total.astype(jnp.int32)


def pack_kernel(*refs):
    sources, out, held, sems = refs[:5], refs[5], refs[6:11], refs[11]
    copies = [
        pltpu.make_async_copy(source, target, sems.at[k])
        for k, (source, target) in enumerate(zip(sources, held))
    ]
    for copy in copies:
        copy.start()
    pos, vel, mass, lists, rim = held
    for copy in copies:
        copy.wait()
    first = out.at[0]
    for c in range(CHUNKS):
        lanes = pl.ds(c * TILE, TILE)
        first[pl.ds(FIELDS * c, 3), :] = pos[:, lanes]
        first[pl.ds(FIELDS * c + 3, 3), :] = vel[:, lanes]
        first[pl.ds(FIELDS * c + 6, 1), :] = mass[pl.ds(c, 1), :]
        spare = rim[...].astype(jnp.float32) if c == 0 else jnp.zeros((1, TILE), jnp.float32)
        first[pl.ds(FIELDS * c + 7, 1), :] = spare
    for level in range(LEVELS):
        for h in range(2):
            row = lists[pl.ds(level, 1), pl.ds(h * TILE, TILE)]
            first[pl.ds(LISTS_AT + 2 * level + h, 1), :] = row.astype(jnp.float32)
    first[pl.ds(LISTS_AT + 2 * LEVELS, 2), :] = jnp.zeros((2, TILE), jnp.float32)
    whole = first[...]
    for m in range(1, GROUP):
        out[m] = whole


def fixed_kernel(pair, tiles, out):
    eye = rows_iota((TILE, TILE)) == lanes_iota((TILE, TILE))
    for t in range(tiles.shape[0]):
        lanes = pl.ds(t * TILE, TILE)
        out[pl.ds(t, 1), :] = pair[pl.ds(0, 1), lanes].astype(jnp.float32)
        out[pl.ds(FIELDS + t, 1), :] = pair[pl.ds(1, 1), lanes].astype(jnp.float32)
        diag = jnp.sum(jnp.where(eye, tiles[t], 0.0), axis=0, keepdims=True)
        out[pl.ds(2 * FIELDS + t, 1), :] = diag


def compose_kernel(stride, raw, own):
    member = lax.axis_index("parts") // stride

    def list_rows(part, level):
        return [raw[part, pl.ds(LISTS_AT + 2 * level + h, 1), :] for h in range(2)]

    def table_rows(table):
        return [table[h : h + 1] for h in range(CHUNKS)]

    aims = [(member + which + (GROUP - 1)) % GROUP for which in range(3)]
    zero = jnp.zeros((FIELDS, TILE), jnp.int32)
    backs = {
        (which, x, level): table_rows(inverse(list_rows(aim ^ x, level)))
        for level in reversed(range(LEVELS))
        for x in range(2 ** (LEVELS - 1 - level))
        for which, aim in enumerate(aims)
    }
    slots = [rows_iota((FIELDS, TILE)) % CHUNKS * TILE + lanes_iota((FIELDS, TILE))] * 3
    shifts = [zero] * 3
    for level in reversed(range(LEVELS)):
        bit = GROUP >> (level + 1)
        candidates = range(2 ** (LEVELS - 1 - level))
        for which, aim in enumerate(aims):
            slot, shift = slots[which], shifts[which]
            place = zero
            for x in candidates:
                found = look_up(backs[which, x, level], slot)
                place = jnp.where(shift == x, found, place) if x else found
            moved = place > 0
            place = jnp.maximum(place - 1, 0)
            for x in candidates:
                found = look_up(list_rows(aim ^ x ^ bit, level), place).astype(jnp.int32)
                slot = jnp.where(moved & (shift == x), found, slot)
            slots[which] = slot
            shifts[which] = jnp.where(moved, shift + bit, shift)
    for which, aim in enumerate(aims):
        there = (member + which >= 1) & (member + which <= GROUP)
        lane = slots[which] & (TILE - 1)
        block = shifts[which] * CHUNKS + (slots[which] >> 7)
        lanes = [wide(lane[c : c + 1]) for c in range(CHUNKS)]
        blocks = [wide(block[c : c + 1]) for c in range(CHUNKS)]
        found = [jnp.zeros((FIELDS, TILE), jnp.float32)] * CHUNKS
        for x in range(GROUP):
            for h in range(CHUNKS):
                table = raw[aim ^ x, pl.ds(FIELDS * h, FIELDS), :]
                for c in range(CHUNKS):
                    here = blocks[c] == x * CHUNKS + h
                    found[c] = jnp.where(here, take(table, lanes[c]), found[c])
        for c in range(CHUNKS):
            own[which, pl.ds(FIELDS * c, FIELDS), :] = jnp.where(there, found[c], 0.0)
        own[which, pl.ds(RIM_AT, 1), :] = jnp.where(there, raw[aim, pl.ds(RIM_AT, 1), :], 0.0)

def join_kernel(stride, states, fixed, paired, across, own, *sends):
    me = lax.axis_index("parts")
    member, kind = me // stride, me % stride
    odd = member % 2 == 1
    for which in range(3):
        own[which, pl.ds(0, FIRST_AT), :] = states[which]
        there = (member + which >= 1) & (member + which <= GROUP)
        for at in range(0, FIXED, FIELDS):
            rows = pl.ds(at, FIELDS)
            if which == 1:
                rest = fixed[rows, :]
            else:
                by_pair = odd if which == 0 else jnp.logical_not(odd)
                rest = jnp.where(by_pair, paired[rows, :], across[rows, :])
            absent = 1.0 if at == DIAG_AT - FIRST_AT else 0.0
            own[which, pl.ds(FIRST_AT + at, FIELDS), :] = jnp.where(there, rest, absent)

    if stride == BLOCK:
        for send, later in zip(sends, (kind % 2 == 0, kind < 2)):
            for k in range(2):
                send[k] = jnp.where(later, own[k + 1], own[k])
    else:
        (send,) = sends

        def fill(to, carry):
            base = jnp.where(kind < to, 1, 0)
            send[to, 0] = own[base]
            send[to, 1] = own[base + 1]
            return carry

        lax.fori_loop(0, stride, fill, 0)


def gather_records(stride, own, sources, records, offsets):
    kind = lax.axis_index("parts") % stride
    even = kind % 2 == 0
    for o in offsets:
        at, later = o + REACH, 1 if o > 0 else 0
        if o % stride == 0:
            records[at] = own[1 + o // stride]
        elif stride != BLOCK:
            records[at] = sources[0][(kind + o + stride) % stride, later]
        elif o % 2 == 0:
            records[at] = sources[2][later]
        else:
            by_chip = even if o in (1, -3) else jnp.logical_not(even)
            records[at] = jnp.where(by_chip, sources[0][later], sources[1][later])


def state_of(record):
    return [record[pl.ds(FIELDS * c, FIELDS), :] for c in range(CHUNKS)]


def ends_of(record):
    first = record[pl.ds(FIRST_AT, FIELDS), :].astype(jnp.int32)
    second = record[pl.ds(SECOND_AT, FIELDS), :].astype(jnp.int32)
    return first, second


def diag_of(record):
    return record[pl.ds(DIAG_AT, FIELDS), :]


def rim_of(record, blocks):
    slots = wide(record[pl.ds(RIM_AT, 1), :].astype(jnp.int32))
    lane, high = slots & (TILE - 1), slots >> 7
    found = take(blocks[0], lane)
    for c in range(1, CHUNKS):
        found = jnp.where(high == c, take(blocks[c], lane), found)
    return found


def difference(local, before, after, field, first, second):
    near = [local[pl.ds(FIELDS * c + field, 1), :] for c in range(CHUNKS)]
    ghosts = [one[pl.ds(field, 1), :] for one in (before, after)]
    return look_up(near, first) - look_up(near + ghosts, second)


def first_lam(record, before, after):
    first, second = ends_of(record)
    normal = [difference(record, before, after, k, first, second) for k in range(3)]
    speed = sum(
        normal[k] * difference(record, before, after, 3 + k, first, second) for k in range(3)
    )
    return normal, jnp.maximum(0.0, -speed / diag_of(record))


def add_up(force, first, second, heads, rows):
    for k in range(3):
        head = force[k].astype(jnp.bfloat16).astype(jnp.float32)
        rows[pl.ds(k, FIELDS, stride=FIELDS), :] = force[k] - head
        rows[pl.ds(3 + k, FIELDS, stride=FIELDS), :] = head
    empty = jnp.zeros((FIELDS, TILE), jnp.float32)
    pad = [empty] * (len(heads) % 2)
    left, right = [], []
    for t in range(FIELDS):
        value = rows[pl.ds(FIELDS * t, FIELDS), :]
        for index, limit, signed in ((first, CHUNKS, value), (second, EXT_CHUNKS, -value)):
            if min(heads) >= limit:
                continue
            row = index[t : t + 1]
            high = wide(row >> 7)
            groups = [jnp.where(high == h, signed, 0.0) if h < limit else empty for h in heads]
            left.append(jnp.concatenate(groups + pad, axis=0))
            right.append(one_hot(row & (TILE - 1)))
    total = 0.0
    for k in range(0, len(left), 2):
        total += lax.dot_general(
            jnp.concatenate(left[k : k + 2], axis=1).astype(jnp.bfloat16),
            jnp.concatenate(right[k : k + 2], axis=1),
            NT,
            preferred_element_type=jnp.float32,
        )
    blocks = [total[FIELDS * k : FIELDS * (k + 1)] for k in range(len(heads))]
    return {h: block + pltpu.roll(block, 3, 0) for h, block in zip(heads, blocks)}


def moved(was, here, incoming, back_row):
    place = wide(back_row)
    extra = jnp.where(place > 0, take(incoming, jnp.maximum(place - 1, 0)), 0.0)
    field = rows_iota((FIELDS, TILE))
    gain = wide(was[6:7]) * (here + extra)
    return was + jnp.where((field >= 3) & (field < 6), gain, 0.0)


def near_kernel(stride, sources, *refs):
    own, came = refs[0], refs[1 : 1 + sources]
    tiles, coupled, records, rims = refs[1 + sources :]
    gather_records(stride, own, came, records, (-1, 0, 1))
    before, here, after = [records.at[o + REACH] for o in (-1, 0, 1)]
    for k, record in ((0, before), (1, after)):
        rims[k] = rim_of(record, state_of(record))
    lam = first_lam(here, rims.at[0], rims.at[1])[1]
    head = lam.astype(jnp.bfloat16).astype(jnp.float32)
    both = jnp.concatenate([head, lam - head], axis=0).astype(jnp.bfloat16)
    total = jnp.zeros((FIELDS, TILE), jnp.float32)
    for t in range(tiles.shape[0]):
        tile = tiles[t]
        tile_head = tile.astype(jnp.bfloat16)
        tile_tail = (tile - tile_head.astype(jnp.float32)).astype(jnp.bfloat16)
        main = lax.dot_general(both, tile_head, NT, preferred_element_type=jnp.float32)
        rest = lax.dot_general(both, tile_tail, NT, preferred_element_type=jnp.float32)
        whole = main[:FIELDS] + main[FIELDS:] + rest[:FIELDS]
        total = jnp.where(rows_iota((FIELDS, TILE)) == t, whole, total)
    coupled[...] = total


def middle_kernel(stride, sources, *refs):
    own, came = refs[0], refs[1 : 1 + sources]
    stage, back_here, fixed_out, gathered, rims, rows, state_next, rims_next = refs[1 + sources :]
    offsets = range(-REACH, REACH + 1)
    gather_records(stride, own, came, gathered, offsets)
    records = {o: gathered.at[o + REACH] for o in offsets}
    for o, record in records.items():
        rims[o + REACH] = rim_of(record, state_of(record))
    sums, contacts = {}, {}
    for o in range(1 - REACH, REACH):
        record = records[o]
        contacts[o] = first_lam(record, rims.at[o + REACH - 1], rims.at[o + REACH + 1])
    for o in range(1 - REACH, REACH):
        normal, lam = contacts[o]
        first, second = ends_of(records[o])
        heads = list(range(CHUNKS)) if abs(o) < REACH - 1 else []
        heads += [CHUNKS] if o > 1 - REACH + 1 else []
        heads += [CHUNKS + 1] if o < REACH - 1 - 1 else []
        force = [one * lam for one in normal]
        sums[o] = add_up(force, first, second, heads, rows.at[o + REACH - 1])
    for o in range(2 - REACH, REACH - 1):
        incoming = sums[o - 1][CHUNKS + 1] + sums[o + 1][CHUNKS]
        back = inverse([records[o][pl.ds(RIM_AT, 1), :]])
        if o == 0:
            back_here[...] = back
        blocks = [
            moved(was, sums[o][c], incoming, back[c : c + 1])
            for c, was in enumerate(state_of(records[o]))
        ]
        rims_next[o + REACH] = rim_of(records[o], blocks)
        if abs(o) < 2:
            for c in range(CHUNKS):
                state_next[o + 1, pl.ds(FIELDS * c, FIELDS), :] = blocks[c]
    for o in (-1, 0, 1):
        normal, lam = contacts[o]
        first, second = ends_of(records[o])
        before, after = rims_next.at[o + REACH - 1], rims_next.at[o + REACH + 1]
        state = state_next.at[o + 1]
        speed = sum(
            normal[k] * difference(state, before, after, 3 + k, first, second) for k in range(3)
        )
        for k in range(3):
            stage[o + 1, k] = normal[k]
        stage[o + 1, 3] = lam
        stage[o + 1, 4] = speed
        fixed_out[o + 1] = records[o][pl.ds(FIRST_AT, FIXED), :]


def last_kernel(
    parts, own, stage, back, here, chip, other, mid, fixed, velocity, impulse, rows
):
    me = lax.axis_index("parts")
    odd = me % 2 == 1
    central = (me == parts // 2) | (me == parts // 2 - 1)
    across = jnp.where(central, mid[...], other[...])
    across = jnp.where((me > 0) & (me < parts - 1), across, 0.0)
    coupled = {
        -1: jnp.where(odd, chip[...], across),
        0: here[...],
        1: jnp.where(odd, across, chip[...]),
    }
    sums = {}
    for o, heads in ((-1, [CHUNKS + 1]), (0, list(range(CHUNKS))), (1, [CHUNKS])):
        record = fixed.at[o + 1]
        lam = stage[o + 1, 3]
        diag = record[pl.ds(DIAG_AT - FIRST_AT, FIELDS), :]
        lam = jnp.maximum(0.0, lam - (coupled[o] + stage[o + 1, 4]) / diag)
        if o == 0:
            impulse[...] = lam
        first = record[pl.ds(0, FIELDS), :].astype(jnp.int32)
        second = record[pl.ds(SECOND_AT - FIRST_AT, FIELDS), :].astype(jnp.int32)
        force = [stage[o + 1, k] * lam for k in range(3)]
        sums[o] = add_up(force, first, second, heads, rows.at[o + 1])
    incoming = sums[-1][CHUNKS + 1] + sums[1][CHUNKS]
    for c, was in enumerate(state_of(own.at[1])):
        block = moved(was, sums[0][c], incoming, back[pl.ds(c, 1), :])
        velocity[:, pl.ds(c * TILE, TILE)] = block[3:6]


def call(kernel, out_shape, inputs, name, space=pltpu.VMEM, scratch=()):
    many = isinstance(out_shape, (tuple, list))
    vmem = pl.BlockSpec(memory_space=pltpu.VMEM)
    return pl.pallas_call(
        kernel,
        out_shape=out_shape,
        in_specs=[pl.BlockSpec(memory_space=space)] * len(inputs),
        out_specs=[vmem] * len(out_shape) if many else vmem,
        scratch_shapes=list(scratch),
        compiler_params=FROM_HBM if space == pltpu.HBM else PARAMS,
        name=name,
    )(*inputs)


def block_borders(parts, stride):
    to = {i: i ^ 1 for i in range(parts)}
    for i in range(stride, parts - stride):
        to[i] = i + stride if i // stride % 2 == 1 else i - stride
    return list(to.items())


def next_pairs(parts):
    half = parts // 2
    most = {i: i + 1 if i % 2 else i - 1 for i in range(parts)}
    most.update({0: half - 1, half - 1: 0, half: parts - 1, parts - 1: half})
    middle = {i: i ^ 1 for i in range(parts)}
    middle.update({half - 1: half, half: half - 1, half - 2: half + 1, half + 1: half - 2})
    return list(most.items()), list(middle.items())


def body(positions, velocity, inv_mass, swap_lists, rim_list, contact_pair, delassus):
    parts = lax.axis_size("parts")
    stride = parts // GROUP
    grains = positions.shape[1]
    contacts = contact_pair.shape[1]
    tiles = delassus.shape[0]
    reach = 2 * REACH + 1
    float32 = functools.partial(jax.ShapeDtypeStruct, dtype=jnp.float32)
    vmem = lambda *shape: pltpu.VMEM(shape, jnp.float32)
    send = functools.partial(lax.ppermute, axis_name="parts")
    inputs = (
        positions,
        velocity,
        inv_mass.reshape(CHUNKS, TILE),
        swap_lists,
        rim_list.reshape(1, TILE),
    )
    packed = call(
        pack_kernel,
        float32((GROUP, RAW, TILE)),
        inputs,
        "pack",
        pltpu.HBM,
        [pltpu.VMEM(one.shape, one.dtype) for one in inputs] + [pltpu.SemaphoreType.DMA((5,))],
    )
    classes = [[r + stride * k for k in range(GROUP)] for r in range(stride)]
    raw = lax.all_to_all(packed, "parts", 0, 0, axis_index_groups=classes)

    fixed = call(fixed_kernel, float32((FIXED, TILE)), (contact_pair, delassus), "fixed")
    paired = send(fixed, perm=[(i, i ^ stride) for i in range(parts)])
    across = send(fixed, perm=block_borders(parts, stride))

    record = (2, RECORD, TILE)
    sends = [float32(record)] * 2 if stride == BLOCK else [float32((stride, *record))]
    states = call(
        functools.partial(compose_kernel, stride),
        float32((3, FIRST_AT, TILE)),
        (raw,),
        "compose",
    )
    own, *sends = call(
        functools.partial(join_kernel, stride),
        (float32((3, RECORD, TILE)), *sends),
        (states, fixed, paired, across),
        "join",
    )
    within = [(i, i ^ 1) for i in range(parts)]
    opposite = [(i, i ^ 3) for i in range(parts)]
    if stride == BLOCK:
        from_far = send(sends[1], perm=opposite)
        from_side = send(sends[1], perm=[(i, i ^ 2) for i in range(parts)])
        near = (send(sends[0], perm=within), from_far)
        came = (*near, from_side)
    else:
        blocks = [[stride * k + r for r in range(stride)] for k in range(GROUP)]
        near = came = (lax.all_to_all(sends[0], "parts", 0, 0, axis_index_groups=blocks),)

    here = call(
        functools.partial(near_kernel, stride, len(near)),
        float32((tiles, TILE)),
        (own, *near, delassus),
        "near",
        scratch=[vmem(reach, RECORD, TILE), vmem(2, FIELDS, TILE)],
    )
    most, middle = next_pairs(parts)
    other = send(here, perm=most)
    chip = send(here, perm=within)
    mid = send(here, perm=middle)
    stage, back, contact_rows = call(
        functools.partial(middle_kernel, stride, len(came)),
        (
            float32((3, 5, FIELDS, TILE)),
            jax.ShapeDtypeStruct((FIELDS, TILE), jnp.int32),
            float32((3, FIXED, TILE)),
        ),
        (own, *came),
        "middle",
        scratch=[
            vmem(reach, RECORD, TILE),
            vmem(reach, FIELDS, TILE),
            vmem(reach - 2, FIELDS * FIELDS, TILE),
            vmem(3, CHUNKS * FIELDS, TILE),
            vmem(reach, FIELDS, TILE),
        ],
    )
    new_velocity, impulse = call(
        functools.partial(last_kernel, parts),
        (float32((3, grains)), float32((tiles, TILE))),
        (own, stage, back, here, chip, other, mid, contact_rows),
        "last",
        scratch=[vmem(3, FIELDS * FIELDS, TILE)],
    )
    return (new_velocity, impulse.reshape(contacts))


def solution(mesh):
    in_specs = (
        P(None, "parts"),
        P(None, "parts"),
        P("parts"),
        P(None, "parts"),
        P("parts"),
        P(None, "parts"),
        P("parts", None, None),
    )
    out_specs = (P(None, "parts"), P("parts"))
    return jax.shard_map(body, mesh=mesh, in_specs=in_specs, out_specs=out_specs, check_vma=False)
```

time: 74.3 us -> 30 us (0.40)
  the two profiles are of different devices: /device:TPU:23 before, /device:TPU:0 now
where the time goes in v1:
time: 30 us; the launch traced here: 29.6 us
  starting transfers between devices  14 us (47%)
  waiting for transfers between devices  7.11 us (24%)
  Pallas kernels  6.71 us (22%)
  local copies, waits for them, and re-layouts  1.05 us (4%)
  between operations  0.71 us (2%)
    all_to_all x1, starting transfers between devices, body(): raw = lax.all_to_all(packed, 'parts', 0, 0, axis_index_groups=classes)  7.29 us
    pallas_call x7, Pallas kernels, call(): pl.pallas_call(kernel, out_shape=out_shape, in_specs=[pl.BlockSpec(memory...  6.71 us
    all_to_all x1, waiting for transfers between devices, body(): raw = lax.all_to_all(packed, 'parts', 0, 0, axis_index_groups=classes)  4.37 us
    ppermute x1, starting transfers between devices, body(): paired = send(fixed, perm=[(i, i ^ stride) for i in range(parts)])  2.08 us
    ppermute x1, starting transfers between devices, body(): other = send(here, perm=most)  1.86 us
    ppermute x1, waiting for transfers between devices, body(): from_far = send(sends[1], perm=opposite)  1.71 us
    ppermute x1, starting transfers between devices, body(): from_far = send(sends[1], perm=opposite)  1.61 us
    unnamed x6, local copies, waits for them, and re-layouts  1.05 us
  transfers between devices with their start and end apart: 9, of which 3 were waited for; matrix products, arithmetic and copies ran while one was open for 0% of the time, Pallas kernels for 14%

profile of v1, /device:TPU:0, one launch (start us, length us, event | category | flops | bytes accessed | tf_op | source)
XLA Modules:
  0.0 29.6 jit_solution(11078423677733921234)
XLA Ops:
  0.6 1.5 %pack.1 = f32[8,40,128]{2,1,0:T(8,128)} custom-call(f32[3,512]{1,0:T(4,128)} %refs_0_.1, f32[3,512]{1,0:T(4,128)} %refs_1_.1, f32[4,128]{1,0:T(4,128)} %bitcast.3, s32[3,256]{1,0:T(4,128)} %refs_3_.2, s32[1,128]{1,0:T(1,128)} %bitcast.4), custom_call_target="tpu_custom_call" | custom-call | tf_op jit(solution)/shard_map/pack/pallas_call | solution.py:396
  2.1 0.0 copy-start.2
  2.1 7.3 %all-to-all-start = ((f32[8,40,128]{2,1,0:T(8,128)}), f32[8,40,128]{2,1,0:T(8,128)S(1)}, u32[]{:S(2)}, u32[]{:S(2)}) async-start(f32[8,40,128]{2,1,0:T(8,128)} %pack.1), calls=%async_computation | async-start | bytes 327680 | tf_op jit(solution)/shard_map/all_to_all | solution.py:449
  9.4 0.0 copy-done.2
  9.4 0.0 copy-start
  9.4 1.0 %copy-done = f32[8,128,128]{2,1,0:T(8,128)S(1)} copy-done((f32[8,128,128]{2,1,0:T(8,128)S(1)}, f32[8,128,128]{2,1,0:T(8,128)}, u32[]{:S(2)}) %copy-start) | copy-done | bytes 524312
  10.5 0.0 copy-start.1
  10.5 0.1 fixed.1
  10.5 2.1 %collective-permute-start = (f32[24,128]{1,0:T(8,128)S(1)}, f32[24,128]{1,0:T(8,128)S(1)}, u32[]{:S(2)}, u32[]{:S(2)}) collective-permute-start(f32[24,128]{1,0:T(8,128)S(1)} %fixed.1), channel_id=1, source_target_pairs={{0,4},{1,5},{2,6},{3,7},{4,0},{5,1},{6,2},{7,3},{8,12},{9,13},{10,... | collective-permute-start | bytes 36872 | tf_op jit(solution)/shard_map/ppermute | solution.py:452
  12.6 0.0 collective-permute-start.1
  12.6 4.4 %all-to-all-done.raw = f32[8,40,128]{2,1,0:T(8,128)S(1)} async-done(((f32[8,40,128]{2,1,0:T(8,128)}), f32[8,40,128]{2,1,0:T(8,128)S(1)}, u32[]{:S(2)}, u32[]{:S(2)}) %all-to-all-start) | async-done | bytes 163872 | tf_op jit(solution)/shard_map/all_to_all | solution.py:449
  17.0 1.8 %compose.1.states = f32[3,32,128]{2,1,0:T(8,128)S(1)} custom-call(f32[8,40,128]{2,1,0:T(8,128)S(1)} %all-to-all-done.raw), custom_call_target="tpu_custom_call" | custom-call | tf_op jit(solution)/shard_map/compose/pallas_call | solution.py:396
  18.8 0.0 collective-permute-done.paired
  18.8 0.0 collective-permute-done.1.across
  18.8 0.1 collective-permute-start.2
  18.9 1.6 %collective-permute-start.3 = (f32[2,56,128]{2,1,0:T(8,128)S(1)}, f32[2,56,128]{2,1,0:T(8,128)S(1)}, u32[]{:S(2)}, u32[]{:S(2)}) collective-permute-start(f32[2,56,128]{2,1,0:T(8,128)S(1)} %get-tuple-element.12), channel_id=1, source_target_pairs={{0,3},{1,2},{2,1},{3,0},{4,7},{5,6},{6,5},{7,4},{8,11},{9,10},{10,... | collective-permute-start | bytes 172040 | tf_op jit(solution)/shard_map/ppermute | solution.py:472
  20.5 0.5 %collective-permute-start.4 = (f32[2,56,128]{2,1,0:T(8,128)S(1)}, f32[2,56,128]{2,1,0:T(8,128)S(1)}, u32[]{:S(2)}, u32[]{:S(2)}) collective-permute-start(f32[2,56,128]{2,1,0:T(8,128)S(1)} %get-tuple-element.12), channel_id=1, source_target_pairs={{0,2},{1,3},{2,0},{3,1},{4,6},{5,7},{6,4},{7,5},{8,10},{9,11},{10,... | collective-permute-start | bytes 172040 | tf_op jit(solution)/shard_map/ppermute | solution.py:473
  21.1 0.0 collective-permute-done.2.refs_1_
  21.1 1.7 %collective-permute-done.3.refs_2_ = f32[2,56,128]{2,1,0:T(8,128)S(1)} collective-permute-done((f32[2,56,128]{2,1,0:T(8,128)S(1)}, f32[2,56,128]{2,1,0:T(8,128)S(1)}, u32[]{:S(2)}, u32[]{:S(2)}) %collective-permute-start.3) | collective-permute-done | bytes 57376 | tf_op jit(solution)/shard_map/ppermute | solution.py:472
  22.8 0.0 copy-done.1
  22.8 0.6 %near.1.here = f32[8,128]{1,0:T(8,128)S(1)} custom-call(f32[3,56,128]{2,1,0:T(8,128)S(1)} %get-tuple-element.10.refs_0_.own, f32[2,56,128]{2,1,0:T(8,128)S(1)} %collective-permute-done.2.refs_1_, f32[2,56,128]{2,1,0:T(8,128)S(1)} %collective-permute-done.3.refs_2_, f32[8,128,128]{2,1,0:T(8,128)S(1)} %copy-done.1), custom_call_target="tpu_custom_call" | custom-call | tf_op jit(solution)/shard_map/near/pallas_call | solution.py:396
  23.3 0.4 %collective-permute-start.5 = (f32[8,128]{1,0:T(8,128)S(1)}, f32[8,128]{1,0:T(8,128)S(1)}, u32[]{:S(2)}, u32[]{:S(2)}) collective-permute-start(f32[8,128]{1,0:T(8,128)S(1)} %near.1.here), channel_id=1, source_target_pairs={{0,1},{1,0},{2,3},{3,2},{4,5},{5,4},{6,7},{7,6},{8,9},{9,8},{10,11... | collective-permute-start | bytes 12296 | tf_op jit(solution)/shard_map/ppermute | solution.py:489
  23.7 1.9 %collective-permute-start.6 = (f32[8,128]{1,0:T(8,128)S(1)}, f32[8,128]{1,0:T(8,128)S(1)}, u32[]{:S(2)}, u32[]{:S(2)}) collective-permute-start(f32[8,128]{1,0:T(8,128)S(1)} %near.1.here), channel_id=1, source_target_pairs={{0,15},{1,2},{2,1},{3,4},{4,3},{5,6},{6,5},{7,8},{8,7},{9,10},{10,... | collective-permute-start | bytes 12296 | tf_op jit(solution)/shard_map/ppermute | solution.py:488
  25.6 0.2 collective-permute-start.7
  25.8 0.0 collective-permute-done.4.refs_3_
  25.8 1.7 %middle.1 = (f32[3,5,8,128]{3,2,1,0:T(8,128)S(1)}, s32[8,128]{1,0:T(8,128)S(1)}, f32[3,24,128]{2,1,0:T(8,128)S(1)}) custom-call(f32[3,56,128]{2,1,0:T(8,128)S(1)} %get-tuple-element.10.refs_0_.own, f32[2,56,128]{2,1,0:T(8,128)S(1)} %collective-permute-done.2.refs_1_, f32[2,56,128]{2,1,0:T(8,128)S(1)} %collective-permute-done.3.refs_2_, ...), custom_call_target="tpu_custom_call" | custom-call | tf_op jit(solution)/shard_map/middle/pallas_call | solution.py:396
  27.5 0.0 collective-permute-done.5.chip
  27.5 1.0 %collective-permute-done.6.other = f32[8,128]{1,0:T(8,128)S(1)} collective-permute-done((f32[8,128]{1,0:T(8,128)S(1)}, f32[8,128]{1,0:T(8,128)S(1)}, u32[]{:S(2)}, u32[]{:S(2)}) %collective-permute-start.6) | collective-permute-done | bytes 4128 | tf_op jit(solution)/shard_map/ppermute | solution.py:488
  28.5 0.0 collective-permute-done.7.mid
  28.5 1.1 %last.1 = (f32[3,512]{1,0:T(4,128)}, f32[8,128]{1,0:T(8,128)}) custom-call(f32[3,56,128]{2,1,0:T(8,128)S(1)} %get-tuple-element.10.refs_0_.own, f32[3,5,8,128]{3,2,1,0:T(8,128)S(1)} %get-tuple-element.13.stage, s32[8,128]{1,0:T(8,128)S(1)} %get-tuple-element.14.back, f32[8,128]{1,0:T(8,128)S(1)} %near.1.here, f32[8,128]{1,0:T(8,128)S(1)} %collective-permute-done.5.chip, ...), custom_call_target="tpu_custom_call" | custom-call | tf_op jit(solution)/shard_map/last/pallas_call | solution.py:396
  (1 shorter events, 0.0 us)
Async XLA Ops:
  2.1 7.3 %copy-start.2 = (s32[2,1024]{1,0:T(2,128)S(1)}, s32[2,1024]{1,0:T(2,128)}, u32[]{:S(2)}) copy-start(s32[2,1024]{1,0:T(2,128)} %pair.1) | copy-start | bytes 24580
  2.1 14.9 %all-to-all-start = ((f32[8,40,128]{2,1,0:T(8,128)}), f32[8,40,128]{2,1,0:T(8,128)S(1)}, u32[]{:S(2)}, u32[]{:S(2)}) async-start(f32[8,40,128]{2,1,0:T(8,128)} %pack.1), calls=%async_computation | async-start | bytes 327680 | tf_op jit(solution)/shard_map/all_to_all | solution.py:449
  9.4 1.0 %copy-start = (f32[8,128,128]{2,1,0:T(8,128)S(1)}, f32[8,128,128]{2,1,0:T(8,128)}, u32[]{:S(2)}) copy-start(f32[8,128,128]{2,1,0:T(8,128)} %refs_3_.3) | copy-start | bytes 1572868
  10.5 12.3 %copy-start.1 = (f32[8,128,128]{2,1,0:T(8,128)S(1)}, f32[8,128,128]{2,1,0:T(8,128)}, u32[]{:S(2)}) copy-start(f32[8,128,128]{2,1,0:T(8,128)} %refs_3_.3) | copy-start | bytes 1572868
  10.5 8.2 %collective-permute-start = (f32[24,128]{1,0:T(8,128)S(1)}, f32[24,128]{1,0:T(8,128)S(1)}, u32[]{:S(2)}, u32[]{:S(2)}) collective-permute-start(f32[24,128]{1,0:T(8,128)S(1)} %fixed.1), channel_id=1, source_target_pairs={{0,4},{1,5},{2,6},{3,7},{4,0},{5,1},{6,2},{7,3},{8,12},{9,13},{10,... | collective-permute-start | bytes 36872 | tf_op jit(solution)/shard_map/ppermute | solution.py:452
  12.6 6.2 %collective-permute-start.1 = (f32[24,128]{1,0:T(8,128)S(1)}, f32[24,128]{1,0:T(8,128)S(1)}, u32[]{:S(2)}, u32[]{:S(2)}) collective-permute-start(f32[24,128]{1,0:T(8,128)S(1)} %fixed.1), channel_id=1, source_target_pairs={{0,1},{1,0},{2,3},{3,2},{4,8},{5,9},{6,10},{7,11},{8,4},{9,5},{10,... | collective-permute-start | bytes 36872 | tf_op jit(solution)/shard_map/ppermute | solution.py:453
  18.8 2.2 %collective-permute-start.2 = (f32[2,56,128]{2,1,0:T(8,128)S(1)}, f32[2,56,128]{2,1,0:T(8,128)S(1)}, u32[]{:S(2)}, u32[]{:S(2)}) collective-permute-start(f32[2,56,128]{2,1,0:T(8,128)S(1)} %get-tuple-element.11), channel_id=1, source_target_pairs={{0,1},{1,0},{2,3},{3,2},{4,5},{5,4},{6,7},{7,6},{8,9},{9,8},{10,11... | collective-permute-start | bytes 172040 | tf_op jit(solution)/shard_map/ppermute | solution.py:474
  18.9 3.9 %collective-permute-start.3 = (f32[2,56,128]{2,1,0:T(8,128)S(1)}, f32[2,56,128]{2,1,0:T(8,128)S(1)}, u32[]{:S(2)}, u32[]{:S(2)}) collective-permute-start(f32[2,56,128]{2,1,0:T(8,128)S(1)} %get-tuple-element.12), channel_id=1, source_target_pairs={{0,3},{1,2},{2,1},{3,0},{4,7},{5,6},{6,5},{7,4},{8,11},{9,10},{10,... | collective-permute-start | bytes 172040 | tf_op jit(solution)/shard_map/ppermute | solution.py:472
  20.5 5.3 %collective-permute-start.4 = (f32[2,56,128]{2,1,0:T(8,128)S(1)}, f32[2,56,128]{2,1,0:T(8,128)S(1)}, u32[]{:S(2)}, u32[]{:S(2)}) collective-permute-start(f32[2,56,128]{2,1,0:T(8,128)S(1)} %get-tuple-element.12), channel_id=1, source_target_pairs={{0,2},{1,3},{2,0},{3,1},{4,6},{5,7},{6,4},{7,5},{8,10},{9,11},{10,... | collective-permute-start | bytes 172040 | tf_op jit(solution)/shard_map/ppermute | solution.py:473
  23.3 4.2 %collective-permute-start.5 = (f32[8,128]{1,0:T(8,128)S(1)}, f32[8,128]{1,0:T(8,128)S(1)}, u32[]{:S(2)}, u32[]{:S(2)}) collective-permute-start(f32[8,128]{1,0:T(8,128)S(1)} %near.1.here), channel_id=1, source_target_pairs={{0,1},{1,0},{2,3},{3,2},{4,5},{5,4},{6,7},{7,6},{8,9},{9,8},{10,11... | collective-permute-start | bytes 12296 | tf_op jit(solution)/shard_map/ppermute | solution.py:489
  23.7 4.8 %collective-permute-start.6 = (f32[8,128]{1,0:T(8,128)S(1)}, f32[8,128]{1,0:T(8,128)S(1)}, u32[]{:S(2)}, u32[]{:S(2)}) collective-permute-start(f32[8,128]{1,0:T(8,128)S(1)} %near.1.here), channel_id=1, source_target_pairs={{0,15},{1,2},{2,1},{3,4},{4,3},{5,6},{6,5},{7,8},{8,7},{9,10},{10,... | collective-permute-start | bytes 12296 | tf_op jit(solution)/shard_map/ppermute | solution.py:488
  25.6 3.0 %collective-permute-start.7 = (f32[8,128]{1,0:T(8,128)S(1)}, f32[8,128]{1,0:T(8,128)S(1)}, u32[]{:S(2)}, u32[]{:S(2)}) collective-permute-start(f32[8,128]{1,0:T(8,128)S(1)} %near.1.here), channel_id=1, source_target_pairs={{0,1},{1,0},{2,3},{3,2},{4,5},{5,4},{6,7},{7,6},{8,9},{9,8},{10,11... | collective-permute-start | bytes 12296 | tf_op jit(solution)/shard_map/ppermute | solution.py:490

commit v2 on v1

v2 whole, which is shorter than its diff:
```python
import functools

import jax
import jax.numpy as jnp
from jax import lax
from jax.experimental import pallas as pl
from jax.experimental.pallas import tpu as pltpu
from jax.sharding import PartitionSpec as P

TILE = 128
LEVELS = 3
GROUP = 2**LEVELS
REACH = 2
FIELDS = 8
CHUNKS = 4
EXT_CHUNKS = 6
RIM_AT = 7
FIRST_AT = 32
SECOND_AT = 40
DIAG_AT = 48
RECORD = 56
LISTS_AT = 32
RAW = 40
FIXED = RECORD - FIRST_AT
BLOCK = 4
EDGE = 8
PARAMS = pltpu.CompilerParams(vmem_limit_bytes=32 * 2**20)
FROM_HBM = pltpu.CompilerParams(vmem_limit_bytes=63 * 2**20)
NT = (((1,), (1,)), ((), ()))


def rows_iota(shape):
    return lax.broadcasted_iota(jnp.int32, shape, 0)


def lanes_iota(shape):
    return lax.broadcasted_iota(jnp.int32, shape, 1)


def wide(row):
    return jnp.broadcast_to(row, (FIELDS, TILE))


def take(table, lane):
    return jnp.take_along_axis(table, lane, axis=1, mode="promise_in_bounds")


def look_up(rows, index):
    lane, high = index & (TILE - 1), index >> 7
    found = take(wide(rows[0]), lane)
    for h in range(1, len(rows)):
        found = jnp.where(high == h, take(wide(rows[h]), lane), found)
    return found


def one_hot(low_row):
    return (rows_iota((TILE, TILE)) == low_row).astype(jnp.float32).astype(jnp.bfloat16)


def inverse(slot_rows):
    left, right = [], []
    for at, row in enumerate(slot_rows):
        slots = row.astype(jnp.int32)
        place = (lanes_iota((FIELDS, TILE)) + (at * TILE + 1)).astype(jnp.float32)
        heads = jnp.where(wide(slots >> 7) == rows_iota((FIELDS, TILE)), place, 0.0)
        left.append(heads.astype(jnp.bfloat16))
        right.append(one_hot(slots & (TILE - 1)))
    total = lax.dot_general(
        jnp.concatenate(left, axis=1),
        jnp.concatenate(right, axis=1),
        NT,
        preferred_element_type=jnp.float32,
    )
    return total.astype(jnp.int32)


def pack_kernel(*refs):
    sources, out, held, sems = refs[:5], refs[5], refs[6:11], refs[11]
    copies = [
        pltpu.make_async_copy(source, target, sems.at[k])
        for k, (source, target) in enumerate(zip(sources, held))
    ]
    for copy in copies:
        copy.start()
    pos, vel, mass, lists, rim = held
    for copy in copies:
        copy.wait()
    first = out.at[0]
    for c in range(CHUNKS):
        lanes = pl.ds(c * TILE, TILE)
        first[pl.ds(FIELDS * c, 3), :] = pos[:, lanes]
        first[pl.ds(FIELDS * c + 3, 3), :] = vel[:, lanes]
        first[pl.ds(FIELDS * c + 6, 1), :] = mass[pl.ds(c, 1), :]
        spare = rim[...].astype(jnp.float32) if c == 0 else jnp.zeros((1, TILE), jnp.float32)
        first[pl.ds(FIELDS * c + 7, 1), :] = spare
    for level in range(LEVELS):
        for h in range(2):
            row = lists[pl.ds(level, 1), pl.ds(h * TILE, TILE)]
            first[pl.ds(LISTS_AT + 2 * level + h, 1), :] = row.astype(jnp.float32)
    first[pl.ds(LISTS_AT + 2 * LEVELS, 2), :] = jnp.zeros((2, TILE), jnp.float32)
    whole = first[...]
    for m in range(1, GROUP):
        out[m] = whole


def fixed_kernel(pair, tiles, out, heads, tails):
    eye = rows_iota((TILE, TILE)) == lanes_iota((TILE, TILE))
    for t in range(tiles.shape[0]):
        lanes = pl.ds(t * TILE, TILE)
        out[pl.ds(t, 1), :] = pair[pl.ds(0, 1), lanes].astype(jnp.float32)
        out[pl.ds(FIELDS + t, 1), :] = pair[pl.ds(1, 1), lanes].astype(jnp.float32)
        tile = tiles[t]
        head = tile.astype(jnp.bfloat16)
        heads[t] = head
        tails[t] = (tile - head.astype(jnp.float32)).astype(jnp.bfloat16)
        diag = jnp.sum(jnp.where(eye, tile, 0.0), axis=0, keepdims=True)
        out[pl.ds(2 * FIELDS + t, 1), :] = diag


def second_part(stride):
    me = lax.axis_index("parts")
    member, kind = me // stride, me % stride
    step = jnp.where(kind < stride // 2, 1, -1)
    return step, (member + step >= 0) & (member + step < GROUP)


def swapped(lists, other_lists, own, other, out):
    back = inverse(lists)
    place = jnp.maximum(back - 1, 0)
    slot = look_up(other_lists, place).astype(jnp.int32)
    lane = slot & (TILE - 1)
    block = jnp.where(back > 0, slot >> 7, -1)
    tables = [other[pl.ds(FIELDS * h, FIELDS), :] for h in range(CHUNKS)]
    for c in range(CHUNKS):
        rows = pl.ds(FIELDS * c, FIELDS)
        lane_c, block_c = wide(lane[c : c + 1]), wide(block[c : c + 1])
        found = own[rows, :]
        for h, table in enumerate(tables):
            found = jnp.where(block_c == h, take(table, lane_c), found)
        out[rows, :] = found


def compose_kernel(stride, raw, own, once, twice):
    member = lax.axis_index("parts") // stride
    step, exists = second_part(stride)

    def came_from(part):
        return raw.at[GROUP - 1 - part]

    def list_rows(part, level):
        rows = came_from(part)
        return [rows[pl.ds(LISTS_AT + 2 * level + h, 1), :] for h in range(2)]

    def level_step(level, part, apart, own_state, other_state, out):
        lists, others = list_rows(part, level), list_rows(part ^ apart, level)
        swapped(lists, others, own_state, other_state, out)

    for r in range(GROUP):
        level_step(0, r, 4, came_from(r), came_from(r ^ 4), once.at[r])
    second = (member + step + GROUP) % GROUP
    for i, part in enumerate((member, member ^ 1, second, second ^ 1)):
        level_step(1, part, 2, once.at[part], once.at[part ^ 2], twice.at[i])
    for i, part in enumerate((member, second)):
        level_step(2, part, 1, twice.at[2 * i], twice.at[2 * i + 1], own.at[i])
        own[i, pl.ds(RIM_AT, 1), :] = came_from(part)[pl.ds(RIM_AT, 1), :]
    for c in range(CHUNKS):
        rows = pl.ds(FIELDS * c, FIELDS)
        own[1, rows, :] = jnp.where(exists, own[1, rows, :], 0.0)


def join_kernel(stride, states, fixed, given, mine, far, low, high):
    kind = lax.axis_index("parts") % stride
    exists = second_part(stride)[1]
    early, outer = kind < stride // 2, (kind == 0) | (kind == stride - 1)
    for at in range(0, RECORD, FIELDS):
        rows = pl.ds(at, FIELDS)
        if at < FIRST_AT:
            one, two = states[0, rows, :], states[1, rows, :]
        else:
            part = pl.ds(at - FIRST_AT, FIELDS)
            absent = 1.0 if at == DIAG_AT else 0.0
            one, two = fixed[part, :], jnp.where(exists, given[part, :], absent)
        mine[rows, :] = one
        far[rows, :] = jnp.where(outer, two, one)
        low[rows, :] = jnp.where(early, one, two)
        high[rows, :] = jnp.where(early, two, one)


def gather_records(stride, parts, came, records):
    me = lax.axis_index("parts")
    swap = (stride == BLOCK) & (me % 2 == 0)
    mine, one, two, *side = came
    for at in range(0, RECORD, FIELDS):
        rows = pl.ds(at, FIELDS)
        blocks = {
            0: mine[rows, :],
            -1: jnp.where(swap, two[rows, :], one[rows, :]),
            1: jnp.where(swap, one[rows, :], two[rows, :]),
        }
        if side:
            blocks[-2], blocks[2] = side[0][rows, :], side[1][rows, :]
        for o, block in blocks.items():
            absent = 1.0 if at == DIAG_AT else 0.0
            there = (me + o >= 0) & (me + o < parts)
            records[o + REACH, rows, :] = jnp.where(there, block, absent) if o else block


def state_of(record):
    return [record[pl.ds(FIELDS * c, FIELDS), :] for c in range(CHUNKS)]


def ends_of(record):
    first = record[pl.ds(FIRST_AT, FIELDS), :].astype(jnp.int32)
    second = record[pl.ds(SECOND_AT, FIELDS), :].astype(jnp.int32)
    return first, second


def diag_of(record):
    return record[pl.ds(DIAG_AT, FIELDS), :]


def rim_of(record, blocks):
    slots = wide(record[pl.ds(RIM_AT, 1), :].astype(jnp.int32))
    lane, high = slots & (TILE - 1), slots >> 7
    found = take(blocks[0], lane)
    for c in range(1, CHUNKS):
        found = jnp.where(high == c, take(blocks[c], lane), found)
    return found


def difference(local, ghosts, field, first, second):
    near = [local[pl.ds(FIELDS * c + field, 1), :] for c in range(CHUNKS)]
    far = [one[pl.ds(field, 1), :] for one in ghosts]
    return look_up(near, first) - look_up(near + far if len(far) > 1 else far, second)


def first_lam(record, ghosts):
    first, second = ends_of(record)
    normal = [difference(record, ghosts, k, first, second) for k in range(3)]
    speed = sum(normal[k] * difference(record, ghosts, 3 + k, first, second) for k in range(3))
    return normal, jnp.maximum(0.0, -speed / diag_of(record))


def add_up(force, first, second, heads, rows):
    for k in range(3):
        head = force[k].astype(jnp.bfloat16).astype(jnp.float32)
        rows[pl.ds(k, FIELDS, stride=FIELDS), :] = force[k] - head
        rows[pl.ds(3 + k, FIELDS, stride=FIELDS), :] = head
    empty = jnp.zeros((FIELDS, TILE), jnp.float32)
    pad = [empty] * (len(heads) % 2)
    left, right = [], []
    for t in range(FIELDS):
        value = rows[pl.ds(FIELDS * t, FIELDS), :]
        for index, limit, signed in ((first, CHUNKS, value), (second, EXT_CHUNKS, -value)):
            if min(heads) >= limit:
                continue
            row = index[t : t + 1]
            high = wide(row >> 7)
            groups = [jnp.where(high == h, signed, 0.0) if h < limit else empty for h in heads]
            left.append(jnp.concatenate(groups + pad, axis=0))
            right.append(one_hot(row & (TILE - 1)))
    total = 0.0
    for k in range(0, len(left), 2):
        total += lax.dot_general(
            jnp.concatenate(left[k : k + 2], axis=1).astype(jnp.bfloat16),
            jnp.concatenate(right[k : k + 2], axis=1),
            NT,
            preferred_element_type=jnp.float32,
        )
    blocks = [total[FIELDS * k : FIELDS * (k + 1)] for k in range(len(heads))]
    return {h: block + pltpu.roll(block, 3, 0) for h, block in zip(heads, blocks)}


def moved(was, here, incoming, back_row):
    place = wide(back_row)
    extra = jnp.where(place > 0, take(incoming, jnp.maximum(place - 1, 0)), 0.0)
    field = rows_iota((FIELDS, TILE))
    gain = wide(was[6:7]) * (here + extra)
    return was + jnp.where((field >= 3) & (field < 6), gain, 0.0)


def near_kernel(stride, parts, *refs):
    came, (heads, tails, coupled, contacts, records, rims) = refs[:3], refs[3:]
    gather_records(stride, parts, came, records)
    for k in (-1, 1):
        record = records.at[REACH + k]
        rims[REACH + k] = rim_of(record, state_of(record))
    normal, lam = first_lam(records.at[REACH], (rims.at[REACH - 1], rims.at[REACH + 1]))
    for k, one in enumerate((*normal, lam)):
        contacts[k] = one
    head = lam.astype(jnp.bfloat16).astype(jnp.float32)
    both = jnp.concatenate([head, lam - head], axis=0).astype(jnp.bfloat16)
    total = jnp.zeros((FIELDS, TILE), jnp.float32)
    for t in range(heads.shape[0]):
        main = lax.dot_general(both, heads[t], NT, preferred_element_type=jnp.float32)
        rest = lax.dot_general(both, tails[t], NT, preferred_element_type=jnp.float32)
        whole = main[:FIELDS] + main[FIELDS:] + rest[:FIELDS]
        total = jnp.where(rows_iota((FIELDS, TILE)) == t, whole, total)
    coupled[...] = total


def middle_kernel(stride, parts, count, *refs):
    came, known = refs[:count], refs[count]
    stage, back_here, fixed_out, gathered, rims, rows, state_next, rims_next = refs[count + 1 :]
    gather_records(stride, parts, came, gathered)
    records = {o: gathered.at[o + REACH] for o in range(-REACH, REACH + 1)}
    rim = {o: rims.at[o + REACH] for o in records}
    rim_next = {o: rims_next.at[o + 1] for o in (-1, 0, 1)}
    left, right = CHUNKS, CHUNKS + 1
    local = list(range(CHUNKS))
    for o, record in records.items():
        rim[o][...] = rim_of(record, state_of(record))
    heads = {-2: [right], -1: local + [right], 0: local + [left, right], 1: local + [left], 2: [left]}
    ghosts = {o: (rim[o - 1], rim[o + 1]) for o in (-1, 1)}
    ghosts.update({-2: (rim[-1],), 2: (rim[1],)})
    sums, contacts = {}, {}
    for o, record in records.items():
        contacts[o] = first_lam(record, ghosts[o]) if o else ([known[k] for k in range(3)], known[3])
    for o, record in records.items():
        normal, lam = contacts[o]
        first, second = ends_of(record)
        force = [one * lam for one in normal]
        sums[o] = add_up(force, first, second, heads[o], rows.at[o + REACH])
    for o in (-1, 0, 1):
        incoming = sums[o - 1][right] + sums[o + 1][left]
        back = inverse([records[o][pl.ds(RIM_AT, 1), :]])
        if o == 0:
            back_here[...] = back
        blocks = [
            moved(was, sums[o][c], incoming, back[c : c + 1])
            for c, was in enumerate(state_of(records[o]))
        ]
        rim_next[o][...] = rim_of(records[o], blocks)
        for c in range(CHUNKS):
            state_next[o + 1, pl.ds(FIELDS * c, FIELDS), :] = blocks[c]
    ghosts = {-1: (rim_next[0],), 0: (rim_next[-1], rim_next[1]), 1: (rim_next[0],)}
    for o in (-1, 0, 1):
        normal, lam = contacts[o]
        first, second = ends_of(records[o])
        state = state_next.at[o + 1]
        speed = sum(
            normal[k] * difference(state, ghosts[o], 3 + k, first, second) for k in range(3)
        )
        for k in range(3):
            stage[o + 1, k] = normal[k]
        stage[o + 1, 3] = lam
        stage[o + 1, 4] = speed
        fixed_out[o + 1] = records[o][pl.ds(FIRST_AT, FIXED), :]


def last_kernel(
    parts, mine, stage, back, here, chip, mid, other, fixed, velocity, impulse, rows
):
    me = lax.axis_index("parts")
    odd = me % 2 == 1
    late = parts - EDGE
    apart = (me == EDGE) | (me == EDGE - 1) | (me == late) | (me == late - 1)
    across = jnp.where(apart, mid[...], other[...])
    across = jnp.where((me > 0) & (me < parts - 1), across, 0.0)
    coupled = {
        -1: jnp.where(odd, chip[...], across),
        0: here[...],
        1: jnp.where(odd, across, chip[...]),
    }
    sums = {}
    for o, heads in ((-1, [CHUNKS + 1]), (0, list(range(CHUNKS))), (1, [CHUNKS])):
        record = fixed.at[o + 1]
        lam = stage[o + 1, 3]
        diag = record[pl.ds(DIAG_AT - FIRST_AT, FIELDS), :]
        lam = jnp.maximum(0.0, lam - (coupled[o] + stage[o + 1, 4]) / diag)
        if o == 0:
            impulse[...] = lam
        first = record[pl.ds(0, FIELDS), :].astype(jnp.int32)
        second = record[pl.ds(SECOND_AT - FIRST_AT, FIELDS), :].astype(jnp.int32)
        force = [stage[o + 1, k] * lam for k in range(3)]
        sums[o] = add_up(force, first, second, heads, rows.at[o + 1])
    incoming = sums[-1][CHUNKS + 1] + sums[1][CHUNKS]
    for c, was in enumerate(state_of(mine)):
        block = moved(was, sums[0][c], incoming, back[pl.ds(c, 1), :])
        velocity[:, pl.ds(c * TILE, TILE)] = block[3:6]


def call(kernel, out_shape, inputs, name, space=pltpu.VMEM, scratch=()):
    many = isinstance(out_shape, (tuple, list))
    vmem = pl.BlockSpec(memory_space=pltpu.VMEM)
    return pl.pallas_call(
        kernel,
        out_shape=out_shape,
        in_specs=[pl.BlockSpec(memory_space=space)] * len(inputs),
        out_specs=[vmem] * len(out_shape) if many else vmem,
        scratch_shapes=list(scratch),
        compiler_params=FROM_HBM if space == pltpu.HBM else PARAMS,
        name=name,
    )(*inputs)


def second_parts(parts, stride):
    pairs = []
    for i in range(parts):
        step = -stride if i % stride < stride // 2 else stride
        to = i + step
        if not 0 <= to < parts:
            to = i + (stride // 2 if step < 0 else -(stride // 2))
        pairs.append((i, to))
    return pairs


def next_pairs(parts):
    late = parts - EDGE
    most = {i: i + 1 if i % 2 else i - 1 for i in range(parts)}
    edge = {i: i ^ 1 for i in range(parts)}
    for i, j in ((0, EDGE), (EDGE - 1, late - 1), (late, parts - 1)):
        most[i], most[j] = j, i
    for at in (EDGE, late):
        for i, j in ((at - 1, at), (at - 2, at + 2), (at + 1, at + 3)):
            edge[i], edge[j] = j, i
    return list(most.items()), list(edge.items())


def body(positions, velocity, inv_mass, swap_lists, rim_list, contact_pair, delassus):
    parts = lax.axis_size("parts")
    stride = parts // GROUP
    grains = positions.shape[1]
    contacts = contact_pair.shape[1]
    tiles = delassus.shape[0]
    reach = 2 * REACH + 1
    float32 = functools.partial(jax.ShapeDtypeStruct, dtype=jnp.float32)
    vmem = lambda *shape: pltpu.VMEM(shape, jnp.float32)
    send = functools.partial(lax.ppermute, axis_name="parts")
    inputs = (
        positions,
        velocity,
        inv_mass.reshape(CHUNKS, TILE),
        swap_lists,
        rim_list.reshape(1, TILE),
    )
    packed = call(
        pack_kernel,
        float32((GROUP, RAW, TILE)),
        inputs,
        "pack",
        pltpu.HBM,
        [pltpu.VMEM(one.shape, one.dtype) for one in inputs]
        + [pltpu.SemaphoreType.DMA((5,))],
    )
    classes = [[r + stride * (GROUP - 1 - k) for k in range(GROUP)] for r in range(stride)]
    raw = lax.all_to_all(packed, "parts", 0, 0, axis_index_groups=classes)

    half = jax.ShapeDtypeStruct(delassus.shape, jnp.bfloat16)
    fixed, heads, tails = call(
        fixed_kernel, (float32((FIXED, TILE)), half, half), (contact_pair, delassus), "fixed"
    )
    given = send(fixed, perm=second_parts(parts, stride))

    states = call(
        functools.partial(compose_kernel, stride),
        float32((2, FIRST_AT, TILE)),
        (raw,),
        "compose",
        scratch=[vmem(GROUP, FIRST_AT, TILE), vmem(4, FIRST_AT, TILE)],
    )
    record = (RECORD, TILE)
    mine, far, low, high = call(
        functools.partial(join_kernel, stride),
        [float32(record)] * 4,
        (states, fixed, given),
        "join",
    )
    within = [(i, i ^ 1) for i in range(parts)]
    if stride == BLOCK:
        from_far = send(far, perm=[(i, i ^ 3) for i in range(parts)])
        near = (mine, send(mine, perm=within), from_far)
        beyond = [(i, i ^ 2) for i in range(parts)]
        came = (*near, send(low, perm=beyond), send(high, perm=beyond))
    else:
        shifts = [[(i, (i + by) % parts) for i in range(parts)] for by in (1, -1, 2, -2)]
        came = (mine, *[send(mine, perm=shift) for shift in shifts])
        near = came[:3]

    here, known = call(
        functools.partial(near_kernel, stride, parts),
        (float32((tiles, TILE)), float32((4, tiles, TILE))),
        (*near, heads, tails),
        "near",
        scratch=[vmem(reach, *record), vmem(reach, FIELDS, TILE)],
    )
    most, edge = next_pairs(parts)
    other = send(here, perm=most)
    chip = send(here, perm=within)
    mid = send(here, perm=edge)
    stage, back, contact_rows = call(
        functools.partial(middle_kernel, stride, parts, len(came)),
        (
            float32((3, 5, FIELDS, TILE)),
            jax.ShapeDtypeStruct((FIELDS, TILE), jnp.int32),
            float32((3, FIXED, TILE)),
        ),
        (*came, known),
        "middle",
        scratch=[
            vmem(reach, *record),
            vmem(reach, FIELDS, TILE),
            vmem(reach, FIELDS * FIELDS, TILE),
            vmem(3, CHUNKS * FIELDS, TILE),
            vmem(3, FIELDS, TILE),
        ],
    )
    new_velocity, impulse = call(
        functools.partial(last_kernel, parts),
        (float32((3, grains)), float32((tiles, TILE))),
        (mine, stage, back, here, chip, mid, other, contact_rows),
        "last",
        scratch=[vmem(3, FIELDS * FIELDS, TILE)],
    )
    return (new_velocity, impulse.reshape(contacts))


def solution(mesh):
    in_specs = (
        P(None, "parts"),
        P(None, "parts"),
        P("parts"),
        P(None, "parts"),
        P("parts"),
        P(None, "parts"),
        P("parts", None, None),
    )
    out_specs = (P(None, "parts"), P("parts"))
    return jax.shard_map(body, mesh=mesh, in_specs=in_specs, out_specs=out_specs, check_vma=False)
```

time: 30 us -> 26.6 us (0.89)
  the two profiles are of different devices: /device:TPU:0 before, /device:TPU:8 now
where the time goes in v2:
time: 26.6 us; the launch traced here: 26.2 us
  starting transfers between devices  15.2 us (57%)
  Pallas kernels  5.36 us (20%)
  waiting for transfers between devices  3.97 us (15%)
  local copies, waits for them, and re-layouts  1.05 us (4%)
  between operations  0.68 us (3%)
    all_to_all x1, starting transfers between devices, body(): raw = lax.all_to_all(packed, 'parts', 0, 0, axis_index_groups=classes)  6.87 us
    pallas_call x7, Pallas kernels, call(): pl.pallas_call(kernel, out_shape=out_shape, in_specs=[pl.BlockSpec(memory...  5.36 us
    ppermute x1, waiting for transfers between devices, body(): mid = send(here, perm=edge)  2.4 us
    ppermute x2, starting transfers between devices, body(): came = (*near, send(low, perm=beyond), send(high, perm=beyond))  2.03 us
    ppermute x1, starting transfers between devices, body(): near = (mine, send(mine, perm=within), from_far)  1.97 us
    all_to_all x1, waiting for transfers between devices, body(): raw = lax.all_to_all(packed, 'parts', 0, 0, axis_index_groups=classes)  1.55 us
    ppermute x1, starting transfers between devices, body(): given = send(fixed, perm=second_parts(parts, stride))  1.52 us
    ppermute x1, starting transfers between devices, body(): other = send(here, perm=most)  1.27 us
  transfers between devices with their start and end apart: 9, of which 2 were waited for; matrix products, arithmetic and copies ran while one was open for 0% of the time, Pallas kernels for 11%

profile of v2, /device:TPU:8, one launch (start us, length us, event | category | flops | bytes accessed | tf_op | source)
XLA Modules:
  0.0 26.2 jit_solution(4824296085315981046)
XLA Ops:
  0.6 1.5 %pack.1 = f32[8,40,128]{2,1,0:T(8,128)} custom-call(f32[3,512]{1,0:T(4,128)} %refs_0_.1, f32[3,512]{1,0:T(4,128)} %refs_1_.1, f32[4,128]{1,0:T(4,128)} %bitcast.3, s32[3,256]{1,0:T(4,128)} %refs_3_.1, s32[1,128]{1,0:T(1,128)} %bitcast.4), custom_call_target="tpu_custom_call" | custom-call | tf_op jit(solution)/shard_map/pack/pallas_call | solution.py:386
  2.1 0.0 copy-start.1
  2.1 6.9 %all-to-all-start = ((f32[8,40,128]{2,1,0:T(8,128)}), f32[8,40,128]{2,1,0:T(8,128)S(1)}, u32[]{:S(2)}, u32[]{:S(2)}) async-start(f32[8,40,128]{2,1,0:T(8,128)} %pack.1), calls=%async_computation | async-start | bytes 327680 | tf_op jit(solution)/shard_map/all_to_all | solution.py:447
  9.0 0.0 copy-done.1
  9.0 0.0 copy-start
  9.0 1.0 %copy-done = f32[8,128,128]{2,1,0:T(8,128)S(1)} copy-done((f32[8,128,128]{2,1,0:T(8,128)S(1)}, f32[8,128,128]{2,1,0:T(8,128)}, u32[]{:S(2)}) %copy-start) | copy-done | bytes 524312
  10.0 0.1 fixed.1
  10.1 1.5 %collective-permute-start = (f32[24,128]{1,0:T(8,128)S(1)}, f32[24,128]{1,0:T(8,128)S(1)}, u32[]{:S(2)}, u32[]{:S(2)}) collective-permute-start(f32[24,128]{1,0:T(8,128)S(1)} %get-tuple-element.16.fixed), channel_id=1, source_target_pairs={{0,2},{1,3},{2,6},{3,7},{4,0},{5,1},{6,10},{7,11},{8,4},{9,5},{10,... | collective-permute-start | bytes 36872 | tf_op jit(solution)/shard_map/ppermute | solution.py:453
  11.7 1.6 %all-to-all-done.raw = f32[8,40,128]{2,1,0:T(8,128)S(1)} async-done(((f32[8,40,128]{2,1,0:T(8,128)}), f32[8,40,128]{2,1,0:T(8,128)S(1)}, u32[]{:S(2)}, u32[]{:S(2)}) %all-to-all-start) | async-done | bytes 163872 | tf_op jit(solution)/shard_map/all_to_all | solution.py:447
  13.2 0.9 %compose.1.states = f32[2,32,128]{2,1,0:T(8,128)S(1)} custom-call(f32[8,40,128]{2,1,0:T(8,128)S(1)} %all-to-all-done.raw), custom_call_target="tpu_custom_call" | custom-call | tf_op jit(solution)/shard_map/compose/pallas_call | solution.py:386
  14.1 0.0 collective-permute-done.given
  14.1 0.4 %collective-permute-start.2 = (f32[56,128]{1,0:T(8,128)S(1)}, f32[56,128]{1,0:T(8,128)S(1)}, u32[]{:S(2)}, u32[]{:S(2)}) collective-permute-start(f32[56,128]{1,0:T(8,128)S(1)} %get-tuple-element.18), channel_id=1, source_target_pairs={{0,3},{1,2},{2,1},{3,0},{4,7},{5,6},{6,5},{7,4},{8,11},{9,10},{10,... | collective-permute-start | bytes 86024 | tf_op jit(solution)/shard_map/ppermute | solution.py:471
  14.5 2.0 %collective-permute-start.1 = (f32[56,128]{1,0:T(8,128)S(1)}, f32[56,128]{1,0:T(8,128)S(1)}, u32[]{:S(2)}, u32[]{:S(2)}) collective-permute-start(f32[56,128]{1,0:T(8,128)S(1)} %get-tuple-element.17.refs_0_.mine), channel_id=1, source_target_pairs={{0,1},{1,0},{2,3},{3,2},{4,5},{5,4},{6,7},{7,6},{8,9},{9,8},{10,11... | collective-permute-start | bytes 86024 | tf_op jit(solution)/shard_map/ppermute | solution.py:472
  16.5 0.0 collective-permute-start.3
  16.5 2.0 %collective-permute-start.4 = (f32[56,128]{1,0:T(8,128)S(1)}, f32[56,128]{1,0:T(8,128)S(1)}, u32[]{:S(2)}, u32[]{:S(2)}) collective-permute-start(f32[56,128]{1,0:T(8,128)S(1)} %get-tuple-element.20), channel_id=1, source_target_pairs={{0,2},{1,3},{2,0},{3,1},{4,6},{5,7},{6,4},{7,5},{8,10},{9,11},{10,... | collective-permute-start | bytes 86024 | tf_op jit(solution)/shard_map/ppermute | solution.py:474
  18.5 0.0 collective-permute-done.2.refs_2_
  18.5 0.0 collective-permute-done.1.refs_1_
  18.5 0.5 %near.1 = (f32[8,128]{1,0:T(8,128)S(1)}, f32[4,8,128]{2,1,0:T(8,128)S(1)}) custom-call(f32[56,128]{1,0:T(8,128)S(1)} %get-tuple-element.17.refs_0_.mine, f32[56,128]{1,0:T(8,128)S(1)} %collective-permute-done.1.refs_1_, f32[56,128]{1,0:T(8,128)S(1)} %collective-permute-done.2.refs_2_, bf16[8,128,128]{2,1,0:T(8,128)(2,1)S(1)} %get-tuple-element.21.refs_3_, ...), custom_call_target="tpu_custom_call" | custom-call | tf_op jit(solution)/shard_map/near/pallas_call | solution.py:386
  19.1 1.3 %collective-permute-start.7 = (f32[8,128]{1,0:T(8,128)S(1)}, f32[8,128]{1,0:T(8,128)S(1)}, u32[]{:S(2)}, u32[]{:S(2)}) collective-permute-start(f32[8,128]{1,0:T(8,128)S(1)} %get-tuple-element.26.here), channel_id=1, source_target_pairs={{0,8},{1,2},{2,1},{3,4},{4,3},{5,6},{6,5},{7,23},{8,0},{9,10},{10,... | collective-permute-start | bytes 12296 | tf_op jit(solution)/shard_map/ppermute | solution.py:488
  20.3 0.4 %collective-permute-start.6 = (f32[8,128]{1,0:T(8,128)S(1)}, f32[8,128]{1,0:T(8,128)S(1)}, u32[]{:S(2)}, u32[]{:S(2)}) collective-permute-start(f32[8,128]{1,0:T(8,128)S(1)} %get-tuple-element.26.here), channel_id=1, source_target_pairs={{0,1},{1,0},{2,3},{3,2},{4,5},{5,4},{6,10},{7,8},{8,7},{9,11},{10,... | collective-permute-start | bytes 12296 | tf_op jit(solution)/shard_map/ppermute | solution.py:490
  20.7 0.8 %collective-permute-start.5 = (f32[8,128]{1,0:T(8,128)S(1)}, f32[8,128]{1,0:T(8,128)S(1)}, u32[]{:S(2)}, u32[]{:S(2)}) collective-permute-start(f32[8,128]{1,0:T(8,128)S(1)} %get-tuple-element.26.here), channel_id=1, source_target_pairs={{0,1},{1,0},{2,3},{3,2},{4,5},{5,4},{6,7},{7,6},{8,9},{9,8},{10,11... | collective-permute-start | bytes 12296 | tf_op jit(solution)/shard_map/ppermute | solution.py:489
  21.5 0.0 collective-permute-done.3.refs_3_
  21.5 0.0 collective-permute-done.4.refs_4_
  21.5 1.3 %middle.1 = (f32[3,5,8,128]{3,2,1,0:T(8,128)S(1)}, s32[8,128]{1,0:T(8,128)S(1)}, f32[3,24,128]{2,1,0:T(8,128)S(1)}) custom-call(f32[56,128]{1,0:T(8,128)S(1)} %get-tuple-element.17.refs_0_.mine, f32[56,128]{1,0:T(8,128)S(1)} %collective-permute-done.1.refs_1_, f32[56,128]{1,0:T(8,128)S(1)} %collective-permute-done.2.refs_2_, ...), custom_call_target="tpu_custom_call" | custom-call | tf_op jit(solution)/shard_map/middle/pallas_call | solution.py:386
  22.8 0.0 collective-permute-done.7.other
  22.8 2.4 %collective-permute-done.6.mid = f32[8,128]{1,0:T(8,128)S(1)} collective-permute-done((f32[8,128]{1,0:T(8,128)S(1)}, f32[8,128]{1,0:T(8,128)S(1)}, u32[]{:S(2)}, u32[]{:S(2)}) %collective-permute-start.6) | collective-permute-done | bytes 4128 | tf_op jit(solution)/shard_map/ppermute | solution.py:490
  25.2 0.0 collective-permute-done.5.chip
  25.2 1.1 %last.1 = (f32[3,512]{1,0:T(4,128)}, f32[8,128]{1,0:T(8,128)}) custom-call(f32[56,128]{1,0:T(8,128)S(1)} %get-tuple-element.17.refs_0_.mine, f32[3,5,8,128]{3,2,1,0:T(8,128)S(1)} %get-tuple-element.24.stage, s32[8,128]{1,0:T(8,128)S(1)} %get-tuple-element.25.back, f32[8,128]{1,0:T(8,128)S(1)} %get-tuple-element.26.here, ...), custom_call_target="tpu_custom_call" | custom-call | tf_op jit(solution)/shard_map/last/pallas_call | solution.py:386
  (1 shorter events, 0.0 us)
Async XLA Ops:
  2.1 6.9 %copy-start.1 = (s32[2,1024]{1,0:T(2,128)S(1)}, s32[2,1024]{1,0:T(2,128)}, u32[]{:S(2)}) copy-start(s32[2,1024]{1,0:T(2,128)} %pair.1) | copy-start | bytes 24580
  2.1 11.1 %all-to-all-start = ((f32[8,40,128]{2,1,0:T(8,128)}), f32[8,40,128]{2,1,0:T(8,128)S(1)}, u32[]{:S(2)}, u32[]{:S(2)}) async-start(f32[8,40,128]{2,1,0:T(8,128)} %pack.1), calls=%async_computation | async-start | bytes 327680 | tf_op jit(solution)/shard_map/all_to_all | solution.py:447
  9.0 1.0 %copy-start = (f32[8,128,128]{2,1,0:T(8,128)S(1)}, f32[8,128,128]{2,1,0:T(8,128)}, u32[]{:S(2)}) copy-start(f32[8,128,128]{2,1,0:T(8,128)} %tiles.1) | copy-start | bytes 1572868
  10.1 3.9 %collective-permute-start = (f32[24,128]{1,0:T(8,128)S(1)}, f32[24,128]{1,0:T(8,128)S(1)}, u32[]{:S(2)}, u32[]{:S(2)}) collective-permute-start(f32[24,128]{1,0:T(8,128)S(1)} %get-tuple-element.16.fixed), channel_id=1, source_target_pairs={{0,2},{1,3},{2,6},{3,7},{4,0},{5,1},{6,10},{7,11},{8,4},{9,5},{10,... | collective-permute-start | bytes 36872 | tf_op jit(solution)/shard_map/ppermute | solution.py:453
  14.1 4.4 %collective-permute-start.2 = (f32[56,128]{1,0:T(8,128)S(1)}, f32[56,128]{1,0:T(8,128)S(1)}, u32[]{:S(2)}, u32[]{:S(2)}) collective-permute-start(f32[56,128]{1,0:T(8,128)S(1)} %get-tuple-element.18), channel_id=1, source_target_pairs={{0,3},{1,2},{2,1},{3,0},{4,7},{5,6},{6,5},{7,4},{8,11},{9,10},{10,... | collective-permute-start | bytes 86024 | tf_op jit(solution)/shard_map/ppermute | solution.py:471
  14.5 4.0 %collective-permute-start.1 = (f32[56,128]{1,0:T(8,128)S(1)}, f32[56,128]{1,0:T(8,128)S(1)}, u32[]{:S(2)}, u32[]{:S(2)}) collective-permute-start(f32[56,128]{1,0:T(8,128)S(1)} %get-tuple-element.17.refs_0_.mine), channel_id=1, source_target_pairs={{0,1},{1,0},{2,3},{3,2},{4,5},{5,4},{6,7},{7,6},{8,9},{9,8},{10,11... | collective-permute-start | bytes 86024 | tf_op jit(solution)/shard_map/ppermute | solution.py:472
  16.5 5.0 %collective-permute-start.3 = (f32[56,128]{1,0:T(8,128)S(1)}, f32[56,128]{1,0:T(8,128)S(1)}, u32[]{:S(2)}, u32[]{:S(2)}) collective-permute-start(f32[56,128]{1,0:T(8,128)S(1)} %get-tuple-element.19), channel_id=1, source_target_pairs={{0,2},{1,3},{2,0},{3,1},{4,6},{5,7},{6,4},{7,5},{8,10},{9,11},{10,... | collective-permute-start | bytes 86024 | tf_op jit(solution)/shard_map/ppermute | solution.py:474
  16.5 5.0 %collective-permute-start.4 = (f32[56,128]{1,0:T(8,128)S(1)}, f32[56,128]{1,0:T(8,128)S(1)}, u32[]{:S(2)}, u32[]{:S(2)}) collective-permute-start(f32[56,128]{1,0:T(8,128)S(1)} %get-tuple-element.20), channel_id=1, source_target_pairs={{0,2},{1,3},{2,0},{3,1},{4,6},{5,7},{6,4},{7,5},{8,10},{9,11},{10,... | collective-permute-start | bytes 86024 | tf_op jit(solution)/shard_map/ppermute | solution.py:474
  19.1 3.7 %collective-permute-start.7 = (f32[8,128]{1,0:T(8,128)S(1)}, f32[8,128]{1,0:T(8,128)S(1)}, u32[]{:S(2)}, u32[]{:S(2)}) collective-permute-start(f32[8,128]{1,0:T(8,128)S(1)} %get-tuple-element.26.here), channel_id=1, source_target_pairs={{0,8},{1,2},{2,1},{3,4},{4,3},{5,6},{6,5},{7,23},{8,0},{9,10},{10,... | collective-permute-start | bytes 12296 | tf_op jit(solution)/shard_map/ppermute | solution.py:488
  20.3 4.8 %collective-permute-start.6 = (f32[8,128]{1,0:T(8,128)S(1)}, f32[8,128]{1,0:T(8,128)S(1)}, u32[]{:S(2)}, u32[]{:S(2)}) collective-permute-start(f32[8,128]{1,0:T(8,128)S(1)} %get-tuple-element.26.here), channel_id=1, source_target_pairs={{0,1},{1,0},{2,3},{3,2},{4,5},{5,4},{6,10},{7,8},{8,7},{9,11},{10,... | collective-permute-start | bytes 12296 | tf_op jit(solution)/shard_map/ppermute | solution.py:490
  20.7 4.5 %collective-permute-start.5 = (f32[8,128]{1,0:T(8,128)S(1)}, f32[8,128]{1,0:T(8,128)S(1)}, u32[]{:S(2)}, u32[]{:S(2)}) collective-permute-start(f32[8,128]{1,0:T(8,128)S(1)} %get-tuple-element.26.here), channel_id=1, source_target_pairs={{0,1},{1,0},{2,3},{3,2},{4,5},{5,4},{6,7},{7,6},{8,9},{9,8},{10,11... | collective-permute-start | bytes 12296 | tf_op jit(solution)/shard_map/ppermute | solution.py:489

commit v3 on v2

--- a/solution.py
+++ b/solution.py
@@ -23,7 +23,6 @@
 RAW = 40
 FIXED = RECORD - FIRST_AT
 BLOCK = 4
-EDGE = 8
 PARAMS = pltpu.CompilerParams(vmem_limit_bytes=32 * 2**20)
 FROM_HBM = pltpu.CompilerParams(vmem_limit_bytes=63 * 2**20)
 NT = (((1,), (1,)), ((), ()))
@@ -54,7 +53,9 @@
 
 
 def one_hot(low_row):
-    return (rows_iota((TILE, TILE)) == low_row).astype(jnp.float32).astype(jnp.bfloat16)
+    row = jnp.broadcast_to(low_row.astype(jnp.float32).astype(jnp.bfloat16), (TILE, TILE))
+    column = rows_iota((TILE, TILE)).astype(jnp.float32).astype(jnp.bfloat16)
+    return jnp.where(row == column, jnp.bfloat16(1), jnp.bfloat16(0))
 
 
 def inverse(slot_rows):
@@ -110,9 +111,10 @@
         out[pl.ds(t, 1), :] = pair[pl.ds(0, 1), lanes].astype(jnp.float32)
         out[pl.ds(FIELDS + t, 1), :] = pair[pl.ds(1, 1), lanes].astype(jnp.float32)
         tile = tiles[t]
-        head = tile.astype(jnp.bfloat16)
+        turned = tile.T
+        head = turned.astype(jnp.bfloat16)
         heads[t] = head
-        tails[t] = (tile - head.astype(jnp.float32)).astype(jnp.bfloat16)
+        tails[t] = (turned - head.astype(jnp.float32)).astype(jnp.bfloat16)
         diag = jnp.sum(jnp.where(eye, tile, 0.0), axis=0, keepdims=True)
         out[pl.ds(2 * FIELDS + t, 1), :] = diag
 
@@ -292,8 +294,8 @@
     both = jnp.concatenate([head, lam - head], axis=0).astype(jnp.bfloat16)
     total = jnp.zeros((FIELDS, TILE), jnp.float32)
     for t in range(heads.shape[0]):
-        main = lax.dot_general(both, heads[t], NT, preferred_element_type=jnp.float32)
-        rest = lax.dot_general(both, tails[t], NT, preferred_element_type=jnp.float32)
+        main = jnp.dot(both, heads[t], preferred_element_type=jnp.float32)
+        rest = jnp.dot(both, tails[t], preferred_element_type=jnp.float32)
         whole = main[:FIELDS] + main[FIELDS:] + rest[:FIELDS]
         total = jnp.where(rows_iota((FIELDS, TILE)) == t, whole, total)
     coupled[...] = total
@@ -353,8 +355,7 @@
 ):
     me = lax.axis_index("parts")
     odd = me % 2 == 1
-    late = parts - EDGE
-    apart = (me == EDGE) | (me == EDGE - 1) | (me == late) | (me == late - 1)
+    apart = (me % (2 * BLOCK) == BLOCK) | (me % (2 * BLOCK) == BLOCK - 1)
     across = jnp.where(apart, mid[...], other[...])
     across = jnp.where((me > 0) & (me < parts - 1), across, 0.0)
     coupled = {
@@ -405,15 +406,24 @@
     return pairs
 
 
+def edges(parts):
+    return range(BLOCK, parts, 2 * BLOCK)
+
+
 def next_pairs(parts):
-    late = parts - EDGE
     most = {i: i + 1 if i % 2 else i - 1 for i in range(parts)}
     edge = {i: i ^ 1 for i in range(parts)}
-    for i, j in ((0, EDGE), (EDGE - 1, late - 1), (late, parts - 1)):
-        most[i], most[j] = j, i
-    for at in (EDGE, late):
+    ends = [0]
+    for at in edges(parts):
+        ends += [at - 1, at]
         for i, j in ((at - 1, at), (at - 2, at + 2), (at + 1, at + 3)):
             edge[i], edge[j] = j, i
+    ends.append(parts - 1)
+    closings = [(0, BLOCK), (ends[-2], parts - 1)]
+    for k in range(1, len(ends) - 4, 2):
+        closings.append((ends[k], ends[k + 2]) if k % 4 == 1 else (ends[k + 1], ends[k + 3]))
+    for i, j in closings:
+        most[i], most[j] = j, i
     return list(most.items()), list(edge.items())
 
 

time: 26.6 us -> 26.3 us (0.989)
  the two profiles are of different devices: /device:TPU:8 before, /device:TPU:0 now
where the time goes in v3:
time: 26.3 us; the launch traced here: 25.9 us
  starting transfers between devices  15.9 us (60%)
  Pallas kernels  5.35 us (20%)
  waiting for transfers between devices  2.94 us (11%)
  local copies, waits for them, and re-layouts  1.05 us (4%)
  between operations  0.68 us (3%)
    all_to_all x1, starting transfers between devices, body(): raw = lax.all_to_all(packed, 'parts', 0, 0, axis_index_groups=classes)  9.34 us
    pallas_call x7, Pallas kernels, call(): pl.pallas_call(kernel, out_shape=out_shape, in_specs=[pl.BlockSpec(memory...  5.35 us
    ppermute x2, starting transfers between devices, body(): came = (*near, send(low, perm=beyond), send(high, perm=beyond))  2.06 us
    all_to_all x1, waiting for transfers between devices, body(): raw = lax.all_to_all(packed, 'parts', 0, 0, axis_index_groups=classes)  1.98 us
    ppermute x1, starting transfers between devices, body(): given = send(fixed, perm=second_parts(parts, stride))  1.54 us
    unnamed x4, local copies, waits for them, and re-layouts  1.05 us
    ppermute x1, starting transfers between devices, body(): near = (mine, send(mine, perm=within), from_far)  0.85 us
    ppermute x1, starting transfers between devices, body(): mid = send(here, perm=edge)  0.8 us
  transfers between devices with their start and end apart: 9, of which 3 were waited for; matrix products, arithmetic and copies ran while one was open for 0% of the time, Pallas kernels for 11%

profile of v3, /device:TPU:0, one launch (start us, length us, event | category | flops | bytes accessed | tf_op | source)
XLA Modules:
  0.0 25.9 jit_solution(13956675925083113938)
XLA Ops:
  0.6 1.5 %pack.1 = f32[8,40,128]{2,1,0:T(8,128)} custom-call(f32[3,512]{1,0:T(4,128)} %refs_0_.1, f32[3,512]{1,0:T(4,128)} %refs_1_.1, f32[4,128]{1,0:T(4,128)} %bitcast.3, s32[3,256]{1,0:T(4,128)} %refs_3_.1, s32[1,128]{1,0:T(1,128)} %bitcast.4), custom_call_target="tpu_custom_call" | custom-call | tf_op jit(solution)/shard_map/pack/pallas_call | solution.py:387
  2.1 0.0 copy-start.1
  2.1 9.3 %all-to-all-start = ((f32[8,40,128]{2,1,0:T(8,128)}), f32[8,40,128]{2,1,0:T(8,128)S(1)}, u32[]{:S(2)}, u32[]{:S(2)}) async-start(f32[8,40,128]{2,1,0:T(8,128)} %pack.1), calls=%async_computation | async-start | bytes 327680 | tf_op jit(solution)/shard_map/all_to_all | solution.py:457
  11.5 0.0 copy-done.1
  11.5 0.0 copy-start
  11.5 1.0 %copy-done = f32[8,128,128]{2,1,0:T(8,128)S(1)} copy-done((f32[8,128,128]{2,1,0:T(8,128)S(1)}, f32[8,128,128]{2,1,0:T(8,128)}, u32[]{:S(2)}) %copy-start) | copy-done | bytes 524312
  12.5 0.2 fixed.1
  12.7 1.5 %collective-permute-start = (f32[24,128]{1,0:T(8,128)S(1)}, f32[24,128]{1,0:T(8,128)S(1)}, u32[]{:S(2)}, u32[]{:S(2)}) collective-permute-start(f32[24,128]{1,0:T(8,128)S(1)} %get-tuple-element.16.fixed), channel_id=1, source_target_pairs={{0,2},{1,3},{2,6},{3,7},{4,0},{5,1},{6,10},{7,11},{8,4},{9,5},{10,... | collective-permute-start | bytes 36872 | tf_op jit(solution)/shard_map/ppermute | solution.py:463
  14.3 2.0 %all-to-all-done.raw = f32[8,40,128]{2,1,0:T(8,128)S(1)} async-done(((f32[8,40,128]{2,1,0:T(8,128)}), f32[8,40,128]{2,1,0:T(8,128)S(1)}, u32[]{:S(2)}, u32[]{:S(2)}) %all-to-all-start) | async-done | bytes 163872 | tf_op jit(solution)/shard_map/all_to_all | solution.py:457
  16.2 0.9 %compose.1.states = f32[2,32,128]{2,1,0:T(8,128)S(1)} custom-call(f32[8,40,128]{2,1,0:T(8,128)S(1)} %all-to-all-done.raw), custom_call_target="tpu_custom_call" | custom-call | tf_op jit(solution)/shard_map/compose/pallas_call | solution.py:387
  17.1 0.0 collective-permute-done.given
  17.1 0.7 %collective-permute-start.2 = (f32[56,128]{1,0:T(8,128)S(1)}, f32[56,128]{1,0:T(8,128)S(1)}, u32[]{:S(2)}, u32[]{:S(2)}) collective-permute-start(f32[56,128]{1,0:T(8,128)S(1)} %get-tuple-element.18), channel_id=1, source_target_pairs={{0,3},{1,2},{2,1},{3,0},{4,7},{5,6},{6,5},{7,4},{8,11},{9,10},{10,... | collective-permute-start | bytes 86024 | tf_op jit(solution)/shard_map/ppermute | solution.py:481
  17.8 0.9 %collective-permute-start.1 = (f32[56,128]{1,0:T(8,128)S(1)}, f32[56,128]{1,0:T(8,128)S(1)}, u32[]{:S(2)}, u32[]{:S(2)}) collective-permute-start(f32[56,128]{1,0:T(8,128)S(1)} %get-tuple-element.17.refs_0_.mine), channel_id=1, source_target_pairs={{0,1},{1,0},{2,3},{3,2},{4,5},{5,4},{6,7},{7,6},{8,9},{9,8},{10,11... | collective-permute-start | bytes 86024 | tf_op jit(solution)/shard_map/ppermute | solution.py:482
  18.7 0.7 %collective-permute-start.3 = (f32[56,128]{1,0:T(8,128)S(1)}, f32[56,128]{1,0:T(8,128)S(1)}, u32[]{:S(2)}, u32[]{:S(2)}) collective-permute-start(f32[56,128]{1,0:T(8,128)S(1)} %get-tuple-element.19), channel_id=1, source_target_pairs={{0,2},{1,3},{2,0},{3,1},{4,6},{5,7},{6,4},{7,5},{8,10},{9,11},{10,... | collective-permute-start | bytes 86024 | tf_op jit(solution)/shard_map/ppermute | solution.py:484
  19.4 1.4 %collective-permute-start.4 = (f32[56,128]{1,0:T(8,128)S(1)}, f32[56,128]{1,0:T(8,128)S(1)}, u32[]{:S(2)}, u32[]{:S(2)}) collective-permute-start(f32[56,128]{1,0:T(8,128)S(1)} %get-tuple-element.20), channel_id=1, source_target_pairs={{0,2},{1,3},{2,0},{3,1},{4,6},{5,7},{6,4},{7,5},{8,10},{9,11},{10,... | collective-permute-start | bytes 86024 | tf_op jit(solution)/shard_map/ppermute | solution.py:484
  20.7 0.0 collective-permute-done.2.refs_2_
  20.7 0.0 collective-permute-done.1.refs_1_
  20.8 0.4 %near.1 = (f32[8,128]{1,0:T(8,128)S(1)}, f32[4,8,128]{2,1,0:T(8,128)S(1)}) custom-call(f32[56,128]{1,0:T(8,128)S(1)} %get-tuple-element.17.refs_0_.mine, f32[56,128]{1,0:T(8,128)S(1)} %collective-permute-done.1.refs_1_, f32[56,128]{1,0:T(8,128)S(1)} %collective-permute-done.2.refs_2_, bf16[8,128,128]{2,1,0:T(8,128)(2,1)S(1)} %get-tuple-element.21.refs_3_, ...), custom_call_target="tpu_custom_call" | custom-call | tf_op jit(solution)/shard_map/near/pallas_call | solution.py:387
  21.2 0.6 %collective-permute-start.7 = (f32[8,128]{1,0:T(8,128)S(1)}, f32[8,128]{1,0:T(8,128)S(1)}, u32[]{:S(2)}, u32[]{:S(2)}) collective-permute-start(f32[8,128]{1,0:T(8,128)S(1)} %get-tuple-element.26.here), channel_id=1, source_target_pairs={{0,4},{1,2},{2,1},{3,11},{4,0},{5,6},{6,5},{7,8},{8,7},{9,10},{10,... | collective-permute-start | bytes 12296 | tf_op jit(solution)/shard_map/ppermute | solution.py:498
  21.8 0.8 %collective-permute-start.6 = (f32[8,128]{1,0:T(8,128)S(1)}, f32[8,128]{1,0:T(8,128)S(1)}, u32[]{:S(2)}, u32[]{:S(2)}) collective-permute-start(f32[8,128]{1,0:T(8,128)S(1)} %get-tuple-element.26.here), channel_id=1, source_target_pairs={{0,1},{1,0},{2,6},{3,4},{4,3},{5,7},{6,2},{7,5},{8,9},{9,8},{10,14... | collective-permute-start | bytes 12296 | tf_op jit(solution)/shard_map/ppermute | solution.py:500
  22.6 0.0 collective-permute-start.5
  22.6 0.0 collective-permute-done.3.refs_3_
  22.6 0.6 %collective-permute-done.4.refs_4_ = f32[56,128]{1,0:T(8,128)S(1)} collective-permute-done((f32[56,128]{1,0:T(8,128)S(1)}, f32[56,128]{1,0:T(8,128)S(1)}, u32[]{:S(2)}, u32[]{:S(2)}) %collective-permute-start.4) | collective-permute-done | bytes 28704 | tf_op jit(solution)/shard_map/ppermute | solution.py:484
  23.2 1.3 %middle.1 = (f32[3,5,8,128]{3,2,1,0:T(8,128)S(1)}, s32[8,128]{1,0:T(8,128)S(1)}, f32[3,24,128]{2,1,0:T(8,128)S(1)}) custom-call(f32[56,128]{1,0:T(8,128)S(1)} %get-tuple-element.17.refs_0_.mine, f32[56,128]{1,0:T(8,128)S(1)} %collective-permute-done.1.refs_1_, f32[56,128]{1,0:T(8,128)S(1)} %collective-permute-done.2.refs_2_, ...), custom_call_target="tpu_custom_call" | custom-call | tf_op jit(solution)/shard_map/middle/pallas_call | solution.py:387
  24.5 0.4 %collective-permute-done.7.other = f32[8,128]{1,0:T(8,128)S(1)} collective-permute-done((f32[8,128]{1,0:T(8,128)S(1)}, f32[8,128]{1,0:T(8,128)S(1)}, u32[]{:S(2)}, u32[]{:S(2)}) %collective-permute-start.7) | collective-permute-done | bytes 4128 | tf_op jit(solution)/shard_map/ppermute | solution.py:498
  24.9 0.0 collective-permute-done.6.mid
  24.9 0.0 collective-permute-done.5.chip
  24.9 1.1 %last.1 = (f32[3,512]{1,0:T(4,128)}, f32[8,128]{1,0:T(8,128)}) custom-call(f32[56,128]{1,0:T(8,128)S(1)} %get-tuple-element.17.refs_0_.mine, f32[3,5,8,128]{3,2,1,0:T(8,128)S(1)} %get-tuple-element.24.stage, s32[8,128]{1,0:T(8,128)S(1)} %get-tuple-element.25.back, f32[8,128]{1,0:T(8,128)S(1)} %get-tuple-element.26.here, ...), custom_call_target="tpu_custom_call" | custom-call | tf_op jit(solution)/shard_map/last/pallas_call | solution.py:387
  (1 shorter events, 0.0 us)
Async XLA Ops:
  2.1 9.4 %copy-start.1 = (s32[2,1024]{1,0:T(2,128)S(1)}, s32[2,1024]{1,0:T(2,128)}, u32[]{:S(2)}) copy-start(s32[2,1024]{1,0:T(2,128)} %pair.1) | copy-start | bytes 24580
  2.1 14.1 %all-to-all-start = ((f32[8,40,128]{2,1,0:T(8,128)}), f32[8,40,128]{2,1,0:T(8,128)S(1)}, u32[]{:S(2)}, u32[]{:S(2)}) async-start(f32[8,40,128]{2,1,0:T(8,128)} %pack.1), calls=%async_computation | async-start | bytes 327680 | tf_op jit(solution)/shard_map/all_to_all | solution.py:457
  11.5 1.0 %copy-start = (f32[8,128,128]{2,1,0:T(8,128)S(1)}, f32[8,128,128]{2,1,0:T(8,128)}, u32[]{:S(2)}) copy-start(f32[8,128,128]{2,1,0:T(8,128)} %tiles.1) | copy-start | bytes 1572868
  12.7 4.4 %collective-permute-start = (f32[24,128]{1,0:T(8,128)S(1)}, f32[24,128]{1,0:T(8,128)S(1)}, u32[]{:S(2)}, u32[]{:S(2)}) collective-permute-start(f32[24,128]{1,0:T(8,128)S(1)} %get-tuple-element.16.fixed), channel_id=1, source_target_pairs={{0,2},{1,3},{2,6},{3,7},{4,0},{5,1},{6,10},{7,11},{8,4},{9,5},{10,... | collective-permute-start | bytes 36872 | tf_op jit(solution)/shard_map/ppermute | solution.py:463
  17.1 3.6 %collective-permute-start.2 = (f32[56,128]{1,0:T(8,128)S(1)}, f32[56,128]{1,0:T(8,128)S(1)}, u32[]{:S(2)}, u32[]{:S(2)}) collective-permute-start(f32[56,128]{1,0:T(8,128)S(1)} %get-tuple-element.18), channel_id=1, source_target_pairs={{0,3},{1,2},{2,1},{3,0},{4,7},{5,6},{6,5},{7,4},{8,11},{9,10},{10,... | collective-permute-start | bytes 86024 | tf_op jit(solution)/shard_map/ppermute | solution.py:481
  17.8 2.9 %collective-permute-start.1 = (f32[56,128]{1,0:T(8,128)S(1)}, f32[56,128]{1,0:T(8,128)S(1)}, u32[]{:S(2)}, u32[]{:S(2)}) collective-permute-start(f32[56,128]{1,0:T(8,128)S(1)} %get-tuple-element.17.refs_0_.mine), channel_id=1, source_target_pairs={{0,1},{1,0},{2,3},{3,2},{4,5},{5,4},{6,7},{7,6},{8,9},{9,8},{10,11... | collective-permute-start | bytes 86024 | tf_op jit(solution)/shard_map/ppermute | solution.py:482
  18.7 3.9 %collective-permute-start.3 = (f32[56,128]{1,0:T(8,128)S(1)}, f32[56,128]{1,0:T(8,128)S(1)}, u32[]{:S(2)}, u32[]{:S(2)}) collective-permute-start(f32[56,128]{1,0:T(8,128)S(1)} %get-tuple-element.19), channel_id=1, source_target_pairs={{0,2},{1,3},{2,0},{3,1},{4,6},{5,7},{6,4},{7,5},{8,10},{9,11},{10,... | collective-permute-start | bytes 86024 | tf_op jit(solution)/shard_map/ppermute | solution.py:484
  19.4 3.9 %collective-permute-start.4 = (f32[56,128]{1,0:T(8,128)S(1)}, f32[56,128]{1,0:T(8,128)S(1)}, u32[]{:S(2)}, u32[]{:S(2)}) collective-permute-start(f32[56,128]{1,0:T(8,128)S(1)} %get-tuple-element.20), channel_id=1, source_target_pairs={{0,2},{1,3},{2,0},{3,1},{4,6},{5,7},{6,4},{7,5},{8,10},{9,11},{10,... | collective-permute-start | bytes 86024 | tf_op jit(solution)/shard_map/ppermute | solution.py:484
  21.2 3.7 %collective-permute-start.7 = (f32[8,128]{1,0:T(8,128)S(1)}, f32[8,128]{1,0:T(8,128)S(1)}, u32[]{:S(2)}, u32[]{:S(2)}) collective-permute-start(f32[8,128]{1,0:T(8,128)S(1)} %get-tuple-element.26.here), channel_id=1, source_target_pairs={{0,4},{1,2},{2,1},{3,11},{4,0},{5,6},{6,5},{7,8},{8,7},{9,10},{10,... | collective-permute-start | bytes 12296 | tf_op jit(solution)/shard_map/ppermute | solution.py:498
  21.8 3.0 %collective-permute-start.6 = (f32[8,128]{1,0:T(8,128)S(1)}, f32[8,128]{1,0:T(8,128)S(1)}, u32[]{:S(2)}, u32[]{:S(2)}) collective-permute-start(f32[8,128]{1,0:T(8,128)S(1)} %get-tuple-element.26.here), channel_id=1, source_target_pairs={{0,1},{1,0},{2,6},{3,4},{4,3},{5,7},{6,2},{7,5},{8,9},{9,8},{10,14... | collective-permute-start | bytes 12296 | tf_op jit(solution)/shard_map/ppermute | solution.py:500
  22.6 2.2 %collective-permute-start.5 = (f32[8,128]{1,0:T(8,128)S(1)}, f32[8,128]{1,0:T(8,128)S(1)}, u32[]{:S(2)}, u32[]{:S(2)}) collective-permute-start(f32[8,128]{1,0:T(8,128)S(1)} %get-tuple-element.26.here), channel_id=1, source_target_pairs={{0,1},{1,0},{2,3},{3,2},{4,5},{5,4},{6,7},{7,6},{8,9},{9,8},{10,11... | collective-permute-start | bytes 12296 | tf_op jit(solution)/shard_map/ppermute | solution.py:499

commit v4 on v3

--- a/solution.py
+++ b/solution.py
@@ -147,7 +147,7 @@
     step, exists = second_part(stride)
 
     def came_from(part):
-        return raw.at[GROUP - 1 - part]
+        return raw.at[(part + 2) % GROUP]
 
     def list_rows(part, level):
         rows = came_from(part)
@@ -302,8 +302,8 @@
 
 
 def middle_kernel(stride, parts, count, *refs):
-    came, known = refs[:count], refs[count]
-    stage, back_here, fixed_out, gathered, rims, rows, state_next, rims_next = refs[count + 1 :]
+    came, known, here = refs[:count], refs[count], refs[count + 1]
+    stage, impulse, base, gathered, rims, rows, state_next, rims_next = refs[count + 2 :]
     gather_records(stride, parts, came, gathered)
     records = {o: gathered.at[o + REACH] for o in range(-REACH, REACH + 1)}
     rim = {o: rims.at[o + REACH] for o in records}
@@ -327,7 +327,7 @@
         incoming = sums[o - 1][right] + sums[o + 1][left]
         back = inverse([records[o][pl.ds(RIM_AT, 1), :]])
         if o == 0:
-            back_here[...] = back
+            base[pl.ds(CHUNKS * FIELDS, FIELDS), :] = back.astype(jnp.float32)
         blocks = [
             moved(was, sums[o][c], incoming, back[c : c + 1])
             for c, was in enumerate(state_of(records[o]))
@@ -343,41 +343,38 @@
         speed = sum(
             normal[k] * difference(state, ghosts[o], 3 + k, first, second) for k in range(3)
         )
-        for k in range(3):
-            stage[o + 1, k] = normal[k]
-        stage[o + 1, 3] = lam
-        stage[o + 1, 4] = speed
-        fixed_out[o + 1] = records[o][pl.ds(FIRST_AT, FIXED), :]
-
-
-def last_kernel(
-    parts, mine, stage, back, here, chip, mid, other, fixed, velocity, impulse, rows
-):
+        diag = diag_of(records[o])
+        if o == 0:
+            lam = jnp.maximum(0.0, lam - (here[...] + speed) / diag)
+            impulse[...] = lam
+            force = [one * lam for one in normal]
+            total = add_up(force, first, second, local, rows.at[2 * REACH + 1])
+            for c in local:
+                base[pl.ds(FIELDS * c, FIELDS), :] = total[c]
+            continue
+        side = stage.at[(o + 1) // 2]
+        for k, one in enumerate((*normal, lam, speed, diag)):
+            side[k] = one
+        side[6] = records[o][pl.ds(SECOND_AT, FIELDS), :]
+
+
+def last_kernel(parts, mine, stage, base, chip, mid, other, velocity, rows):
     me = lax.axis_index("parts")
     odd = me % 2 == 1
     apart = (me % (2 * BLOCK) == BLOCK) | (me % (2 * BLOCK) == BLOCK - 1)
     across = jnp.where(apart, mid[...], other[...])
     across = jnp.where((me > 0) & (me < parts - 1), across, 0.0)
-    coupled = {
-        -1: jnp.where(odd, chip[...], across),
-        0: here[...],
-        1: jnp.where(odd, across, chip[...]),
-    }
-    sums = {}
-    for o, heads in ((-1, [CHUNKS + 1]), (0, list(range(CHUNKS))), (1, [CHUNKS])):
-        record = fixed.at[o + 1]
-        lam = stage[o + 1, 3]
-        diag = record[pl.ds(DIAG_AT - FIRST_AT, FIELDS), :]
-        lam = jnp.maximum(0.0, lam - (coupled[o] + stage[o + 1, 4]) / diag)
-        if o == 0:
-            impulse[...] = lam
-        first = record[pl.ds(0, FIELDS), :].astype(jnp.int32)
-        second = record[pl.ds(SECOND_AT - FIRST_AT, FIELDS), :].astype(jnp.int32)
-        force = [stage[o + 1, k] * lam for k in range(3)]
-        sums[o] = add_up(force, first, second, heads, rows.at[o + 1])
-    incoming = sums[-1][CHUNKS + 1] + sums[1][CHUNKS]
+    products = (jnp.where(odd, chip[...], across), jnp.where(odd, across, chip[...]))
+    incoming = 0.0
+    for k, head in ((0, CHUNKS + 1), (1, CHUNKS)):
+        lam = jnp.maximum(0.0, stage[k, 3] - (products[k] + stage[k, 4]) / stage[k, 5])
+        second = stage[k, 6].astype(jnp.int32)
+        force = [stage[k, d] * lam for d in range(3)]
+        incoming += add_up(force, None, second, [head], rows.at[k])[head]
+    back = base[pl.ds(CHUNKS * FIELDS, FIELDS), :].astype(jnp.int32)
     for c, was in enumerate(state_of(mine)):
-        block = moved(was, sums[0][c], incoming, back[pl.ds(c, 1), :])
+        here = base[pl.ds(FIELDS * c, FIELDS), :]
+        block = moved(was, here, incoming, back[c : c + 1])
         velocity[:, pl.ds(c * TILE, TILE)] = block[3:6]
 
 
@@ -453,7 +450,7 @@
         [pltpu.VMEM(one.shape, one.dtype) for one in inputs]
         + [pltpu.SemaphoreType.DMA((5,))],
     )
-    classes = [[r + stride * (GROUP - 1 - k) for k in range(GROUP)] for r in range(stride)]
+    classes = [[r + stride * ((k - 2) % GROUP) for k in range(GROUP)] for r in range(stride)]
     raw = lax.all_to_all(packed, "parts", 0, 0, axis_index_groups=classes)
 
     half = jax.ShapeDtypeStruct(delassus.shape, jnp.bfloat16)
@@ -498,29 +495,29 @@
     other = send(here, perm=most)
     chip = send(here, perm=within)
     mid = send(here, perm=edge)
-    stage, back, contact_rows = call(
+    stage, impulse, base = call(
         functools.partial(middle_kernel, stride, parts, len(came)),
         (
-            float32((3, 5, FIELDS, TILE)),
-            jax.ShapeDtypeStruct((FIELDS, TILE), jnp.int32),
-            float32((3, FIXED, TILE)),
+            float32((2, 7, FIELDS, TILE)),
+            float32((tiles, TILE)),
+            float32(((CHUNKS + 1) * FIELDS, TILE)),
         ),
-        (*came, known),
+        (*came, known, here),
         "middle",
         scratch=[
             vmem(reach, *record),
             vmem(reach, FIELDS, TILE),
-            vmem(reach, FIELDS * FIELDS, TILE),
+            vmem(reach + 1, FIELDS * FIELDS, TILE),
             vmem(3, CHUNKS * FIELDS, TILE),
             vmem(3, FIELDS, TILE),
         ],
     )
-    new_velocity, impulse = call(
+    new_velocity = call(
         functools.partial(last_kernel, parts),
-        (float32((3, grains)), float32((tiles, TILE))),
-        (mine, stage, back, here, chip, mid, other, contact_rows),
+        float32((3, grains)),
+        (mine, stage, base, chip, mid, other),
         "last",
-        scratch=[vmem(3, FIELDS * FIELDS, TILE)],
+        scratch=[vmem(2, FIELDS * FIELDS, TILE)],
     )
     return (new_velocity, impulse.reshape(contacts))
 

time: 26.3 us -> 25.6 us (0.973)
  waiting for transfers between devices: 2.94 us -> 2.04 us
  Pallas kernels: 5.35 us -> 6.03 us
  starting transfers between devices: 15.9 us -> 15.5 us
    all_to_all x1, starting transfers between devices: 9.34 us -> 8.35 us  [body(): raw = lax.all_to_all(packed, 'parts', 0, 0, axis_index_groups=classes)]
    ppermute x1, starting transfers between devices: 0.64 us -> 1.5 us  [body(): other = send(here, perm=most)]
    ppermute x1, starting transfers between devices: 0.8 us -> 0.01 us  [body(): mid = send(here, perm=edge)]
    pallas_call x7, Pallas kernels: 5.35 us -> 6.03 us  [call(): pl.pallas_call(kernel, out_shape=out_shape, in_specs=[pl.BlockSpec(memory...]
    ppermute x2, waiting for transfers between devices: 0.6 us -> 0.01 us  [body(): came = (*near, send(low, perm=beyond), send(high, perm=beyond))]
    ppermute x1, starting transfers between devices: 0.01 us -> 0.51 us  [body(): chip = send(here, perm=within)]
    ppermute x1, waiting for transfers between devices: 0.35 us -> 0.01 us  [body(): other = send(here, perm=most)]
  transfers between devices with their start and end apart: 9 -> 9, of which waited for: 3 -> 1; matrix products, arithmetic and copies ran while one was open for 0% -> 0% of each run, Pallas kernels for 11% -> 14%
where the time goes in v4:
time: 25.6 us; the launch traced here: 25.3 us
  starting transfers between devices  15.5 us (61%)
  Pallas kernels  6.03 us (24%)
  waiting for transfers between devices  2.04 us (8%)
  local copies, waits for them, and re-layouts  1.05 us (4%)
  between operations  0.69 us (3%)
    all_to_all x1, starting transfers between devices, body(): raw = lax.all_to_all(packed, 'parts', 0, 0, axis_index_groups=classes)  8.35 us
    pallas_call x7, Pallas kernels, call(): pl.pallas_call(kernel, out_shape=out_shape, in_specs=[pl.BlockSpec(memory...  6.03 us
    ppermute x2, starting transfers between devices, body(): came = (*near, send(low, perm=beyond), send(high, perm=beyond))  2.03 us
    all_to_all x1, waiting for transfers between devices, body(): raw = lax.all_to_all(packed, 'parts', 0, 0, axis_index_groups=classes)  2 us
    ppermute x1, starting transfers between devices, body(): given = send(fixed, perm=second_parts(parts, stride))  1.54 us
    ppermute x1, starting transfers between devices, body(): other = send(here, perm=most)  1.5 us
    unnamed x4, local copies, waits for them, and re-layouts  1.05 us
    ppermute x1, starting transfers between devices, body(): near = (mine, send(mine, perm=within), from_far)  0.89 us
  transfers between devices with their start and end apart: 9, of which 1 were waited for; matrix products, arithmetic and copies ran while one was open for 0% of the time, Pallas kernels for 14%

profile of v4, /device:TPU:0, one launch (start us, length us, event | category | flops | bytes accessed | tf_op | source)
XLA Modules:
  0.0 25.3 jit_solution(17486451314421171982)
XLA Ops:
  0.6 1.5 %pack.1 = f32[8,40,128]{2,1,0:T(8,128)} custom-call(f32[3,512]{1,0:T(4,128)} %refs_0_.1, f32[3,512]{1,0:T(4,128)} %refs_1_.1, f32[4,128]{1,0:T(4,128)} %bitcast.3, s32[3,256]{1,0:T(4,128)} %refs_3_.1, s32[1,128]{1,0:T(1,128)} %bitcast.4), custom_call_target="tpu_custom_call" | custom-call | tf_op jit(solution)/shard_map/pack/pallas_call | solution.py:384
  2.1 0.0 copy-start.1
  2.1 8.3 %all-to-all-start = ((f32[8,40,128]{2,1,0:T(8,128)}), f32[8,40,128]{2,1,0:T(8,128)S(1)}, u32[]{:S(2)}, u32[]{:S(2)}) async-start(f32[8,40,128]{2,1,0:T(8,128)} %pack.1), calls=%async_computation | async-start | bytes 327680 | tf_op jit(solution)/shard_map/all_to_all | solution.py:454
  10.5 0.0 copy-done.1
  10.5 0.0 copy-start
  10.5 1.0 %copy-done = f32[8,128,128]{2,1,0:T(8,128)S(1)} copy-done((f32[8,128,128]{2,1,0:T(8,128)S(1)}, f32[8,128,128]{2,1,0:T(8,128)}, u32[]{:S(2)}) %copy-start) | copy-done | bytes 524312
  11.5 0.2 fixed.1
  11.7 1.5 %collective-permute-start = (f32[24,128]{1,0:T(8,128)S(1)}, f32[24,128]{1,0:T(8,128)S(1)}, u32[]{:S(2)}, u32[]{:S(2)}) collective-permute-start(f32[24,128]{1,0:T(8,128)S(1)} %get-tuple-element.14.fixed), channel_id=1, source_target_pairs={{0,2},{1,3},{2,6},{3,7},{4,0},{5,1},{6,10},{7,11},{8,4},{9,5},{10,... | collective-permute-start | bytes 36872 | tf_op jit(solution)/shard_map/ppermute | solution.py:460
  13.3 2.0 %all-to-all-done.raw = f32[8,40,128]{2,1,0:T(8,128)S(1)} async-done(((f32[8,40,128]{2,1,0:T(8,128)}), f32[8,40,128]{2,1,0:T(8,128)S(1)}, u32[]{:S(2)}, u32[]{:S(2)}) %all-to-all-start) | async-done | bytes 163872 | tf_op jit(solution)/shard_map/all_to_all | solution.py:454
  15.3 0.9 %compose.1.states = f32[2,32,128]{2,1,0:T(8,128)S(1)} custom-call(f32[8,40,128]{2,1,0:T(8,128)S(1)} %all-to-all-done.raw), custom_call_target="tpu_custom_call" | custom-call | tf_op jit(solution)/shard_map/compose/pallas_call | solution.py:384
  16.1 0.0 collective-permute-done.given
  16.2 0.7 %collective-permute-start.2 = (f32[56,128]{1,0:T(8,128)S(1)}, f32[56,128]{1,0:T(8,128)S(1)}, u32[]{:S(2)}, u32[]{:S(2)}) collective-permute-start(f32[56,128]{1,0:T(8,128)S(1)} %get-tuple-element.16), channel_id=1, source_target_pairs={{0,3},{1,2},{2,1},{3,0},{4,7},{5,6},{6,5},{7,4},{8,11},{9,10},{10,... | collective-permute-start | bytes 86024 | tf_op jit(solution)/shard_map/ppermute | solution.py:478
  16.9 0.9 %collective-permute-start.1 = (f32[56,128]{1,0:T(8,128)S(1)}, f32[56,128]{1,0:T(8,128)S(1)}, u32[]{:S(2)}, u32[]{:S(2)}) collective-permute-start(f32[56,128]{1,0:T(8,128)S(1)} %get-tuple-element.15.refs_0_.mine), channel_id=1, source_target_pairs={{0,1},{1,0},{2,3},{3,2},{4,5},{5,4},{6,7},{7,6},{8,9},{9,8},{10,11... | collective-permute-start | bytes 86024 | tf_op jit(solution)/shard_map/ppermute | solution.py:479
  17.8 0.6 %collective-permute-start.3 = (f32[56,128]{1,0:T(8,128)S(1)}, f32[56,128]{1,0:T(8,128)S(1)}, u32[]{:S(2)}, u32[]{:S(2)}) collective-permute-start(f32[56,128]{1,0:T(8,128)S(1)} %get-tuple-element.17), channel_id=1, source_target_pairs={{0,2},{1,3},{2,0},{3,1},{4,6},{5,7},{6,4},{7,5},{8,10},{9,11},{10,... | collective-permute-start | bytes 86024 | tf_op jit(solution)/shard_map/ppermute | solution.py:481
  18.4 1.4 %collective-permute-start.4 = (f32[56,128]{1,0:T(8,128)S(1)}, f32[56,128]{1,0:T(8,128)S(1)}, u32[]{:S(2)}, u32[]{:S(2)}) collective-permute-start(f32[56,128]{1,0:T(8,128)S(1)} %get-tuple-element.18), channel_id=1, source_target_pairs={{0,2},{1,3},{2,0},{3,1},{4,6},{5,7},{6,4},{7,5},{8,10},{9,11},{10,... | collective-permute-start | bytes 86024 | tf_op jit(solution)/shard_map/ppermute | solution.py:481
  19.8 0.0 collective-permute-done.2.refs_2_
  19.8 0.0 collective-permute-done.1.refs_1_
  19.8 0.4 %near.1 = (f32[8,128]{1,0:T(8,128)S(1)}, f32[4,8,128]{2,1,0:T(8,128)S(1)}) custom-call(f32[56,128]{1,0:T(8,128)S(1)} %get-tuple-element.15.refs_0_.mine, f32[56,128]{1,0:T(8,128)S(1)} %collective-permute-done.1.refs_1_, f32[56,128]{1,0:T(8,128)S(1)} %collective-permute-done.2.refs_2_, bf16[8,128,128]{2,1,0:T(8,128)(2,1)S(1)} %get-tuple-element.19.refs_3_, ...), custom_call_target="tpu_custom_call" | custom-call | tf_op jit(solution)/shard_map/near/pallas_call | solution.py:384
  20.2 1.5 %collective-permute-start.7 = (f32[8,128]{1,0:T(8,128)S(1)}, f32[8,128]{1,0:T(8,128)S(1)}, u32[]{:S(2)}, u32[]{:S(2)}) collective-permute-start(f32[8,128]{1,0:T(8,128)S(1)} %get-tuple-element.22.refs_6_), channel_id=1, source_target_pairs={{0,4},{1,2},{2,1},{3,11},{4,0},{5,6},{6,5},{7,8},{8,7},{9,10},{10,... | collective-permute-start | bytes 12296 | tf_op jit(solution)/shard_map/ppermute | solution.py:495
  21.7 0.0 collective-permute-start.6
  21.7 0.5 %collective-permute-start.5 = (f32[8,128]{1,0:T(8,128)S(1)}, f32[8,128]{1,0:T(8,128)S(1)}, u32[]{:S(2)}, u32[]{:S(2)}) collective-permute-start(f32[8,128]{1,0:T(8,128)S(1)} %get-tuple-element.22.refs_6_), channel_id=1, source_target_pairs={{0,1},{1,0},{2,3},{3,2},{4,5},{5,4},{6,7},{7,6},{8,9},{9,8},{10,11... | collective-permute-start | bytes 12296 | tf_op jit(solution)/shard_map/ppermute | solution.py:496
  22.2 0.0 collective-permute-done.3.refs_3_
  22.2 0.0 collective-permute-done.4.refs_4_
  22.2 2.1 %middle.1 = (f32[2,7,8,128]{3,2,1,0:T(8,128)S(1)}, f32[8,128]{1,0:T(8,128)}, f32[40,128]{1,0:T(8,128)S(1)}) custom-call(f32[56,128]{1,0:T(8,128)S(1)} %get-tuple-element.15.refs_0_.mine, f32[56,128]{1,0:T(8,128)S(1)} %collective-permute-done.1.refs_1_, f32[56,128]{1,0:T(8,128)S(1)} %collective-permute-done.2.refs_2_, ...), custom_call_target="tpu_custom_call" | custom-call | tf_op jit(solution)/shard_map/middle/pallas_call | solution.py:384
  24.3 0.0 collective-permute-done.7.other
  24.4 0.0 collective-permute-done.6.mid
  24.4 0.0 collective-permute-done.5.chip
  24.4 0.9 %last.1 = f32[3,512]{1,0:T(4,128)} custom-call(f32[56,128]{1,0:T(8,128)S(1)} %get-tuple-element.15.refs_0_.mine, f32[2,7,8,128]{3,2,1,0:T(8,128)S(1)} %get-tuple-element.23.stage, f32[40,128]{1,0:T(8,128)S(1)} %get-tuple-element.24.base, f32[8,128]{1,0:T(8,128)S(1)} %collective-permute-done.5.chip, f32[8,128]{1,0:T(8,128)S(1)} %collective-permute-done.6.mid, ...), custom_call_target="tpu_custom_call" | custom-call | tf_op jit(solution)/shard_map/last/pallas_call | solution.py:384
  (1 shorter events, 0.0 us)
Async XLA Ops:
  2.1 8.4 %copy-start.1 = (s32[2,1024]{1,0:T(2,128)S(1)}, s32[2,1024]{1,0:T(2,128)}, u32[]{:S(2)}) copy-start(s32[2,1024]{1,0:T(2,128)} %pair.1) | copy-start | bytes 24580
  2.1 13.1 %all-to-all-start = ((f32[8,40,128]{2,1,0:T(8,128)}), f32[8,40,128]{2,1,0:T(8,128)S(1)}, u32[]{:S(2)}, u32[]{:S(2)}) async-start(f32[8,40,128]{2,1,0:T(8,128)} %pack.1), calls=%async_computation | async-start | bytes 327680 | tf_op jit(solution)/shard_map/all_to_all | solution.py:454
  10.5 1.0 %copy-start = (f32[8,128,128]{2,1,0:T(8,128)S(1)}, f32[8,128,128]{2,1,0:T(8,128)}, u32[]{:S(2)}) copy-start(f32[8,128,128]{2,1,0:T(8,128)} %tiles.1) | copy-start | bytes 1572868
  11.7 4.4 %collective-permute-start = (f32[24,128]{1,0:T(8,128)S(1)}, f32[24,128]{1,0:T(8,128)S(1)}, u32[]{:S(2)}, u32[]{:S(2)}) collective-permute-start(f32[24,128]{1,0:T(8,128)S(1)} %get-tuple-element.14.fixed), channel_id=1, source_target_pairs={{0,2},{1,3},{2,6},{3,7},{4,0},{5,1},{6,10},{7,11},{8,4},{9,5},{10,... | collective-permute-start | bytes 36872 | tf_op jit(solution)/shard_map/ppermute | solution.py:460
  16.2 3.6 %collective-permute-start.2 = (f32[56,128]{1,0:T(8,128)S(1)}, f32[56,128]{1,0:T(8,128)S(1)}, u32[]{:S(2)}, u32[]{:S(2)}) collective-permute-start(f32[56,128]{1,0:T(8,128)S(1)} %get-tuple-element.16), channel_id=1, source_target_pairs={{0,3},{1,2},{2,1},{3,0},{4,7},{5,6},{6,5},{7,4},{8,11},{9,10},{10,... | collective-permute-start | bytes 86024 | tf_op jit(solution)/shard_map/ppermute | solution.py:478
  16.9 2.9 %collective-permute-start.1 = (f32[56,128]{1,0:T(8,128)S(1)}, f32[56,128]{1,0:T(8,128)S(1)}, u32[]{:S(2)}, u32[]{:S(2)}) collective-permute-start(f32[56,128]{1,0:T(8,128)S(1)} %get-tuple-element.15.refs_0_.mine), channel_id=1, source_target_pairs={{0,1},{1,0},{2,3},{3,2},{4,5},{5,4},{6,7},{7,6},{8,9},{9,8},{10,11... | collective-permute-start | bytes 86024 | tf_op jit(solution)/shard_map/ppermute | solution.py:479
  17.8 4.5 %collective-permute-start.3 = (f32[56,128]{1,0:T(8,128)S(1)}, f32[56,128]{1,0:T(8,128)S(1)}, u32[]{:S(2)}, u32[]{:S(2)}) collective-permute-start(f32[56,128]{1,0:T(8,128)S(1)} %get-tuple-element.17), channel_id=1, source_target_pairs={{0,2},{1,3},{2,0},{3,1},{4,6},{5,7},{6,4},{7,5},{8,10},{9,11},{10,... | collective-permute-start | bytes 86024 | tf_op jit(solution)/shard_map/ppermute | solution.py:481
  18.4 3.9 %collective-permute-start.4 = (f32[56,128]{1,0:T(8,128)S(1)}, f32[56,128]{1,0:T(8,128)S(1)}, u32[]{:S(2)}, u32[]{:S(2)}) collective-permute-start(f32[56,128]{1,0:T(8,128)S(1)} %get-tuple-element.18), channel_id=1, source_target_pairs={{0,2},{1,3},{2,0},{3,1},{4,6},{5,7},{6,4},{7,5},{8,10},{9,11},{10,... | collective-permute-start | bytes 86024 | tf_op jit(solution)/shard_map/ppermute | solution.py:481
  20.2 4.1 %collective-permute-start.7 = (f32[8,128]{1,0:T(8,128)S(1)}, f32[8,128]{1,0:T(8,128)S(1)}, u32[]{:S(2)}, u32[]{:S(2)}) collective-permute-start(f32[8,128]{1,0:T(8,128)S(1)} %get-tuple-element.22.refs_6_), channel_id=1, source_target_pairs={{0,4},{1,2},{2,1},{3,11},{4,0},{5,6},{6,5},{7,8},{8,7},{9,10},{10,... | collective-permute-start | bytes 12296 | tf_op jit(solution)/shard_map/ppermute | solution.py:495
  21.7 2.6 %collective-permute-start.6 = (f32[8,128]{1,0:T(8,128)S(1)}, f32[8,128]{1,0:T(8,128)S(1)}, u32[]{:S(2)}, u32[]{:S(2)}) collective-permute-start(f32[8,128]{1,0:T(8,128)S(1)} %get-tuple-element.22.refs_6_), channel_id=1, source_target_pairs={{0,1},{1,0},{2,6},{3,4},{4,3},{5,7},{6,2},{7,5},{8,9},{9,8},{10,14... | collective-permute-start | bytes 12296 | tf_op jit(solution)/shard_map/ppermute | solution.py:497
  21.7 2.6 %collective-permute-start.5 = (f32[8,128]{1,0:T(8,128)S(1)}, f32[8,128]{1,0:T(8,128)S(1)}, u32[]{:S(2)}, u32[]{:S(2)}) collective-permute-start(f32[8,128]{1,0:T(8,128)S(1)} %get-tuple-element.22.refs_6_), channel_id=1, source_target_pairs={{0,1},{1,0},{2,3},{3,2},{4,5},{5,4},{6,7},{7,6},{8,9},{9,8},{10,11... | collective-permute-start | bytes 12296 | tf_op jit(solution)/shard_map/ppermute | solution.py:496

commit v5 on v3

--- a/solution.py
+++ b/solution.py
@@ -147,7 +147,7 @@
     step, exists = second_part(stride)
 
     def came_from(part):
-        return raw.at[GROUP - 1 - part]
+        return raw.at[(part + 2) % GROUP]
 
     def list_rows(part, level):
         rows = came_from(part)
@@ -264,11 +264,12 @@
     total = 0.0
     for k in range(0, len(left), 2):
         total += lax.dot_general(
+            jnp.concatenate(right[k : k + 2], axis=1),
             jnp.concatenate(left[k : k + 2], axis=1).astype(jnp.bfloat16),
-            jnp.concatenate(right[k : k + 2], axis=1),
             NT,
             preferred_element_type=jnp.float32,
         )
+    total = total.T
     blocks = [total[FIELDS * k : FIELDS * (k + 1)] for k in range(len(heads))]
     return {h: block + pltpu.roll(block, 3, 0) for h, block in zip(heads, blocks)}
 
@@ -453,7 +454,7 @@
         [pltpu.VMEM(one.shape, one.dtype) for one in inputs]
         + [pltpu.SemaphoreType.DMA((5,))],
     )
-    classes = [[r + stride * (GROUP - 1 - k) for k in range(GROUP)] for r in range(stride)]
+    classes = [[r + stride * ((k - 2) % GROUP) for k in range(GROUP)] for r in range(stride)]
     raw = lax.all_to_all(packed, "parts", 0, 0, axis_index_groups=classes)
 
     half = jax.ShapeDtypeStruct(delassus.shape, jnp.bfloat16)

time: 26.3 us -> 25.4 us (0.966)
  waiting for transfers between devices: 2.94 us -> 2.37 us
  starting transfers between devices: 15.9 us -> 15.5 us
    all_to_all x1, starting transfers between devices: 9.34 us -> 8.35 us  [body(): raw = lax.all_to_all(packed, 'parts', 0, 0, axis_index_groups=classes)]
    ppermute x1, starting transfers between devices: 0.64 us -> 1.5 us  [body(): other = send(here, perm=most)]
    ppermute x1, starting transfers between devices: 0.8 us -> 0.01 us  [body(): mid = send(here, perm=edge)]
    ppermute x2, waiting for transfers between devices: 0.6 us -> 0.01 us  [body(): came = (*near, send(low, perm=beyond), send(high, perm=beyond))]
    ppermute x1, starting transfers between devices: 0.01 us -> 0.51 us  [body(): chip = send(here, perm=within)]
  transfers between devices with their start and end apart: 9 -> 9, of which waited for: 3 -> 2; matrix products, arithmetic and copies ran while one was open for 0% -> 0% of each run, Pallas kernels for 11% -> 11%
where the time goes in v5:
time: 25.4 us; the launch traced here: 25.1 us
  starting transfers between devices  15.5 us (61%)
  Pallas kernels  5.5 us (22%)
  waiting for transfers between devices  2.37 us (9%)
  local copies, waits for them, and re-layouts  1.05 us (4%)
  between operations  0.69 us (3%)
    all_to_all x1, starting transfers between devices, body(): raw = lax.all_to_all(packed, 'parts', 0, 0, axis_index_groups=classes)  8.35 us
    pallas_call x7, Pallas kernels, call(): pl.pallas_call(kernel, out_shape=out_shape, in_specs=[pl.BlockSpec(memory...  5.5 us
    ppermute x2, starting transfers between devices, body(): came = (*near, send(low, perm=beyond), send(high, perm=beyond))  2.03 us
    all_to_all x1, waiting for transfers between devices, body(): raw = lax.all_to_all(packed, 'parts', 0, 0, axis_index_groups=classes)  2 us
    ppermute x1, starting transfers between devices, body(): given = send(fixed, perm=second_parts(parts, stride))  1.54 us
    ppermute x1, starting transfers between devices, body(): other = send(here, perm=most)  1.5 us
    unnamed x4, local copies, waits for them, and re-layouts  1.05 us
    ppermute x1, starting transfers between devices, body(): near = (mine, send(mine, perm=within), from_far)  0.89 us
  transfers between devices with their start and end apart: 9, of which 2 were waited for; matrix products, arithmetic and copies ran while one was open for 0% of the time, Pallas kernels for 11%

profile of v5, /device:TPU:0, one launch (start us, length us, event | category | flops | bytes accessed | tf_op | source)
XLA Modules:
  0.0 25.1 jit_solution(15835880413335871763)
XLA Ops:
  0.6 1.5 %pack.1 = f32[8,40,128]{2,1,0:T(8,128)} custom-call(f32[3,512]{1,0:T(4,128)} %refs_0_.1, f32[3,512]{1,0:T(4,128)} %refs_1_.1, f32[4,128]{1,0:T(4,128)} %bitcast.3, s32[3,256]{1,0:T(4,128)} %refs_3_.1, s32[1,128]{1,0:T(1,128)} %bitcast.4), custom_call_target="tpu_custom_call" | custom-call | tf_op jit(solution)/shard_map/pack/pallas_call | solution.py:388
  2.1 0.0 copy-start.1
  2.1 8.3 %all-to-all-start = ((f32[8,40,128]{2,1,0:T(8,128)}), f32[8,40,128]{2,1,0:T(8,128)S(1)}, u32[]{:S(2)}, u32[]{:S(2)}) async-start(f32[8,40,128]{2,1,0:T(8,128)} %pack.1), calls=%async_computation | async-start | bytes 327680 | tf_op jit(solution)/shard_map/all_to_all | solution.py:458
  10.5 0.0 copy-done.1
  10.5 0.0 copy-start
  10.5 1.0 %copy-done = f32[8,128,128]{2,1,0:T(8,128)S(1)} copy-done((f32[8,128,128]{2,1,0:T(8,128)S(1)}, f32[8,128,128]{2,1,0:T(8,128)}, u32[]{:S(2)}) %copy-start) | copy-done | bytes 524312
  11.5 0.2 fixed.1
  11.7 1.5 %collective-permute-start = (f32[24,128]{1,0:T(8,128)S(1)}, f32[24,128]{1,0:T(8,128)S(1)}, u32[]{:S(2)}, u32[]{:S(2)}) collective-permute-start(f32[24,128]{1,0:T(8,128)S(1)} %get-tuple-element.16.fixed), channel_id=1, source_target_pairs={{0,2},{1,3},{2,6},{3,7},{4,0},{5,1},{6,10},{7,11},{8,4},{9,5},{10,... | collective-permute-start | bytes 36872 | tf_op jit(solution)/shard_map/ppermute | solution.py:464
  13.3 2.0 %all-to-all-done.raw = f32[8,40,128]{2,1,0:T(8,128)S(1)} async-done(((f32[8,40,128]{2,1,0:T(8,128)}), f32[8,40,128]{2,1,0:T(8,128)S(1)}, u32[]{:S(2)}, u32[]{:S(2)}) %all-to-all-start) | async-done | bytes 163872 | tf_op jit(solution)/shard_map/all_to_all | solution.py:458
  15.3 0.9 %compose.1.states = f32[2,32,128]{2,1,0:T(8,128)S(1)} custom-call(f32[8,40,128]{2,1,0:T(8,128)S(1)} %all-to-all-done.raw), custom_call_target="tpu_custom_call" | custom-call | tf_op jit(solution)/shard_map/compose/pallas_call | solution.py:388
  16.1 0.0 collective-permute-done.given
  16.2 0.7 %collective-permute-start.2 = (f32[56,128]{1,0:T(8,128)S(1)}, f32[56,128]{1,0:T(8,128)S(1)}, u32[]{:S(2)}, u32[]{:S(2)}) collective-permute-start(f32[56,128]{1,0:T(8,128)S(1)} %get-tuple-element.18), channel_id=1, source_target_pairs={{0,3},{1,2},{2,1},{3,0},{4,7},{5,6},{6,5},{7,4},{8,11},{9,10},{10,... | collective-permute-start | bytes 86024 | tf_op jit(solution)/shard_map/ppermute | solution.py:482
  16.9 0.9 %collective-permute-start.1 = (f32[56,128]{1,0:T(8,128)S(1)}, f32[56,128]{1,0:T(8,128)S(1)}, u32[]{:S(2)}, u32[]{:S(2)}) collective-permute-start(f32[56,128]{1,0:T(8,128)S(1)} %get-tuple-element.17.refs_0_.mine), channel_id=1, source_target_pairs={{0,1},{1,0},{2,3},{3,2},{4,5},{5,4},{6,7},{7,6},{8,9},{9,8},{10,11... | collective-permute-start | bytes 86024 | tf_op jit(solution)/shard_map/ppermute | solution.py:483
  17.8 0.6 %collective-permute-start.3 = (f32[56,128]{1,0:T(8,128)S(1)}, f32[56,128]{1,0:T(8,128)S(1)}, u32[]{:S(2)}, u32[]{:S(2)}) collective-permute-start(f32[56,128]{1,0:T(8,128)S(1)} %get-tuple-element.19), channel_id=1, source_target_pairs={{0,2},{1,3},{2,0},{3,1},{4,6},{5,7},{6,4},{7,5},{8,10},{9,11},{10,... | collective-permute-start | bytes 86024 | tf_op jit(solution)/shard_map/ppermute | solution.py:485
  18.4 1.4 %collective-permute-start.4 = (f32[56,128]{1,0:T(8,128)S(1)}, f32[56,128]{1,0:T(8,128)S(1)}, u32[]{:S(2)}, u32[]{:S(2)}) collective-permute-start(f32[56,128]{1,0:T(8,128)S(1)} %get-tuple-element.20), channel_id=1, source_target_pairs={{0,2},{1,3},{2,0},{3,1},{4,6},{5,7},{6,4},{7,5},{8,10},{9,11},{10,... | collective-permute-start | bytes 86024 | tf_op jit(solution)/shard_map/ppermute | solution.py:485
  19.8 0.0 collective-permute-done.2.refs_2_
  19.8 0.0 collective-permute-done.1.refs_1_
  19.8 0.4 %near.1 = (f32[8,128]{1,0:T(8,128)S(1)}, f32[4,8,128]{2,1,0:T(8,128)S(1)}) custom-call(f32[56,128]{1,0:T(8,128)S(1)} %get-tuple-element.17.refs_0_.mine, f32[56,128]{1,0:T(8,128)S(1)} %collective-permute-done.1.refs_1_, f32[56,128]{1,0:T(8,128)S(1)} %collective-permute-done.2.refs_2_, bf16[8,128,128]{2,1,0:T(8,128)(2,1)S(1)} %get-tuple-element.21.refs_3_, ...), custom_call_target="tpu_custom_call" | custom-call | tf_op jit(solution)/shard_map/near/pallas_call | solution.py:388
  20.2 1.5 %collective-permute-start.7 = (f32[8,128]{1,0:T(8,128)S(1)}, f32[8,128]{1,0:T(8,128)S(1)}, u32[]{:S(2)}, u32[]{:S(2)}) collective-permute-start(f32[8,128]{1,0:T(8,128)S(1)} %get-tuple-element.26.here), channel_id=1, source_target_pairs={{0,4},{1,2},{2,1},{3,11},{4,0},{5,6},{6,5},{7,8},{8,7},{9,10},{10,... | collective-permute-start | bytes 12296 | tf_op jit(solution)/shard_map/ppermute | solution.py:499
  21.7 0.0 collective-permute-start.6
  21.7 0.5 %collective-permute-start.5 = (f32[8,128]{1,0:T(8,128)S(1)}, f32[8,128]{1,0:T(8,128)S(1)}, u32[]{:S(2)}, u32[]{:S(2)}) collective-permute-start(f32[8,128]{1,0:T(8,128)S(1)} %get-tuple-element.26.here), channel_id=1, source_target_pairs={{0,1},{1,0},{2,3},{3,2},{4,5},{5,4},{6,7},{7,6},{8,9},{9,8},{10,11... | collective-permute-start | bytes 12296 | tf_op jit(solution)/shard_map/ppermute | solution.py:500
  22.2 0.0 collective-permute-done.3.refs_3_
  22.2 0.0 collective-permute-done.4.refs_4_
  22.3 1.3 %middle.1 = (f32[3,5,8,128]{3,2,1,0:T(8,128)S(1)}, s32[8,128]{1,0:T(8,128)S(1)}, f32[3,24,128]{2,1,0:T(8,128)S(1)}) custom-call(f32[56,128]{1,0:T(8,128)S(1)} %get-tuple-element.17.refs_0_.mine, f32[56,128]{1,0:T(8,128)S(1)} %collective-permute-done.1.refs_1_, f32[56,128]{1,0:T(8,128)S(1)} %collective-permute-done.2.refs_2_, ...), custom_call_target="tpu_custom_call" | custom-call | tf_op jit(solution)/shard_map/middle/pallas_call | solution.py:388
  23.6 0.3 %collective-permute-done.7.other = f32[8,128]{1,0:T(8,128)S(1)} collective-permute-done((f32[8,128]{1,0:T(8,128)S(1)}, f32[8,128]{1,0:T(8,128)S(1)}, u32[]{:S(2)}, u32[]{:S(2)}) %collective-permute-start.7) | collective-permute-done | bytes 4128 | tf_op jit(solution)/shard_map/ppermute | solution.py:499
  23.9 0.0 collective-permute-done.6.mid
  23.9 0.0 collective-permute-done.5.chip
  23.9 1.2 %last.1 = (f32[3,512]{1,0:T(4,128)}, f32[8,128]{1,0:T(8,128)}) custom-call(f32[56,128]{1,0:T(8,128)S(1)} %get-tuple-element.17.refs_0_.mine, f32[3,5,8,128]{3,2,1,0:T(8,128)S(1)} %get-tuple-element.24.stage, s32[8,128]{1,0:T(8,128)S(1)} %get-tuple-element.25.back, f32[8,128]{1,0:T(8,128)S(1)} %get-tuple-element.26.here, ...), custom_call_target="tpu_custom_call" | custom-call | tf_op jit(solution)/shard_map/last/pallas_call | solution.py:388
  (1 shorter events, 0.0 us)
Async XLA Ops:
  2.1 8.4 %copy-start.1 = (s32[2,1024]{1,0:T(2,128)S(1)}, s32[2,1024]{1,0:T(2,128)}, u32[]{:S(2)}) copy-start(s32[2,1024]{1,0:T(2,128)} %pair.1) | copy-start | bytes 24580
  2.1 13.1 %all-to-all-start = ((f32[8,40,128]{2,1,0:T(8,128)}), f32[8,40,128]{2,1,0:T(8,128)S(1)}, u32[]{:S(2)}, u32[]{:S(2)}) async-start(f32[8,40,128]{2,1,0:T(8,128)} %pack.1), calls=%async_computation | async-start | bytes 327680 | tf_op jit(solution)/shard_map/all_to_all | solution.py:458
  10.5 1.0 %copy-start = (f32[8,128,128]{2,1,0:T(8,128)S(1)}, f32[8,128,128]{2,1,0:T(8,128)}, u32[]{:S(2)}) copy-start(f32[8,128,128]{2,1,0:T(8,128)} %tiles.1) | copy-start | bytes 1572868
  11.7 4.4 %collective-permute-start = (f32[24,128]{1,0:T(8,128)S(1)}, f32[24,128]{1,0:T(8,128)S(1)}, u32[]{:S(2)}, u32[]{:S(2)}) collective-permute-start(f32[24,128]{1,0:T(8,128)S(1)} %get-tuple-element.16.fixed), channel_id=1, source_target_pairs={{0,2},{1,3},{2,6},{3,7},{4,0},{5,1},{6,10},{7,11},{8,4},{9,5},{10,... | collective-permute-start | bytes 36872 | tf_op jit(solution)/shard_map/ppermute | solution.py:464
  16.2 3.6 %collective-permute-start.2 = (f32[56,128]{1,0:T(8,128)S(1)}, f32[56,128]{1,0:T(8,128)S(1)}, u32[]{:S(2)}, u32[]{:S(2)}) collective-permute-start(f32[56,128]{1,0:T(8,128)S(1)} %get-tuple-element.18), channel_id=1, source_target_pairs={{0,3},{1,2},{2,1},{3,0},{4,7},{5,6},{6,5},{7,4},{8,11},{9,10},{10,... | collective-permute-start | bytes 86024 | tf_op jit(solution)/shard_map/ppermute | solution.py:482
  16.9 2.9 %collective-permute-start.1 = (f32[56,128]{1,0:T(8,128)S(1)}, f32[56,128]{1,0:T(8,128)S(1)}, u32[]{:S(2)}, u32[]{:S(2)}) collective-permute-start(f32[56,128]{1,0:T(8,128)S(1)} %get-tuple-element.17.refs_0_.mine), channel_id=1, source_target_pairs={{0,1},{1,0},{2,3},{3,2},{4,5},{5,4},{6,7},{7,6},{8,9},{9,8},{10,11... | collective-permute-start | bytes 86024 | tf_op jit(solution)/shard_map/ppermute | solution.py:483
  17.8 4.5 %collective-permute-start.3 = (f32[56,128]{1,0:T(8,128)S(1)}, f32[56,128]{1,0:T(8,128)S(1)}, u32[]{:S(2)}, u32[]{:S(2)}) collective-permute-start(f32[56,128]{1,0:T(8,128)S(1)} %get-tuple-element.19), channel_id=1, source_target_pairs={{0,2},{1,3},{2,0},{3,1},{4,6},{5,7},{6,4},{7,5},{8,10},{9,11},{10,... | collective-permute-start | bytes 86024 | tf_op jit(solution)/shard_map/ppermute | solution.py:485
  18.4 3.9 %collective-permute-start.4 = (f32[56,128]{1,0:T(8,128)S(1)}, f32[56,128]{1,0:T(8,128)S(1)}, u32[]{:S(2)}, u32[]{:S(2)}) collective-permute-start(f32[56,128]{1,0:T(8,128)S(1)} %get-tuple-element.20), channel_id=1, source_target_pairs={{0,2},{1,3},{2,0},{3,1},{4,6},{5,7},{6,4},{7,5},{8,10},{9,11},{10,... | collective-permute-start | bytes 86024 | tf_op jit(solution)/shard_map/ppermute | solution.py:485
  20.2 3.7 %collective-permute-start.7 = (f32[8,128]{1,0:T(8,128)S(1)}, f32[8,128]{1,0:T(8,128)S(1)}, u32[]{:S(2)}, u32[]{:S(2)}) collective-permute-start(f32[8,128]{1,0:T(8,128)S(1)} %get-tuple-element.26.here), channel_id=1, source_target_pairs={{0,4},{1,2},{2,1},{3,11},{4,0},{5,6},{6,5},{7,8},{8,7},{9,10},{10,... | collective-permute-start | bytes 12296 | tf_op jit(solution)/shard_map/ppermute | solution.py:499
  21.7 2.2 %collective-permute-start.6 = (f32[8,128]{1,0:T(8,128)S(1)}, f32[8,128]{1,0:T(8,128)S(1)}, u32[]{:S(2)}, u32[]{:S(2)}) collective-permute-start(f32[8,128]{1,0:T(8,128)S(1)} %get-tuple-element.26.here), channel_id=1, source_target_pairs={{0,1},{1,0},{2,6},{3,4},{4,3},{5,7},{6,2},{7,5},{8,9},{9,8},{10,14... | collective-permute-start | bytes 12296 | tf_op jit(solution)/shard_map/ppermute | solution.py:501
  21.7 2.2 %collective-permute-start.5 = (f32[8,128]{1,0:T(8,128)S(1)}, f32[8,128]{1,0:T(8,128)S(1)}, u32[]{:S(2)}, u32[]{:S(2)}) collective-permute-start(f32[8,128]{1,0:T(8,128)S(1)} %get-tuple-element.26.here), channel_id=1, source_target_pairs={{0,1},{1,0},{2,3},{3,2},{4,5},{5,4},{6,7},{7,6},{8,9},{9,8},{10,11... | collective-permute-start | bytes 12296 | tf_op jit(solution)/shard_map/ppermute | solution.py:500

commit v6 on v5

--- a/solution.py
+++ b/solution.py
@@ -157,9 +157,20 @@
         lists, others = list_rows(part, level), list_rows(part ^ apart, level)
         swapped(lists, others, own_state, other_state, out)
 
-    for r in range(GROUP):
-        level_step(0, r, 4, came_from(r), came_from(r ^ 4), once.at[r])
     second = (member + step + GROUP) % GROUP
+
+    def first_swap(half):
+        for i in range(GROUP // 2):
+            r = half + i
+            level_step(0, r, 4, came_from(r), came_from(r ^ 4), once.at[r])
+
+    near_half = member // 4 * 4
+    first_swap(near_half)
+
+    @pl.when(second // 4 * 4 != near_half)
+    def _():
+        first_swap(4 - near_half)
+
     for i, part in enumerate((member, member ^ 1, second, second ^ 1)):
         level_step(1, part, 2, once.at[part], once.at[part ^ 2], twice.at[i])
     for i, part in enumerate((member, second)):
@@ -261,15 +272,12 @@
             groups = [jnp.where(high == h, signed, 0.0) if h < limit else empty for h in heads]
             left.append(jnp.concatenate(groups + pad, axis=0))
             right.append(one_hot(row & (TILE - 1)))
-    total = 0.0
-    for k in range(0, len(left), 2):
-        total += lax.dot_general(
-            jnp.concatenate(right[k : k + 2], axis=1),
-            jnp.concatenate(left[k : k + 2], axis=1).astype(jnp.bfloat16),
-            NT,
-            preferred_element_type=jnp.float32,
-        )
-    total = total.T
+    total = lax.dot_general(
+        jnp.concatenate(left, axis=1).astype(jnp.bfloat16),
+        jnp.concatenate(right, axis=1),
+        NT,
+        preferred_element_type=jnp.float32,
+    )
     blocks = [total[FIELDS * k : FIELDS * (k + 1)] for k in range(len(heads))]
     return {h: block + pltpu.roll(block, 3, 0) for h, block in zip(heads, blocks)}
 

time: 25.4 us -> 25.9 us (1.020)
  waiting for transfers between devices: 2.37 us -> 2.84 us
    ppermute x1, starting transfers between devices: 0.69 us -> 1.13 us  [body(): from_far = send(far, perm=[(i, i ^ 3) for i in range(parts)])]
    ppermute x1, starting transfers between devices: 1.5 us -> 1.06 us  [body(): other = send(here, perm=most)]
    ppermute x1, starting transfers between devices: 0.51 us -> 0.14 us  [body(): chip = send(here, perm=within)]
    ppermute x1, starting transfers between devices: 0.01 us -> 0.37 us  [body(): mid = send(here, perm=edge)]
    ppermute x1, waiting for transfers between devices: 0.33 us -> 0.68 us  [body(): other = send(here, perm=most)]
  transfers between devices with their start and end apart: 9 -> 9, of which waited for: 2 -> 3; matrix products, arithmetic and copies ran while one was open for 0% -> 0% of each run, Pallas kernels for 11% -> 11%
where the time goes in v6:
time: 25.9 us; the launch traced here: 25.5 us
  starting transfers between devices  15.5 us (60%)
  Pallas kernels  5.46 us (21%)
  waiting for transfers between devices  2.84 us (11%)
  local copies, waits for them, and re-layouts  1.05 us (4%)
  between operations  0.68 us (3%)
    all_to_all x1, starting transfers between devices, body(): raw = lax.all_to_all(packed, 'parts', 0, 0, axis_index_groups=classes)  8.35 us
    pallas_call x7, Pallas kernels, call(): pl.pallas_call(kernel, out_shape=out_shape, in_specs=[pl.BlockSpec(memory...  5.46 us
    ppermute x2, starting transfers between devices, body(): came = (*near, send(low, perm=beyond), send(high, perm=beyond))  2.03 us
    all_to_all x1, waiting for transfers between devices, body(): raw = lax.all_to_all(packed, 'parts', 0, 0, axis_index_groups=classes)  2 us
    ppermute x1, starting transfers between devices, body(): given = send(fixed, perm=second_parts(parts, stride))  1.54 us
    ppermute x1, starting transfers between devices, body(): from_far = send(far, perm=[(i, i ^ 3) for i in range(parts)])  1.13 us
    ppermute x1, starting transfers between devices, body(): other = send(here, perm=most)  1.06 us
    unnamed x4, local copies, waits for them, and re-layouts  1.05 us
  transfers between devices with their start and end apart: 9, of which 3 were waited for; matrix products, arithmetic and copies ran while one was open for 0% of the time, Pallas kernels for 11%

profile of v6, /device:TPU:0, one launch (start us, length us, event | category | flops | bytes accessed | tf_op | source)
XLA Modules:
  0.0 25.5 jit_solution(176377661497321849)
XLA Ops:
  0.6 1.5 %pack.1 = f32[8,40,128]{2,1,0:T(8,128)} custom-call(f32[3,512]{1,0:T(4,128)} %refs_0_.1, f32[3,512]{1,0:T(4,128)} %refs_1_.1, f32[4,128]{1,0:T(4,128)} %bitcast.3, s32[3,256]{1,0:T(4,128)} %refs_3_.1, s32[1,128]{1,0:T(1,128)} %bitcast.4), custom_call_target="tpu_custom_call" | custom-call | tf_op jit(solution)/shard_map/pack/pallas_call | solution.py:396
  2.1 0.0 copy-start.1
  2.1 8.3 %all-to-all-start = ((f32[8,40,128]{2,1,0:T(8,128)}), f32[8,40,128]{2,1,0:T(8,128)S(1)}, u32[]{:S(2)}, u32[]{:S(2)}) async-start(f32[8,40,128]{2,1,0:T(8,128)} %pack.1), calls=%async_computation | async-start | bytes 327680 | tf_op jit(solution)/shard_map/all_to_all | solution.py:466
  10.5 0.0 copy-done.1
  10.5 0.0 copy-start
  10.5 1.0 %copy-done = f32[8,128,128]{2,1,0:T(8,128)S(1)} copy-done((f32[8,128,128]{2,1,0:T(8,128)S(1)}, f32[8,128,128]{2,1,0:T(8,128)}, u32[]{:S(2)}) %copy-start) | copy-done | bytes 524312
  11.5 0.2 fixed.1
  11.7 1.5 %collective-permute-start = (f32[24,128]{1,0:T(8,128)S(1)}, f32[24,128]{1,0:T(8,128)S(1)}, u32[]{:S(2)}, u32[]{:S(2)}) collective-permute-start(f32[24,128]{1,0:T(8,128)S(1)} %get-tuple-element.16.fixed), channel_id=1, source_target_pairs={{0,2},{1,3},{2,6},{3,7},{4,0},{5,1},{6,10},{7,11},{8,4},{9,5},{10,... | collective-permute-start | bytes 36872 | tf_op jit(solution)/shard_map/ppermute | solution.py:472
  13.3 2.0 %all-to-all-done.raw = f32[8,40,128]{2,1,0:T(8,128)S(1)} async-done(((f32[8,40,128]{2,1,0:T(8,128)}), f32[8,40,128]{2,1,0:T(8,128)S(1)}, u32[]{:S(2)}, u32[]{:S(2)}) %all-to-all-start) | async-done | bytes 163872 | tf_op jit(solution)/shard_map/all_to_all | solution.py:466
  15.3 1.0 %compose.1.states = f32[2,32,128]{2,1,0:T(8,128)S(1)} custom-call(f32[8,40,128]{2,1,0:T(8,128)S(1)} %all-to-all-done.raw), custom_call_target="tpu_custom_call" | custom-call | tf_op jit(solution)/shard_map/compose/pallas_call | solution.py:396
  16.2 0.0 collective-permute-done.given
  16.3 1.1 %collective-permute-start.2 = (f32[56,128]{1,0:T(8,128)S(1)}, f32[56,128]{1,0:T(8,128)S(1)}, u32[]{:S(2)}, u32[]{:S(2)}) collective-permute-start(f32[56,128]{1,0:T(8,128)S(1)} %get-tuple-element.18), channel_id=1, source_target_pairs={{0,3},{1,2},{2,1},{3,0},{4,7},{5,6},{6,5},{7,4},{8,11},{9,10},{10,... | collective-permute-start | bytes 86024 | tf_op jit(solution)/shard_map/ppermute | solution.py:490
  17.4 0.9 %collective-permute-start.1 = (f32[56,128]{1,0:T(8,128)S(1)}, f32[56,128]{1,0:T(8,128)S(1)}, u32[]{:S(2)}, u32[]{:S(2)}) collective-permute-start(f32[56,128]{1,0:T(8,128)S(1)} %get-tuple-element.17.refs_0_.mine), channel_id=1, source_target_pairs={{0,1},{1,0},{2,3},{3,2},{4,5},{5,4},{6,7},{7,6},{8,9},{9,8},{10,11... | collective-permute-start | bytes 86024 | tf_op jit(solution)/shard_map/ppermute | solution.py:491
  18.3 0.2 collective-permute-start.3
  18.5 1.8 %collective-permute-start.4 = (f32[56,128]{1,0:T(8,128)S(1)}, f32[56,128]{1,0:T(8,128)S(1)}, u32[]{:S(2)}, u32[]{:S(2)}) collective-permute-start(f32[56,128]{1,0:T(8,128)S(1)} %get-tuple-element.20), channel_id=1, source_target_pairs={{0,2},{1,3},{2,0},{3,1},{4,6},{5,7},{6,4},{7,5},{8,10},{9,11},{10,... | collective-permute-start | bytes 86024 | tf_op jit(solution)/shard_map/ppermute | solution.py:493
  20.3 0.0 collective-permute-done.2.refs_2_
  20.4 0.0 collective-permute-done.1.refs_1_
  20.4 0.4 %near.1 = (f32[8,128]{1,0:T(8,128)S(1)}, f32[4,8,128]{2,1,0:T(8,128)S(1)}) custom-call(f32[56,128]{1,0:T(8,128)S(1)} %get-tuple-element.17.refs_0_.mine, f32[56,128]{1,0:T(8,128)S(1)} %collective-permute-done.1.refs_1_, f32[56,128]{1,0:T(8,128)S(1)} %collective-permute-done.2.refs_2_, bf16[8,128,128]{2,1,0:T(8,128)(2,1)S(1)} %get-tuple-element.21.refs_3_, ...), custom_call_target="tpu_custom_call" | custom-call | tf_op jit(solution)/shard_map/near/pallas_call | solution.py:396
  20.8 1.1 %collective-permute-start.7 = (f32[8,128]{1,0:T(8,128)S(1)}, f32[8,128]{1,0:T(8,128)S(1)}, u32[]{:S(2)}, u32[]{:S(2)}) collective-permute-start(f32[8,128]{1,0:T(8,128)S(1)} %get-tuple-element.26.here), channel_id=1, source_target_pairs={{0,4},{1,2},{2,1},{3,11},{4,0},{5,6},{6,5},{7,8},{8,7},{9,10},{10,... | collective-permute-start | bytes 12296 | tf_op jit(solution)/shard_map/ppermute | solution.py:507
  21.8 0.4 %collective-permute-start.6 = (f32[8,128]{1,0:T(8,128)S(1)}, f32[8,128]{1,0:T(8,128)S(1)}, u32[]{:S(2)}, u32[]{:S(2)}) collective-permute-start(f32[8,128]{1,0:T(8,128)S(1)} %get-tuple-element.26.here), channel_id=1, source_target_pairs={{0,1},{1,0},{2,6},{3,4},{4,3},{5,7},{6,2},{7,5},{8,9},{9,8},{10,14... | collective-permute-start | bytes 12296 | tf_op jit(solution)/shard_map/ppermute | solution.py:509
  22.2 0.1 collective-permute-start.5
  22.4 0.0 collective-permute-done.3.refs_3_
  22.4 0.1 collective-permute-done.4.refs_4_
  22.5 1.3 %middle.1 = (f32[3,5,8,128]{3,2,1,0:T(8,128)S(1)}, s32[8,128]{1,0:T(8,128)S(1)}, f32[3,24,128]{2,1,0:T(8,128)S(1)}) custom-call(f32[56,128]{1,0:T(8,128)S(1)} %get-tuple-element.17.refs_0_.mine, f32[56,128]{1,0:T(8,128)S(1)} %collective-permute-done.1.refs_1_, f32[56,128]{1,0:T(8,128)S(1)} %collective-permute-done.2.refs_2_, ...), custom_call_target="tpu_custom_call" | custom-call | tf_op jit(solution)/shard_map/middle/pallas_call | solution.py:396
  23.8 0.7 %collective-permute-done.7.other = f32[8,128]{1,0:T(8,128)S(1)} collective-permute-done((f32[8,128]{1,0:T(8,128)S(1)}, f32[8,128]{1,0:T(8,128)S(1)}, u32[]{:S(2)}, u32[]{:S(2)}) %collective-permute-start.7) | collective-permute-done | bytes 4128 | tf_op jit(solution)/shard_map/ppermute | solution.py:507
  24.5 0.0 collective-permute-done.6.mid
  24.5 0.0 collective-permute-done.5.chip
  24.5 1.1 %last.1 = (f32[3,512]{1,0:T(4,128)}, f32[8,128]{1,0:T(8,128)}) custom-call(f32[56,128]{1,0:T(8,128)S(1)} %get-tuple-element.17.refs_0_.mine, f32[3,5,8,128]{3,2,1,0:T(8,128)S(1)} %get-tuple-element.24.stage, s32[8,128]{1,0:T(8,128)S(1)} %get-tuple-element.25.back, f32[8,128]{1,0:T(8,128)S(1)} %get-tuple-element.26.here, ...), custom_call_target="tpu_custom_call" | custom-call | tf_op jit(solution)/shard_map/last/pallas_call | solution.py:396
  (1 shorter events, 0.0 us)
Async XLA Ops:
  2.1 8.4 %copy-start.1 = (s32[2,1024]{1,0:T(2,128)S(1)}, s32[2,1024]{1,0:T(2,128)}, u32[]{:S(2)}) copy-start(s32[2,1024]{1,0:T(2,128)} %pair.1) | copy-start | bytes 24580
  2.1 13.1 %all-to-all-start = ((f32[8,40,128]{2,1,0:T(8,128)}), f32[8,40,128]{2,1,0:T(8,128)S(1)}, u32[]{:S(2)}, u32[]{:S(2)}) async-start(f32[8,40,128]{2,1,0:T(8,128)} %pack.1), calls=%async_computation | async-start | bytes 327680 | tf_op jit(solution)/shard_map/all_to_all | solution.py:466
  10.5 1.0 %copy-start = (f32[8,128,128]{2,1,0:T(8,128)S(1)}, f32[8,128,128]{2,1,0:T(8,128)}, u32[]{:S(2)}) copy-start(f32[8,128,128]{2,1,0:T(8,128)} %tiles.1) | copy-start | bytes 1572868
  11.7 4.5 %collective-permute-start = (f32[24,128]{1,0:T(8,128)S(1)}, f32[24,128]{1,0:T(8,128)S(1)}, u32[]{:S(2)}, u32[]{:S(2)}) collective-permute-start(f32[24,128]{1,0:T(8,128)S(1)} %get-tuple-element.16.fixed), channel_id=1, source_target_pairs={{0,2},{1,3},{2,6},{3,7},{4,0},{5,1},{6,10},{7,11},{8,4},{9,5},{10,... | collective-permute-start | bytes 36872 | tf_op jit(solution)/shard_map/ppermute | solution.py:472
  16.3 4.1 %collective-permute-start.2 = (f32[56,128]{1,0:T(8,128)S(1)}, f32[56,128]{1,0:T(8,128)S(1)}, u32[]{:S(2)}, u32[]{:S(2)}) collective-permute-start(f32[56,128]{1,0:T(8,128)S(1)} %get-tuple-element.18), channel_id=1, source_target_pairs={{0,3},{1,2},{2,1},{3,0},{4,7},{5,6},{6,5},{7,4},{8,11},{9,10},{10,... | collective-permute-start | bytes 86024 | tf_op jit(solution)/shard_map/ppermute | solution.py:490
  17.4 2.9 %collective-permute-start.1 = (f32[56,128]{1,0:T(8,128)S(1)}, f32[56,128]{1,0:T(8,128)S(1)}, u32[]{:S(2)}, u32[]{:S(2)}) collective-permute-start(f32[56,128]{1,0:T(8,128)S(1)} %get-tuple-element.17.refs_0_.mine), channel_id=1, source_target_pairs={{0,1},{1,0},{2,3},{3,2},{4,5},{5,4},{6,7},{7,6},{8,9},{9,8},{10,11... | collective-permute-start | bytes 86024 | tf_op jit(solution)/shard_map/ppermute | solution.py:491
  18.3 4.0 %collective-permute-start.3 = (f32[56,128]{1,0:T(8,128)S(1)}, f32[56,128]{1,0:T(8,128)S(1)}, u32[]{:S(2)}, u32[]{:S(2)}) collective-permute-start(f32[56,128]{1,0:T(8,128)S(1)} %get-tuple-element.19), channel_id=1, source_target_pairs={{0,2},{1,3},{2,0},{3,1},{4,6},{5,7},{6,4},{7,5},{8,10},{9,11},{10,... | collective-permute-start | bytes 86024 | tf_op jit(solution)/shard_map/ppermute | solution.py:493
  18.5 4.0 %collective-permute-start.4 = (f32[56,128]{1,0:T(8,128)S(1)}, f32[56,128]{1,0:T(8,128)S(1)}, u32[]{:S(2)}, u32[]{:S(2)}) collective-permute-start(f32[56,128]{1,0:T(8,128)S(1)} %get-tuple-element.20), channel_id=1, source_target_pairs={{0,2},{1,3},{2,0},{3,1},{4,6},{5,7},{6,4},{7,5},{8,10},{9,11},{10,... | collective-permute-start | bytes 86024 | tf_op jit(solution)/shard_map/ppermute | solution.py:493
  20.8 3.7 %collective-permute-start.7 = (f32[8,128]{1,0:T(8,128)S(1)}, f32[8,128]{1,0:T(8,128)S(1)}, u32[]{:S(2)}, u32[]{:S(2)}) collective-permute-start(f32[8,128]{1,0:T(8,128)S(1)} %get-tuple-element.26.here), channel_id=1, source_target_pairs={{0,4},{1,2},{2,1},{3,11},{4,0},{5,6},{6,5},{7,8},{8,7},{9,10},{10,... | collective-permute-start | bytes 12296 | tf_op jit(solution)/shard_map/ppermute | solution.py:507
  21.8 2.6 %collective-permute-start.6 = (f32[8,128]{1,0:T(8,128)S(1)}, f32[8,128]{1,0:T(8,128)S(1)}, u32[]{:S(2)}, u32[]{:S(2)}) collective-permute-start(f32[8,128]{1,0:T(8,128)S(1)} %get-tuple-element.26.here), channel_id=1, source_target_pairs={{0,1},{1,0},{2,6},{3,4},{4,3},{5,7},{6,2},{7,5},{8,9},{9,8},{10,14... | collective-permute-start | bytes 12296 | tf_op jit(solution)/shard_map/ppermute | solution.py:509
  22.2 2.2 %collective-permute-start.5 = (f32[8,128]{1,0:T(8,128)S(1)}, f32[8,128]{1,0:T(8,128)S(1)}, u32[]{:S(2)}, u32[]{:S(2)}) collective-permute-start(f32[8,128]{1,0:T(8,128)S(1)} %get-tuple-element.26.here), channel_id=1, source_target_pairs={{0,1},{1,0},{2,3},{3,2},{4,5},{5,4},{6,7},{7,6},{8,9},{9,8},{10,11... | collective-permute-start | bytes 12296 | tf_op jit(solution)/shard_map/ppermute | solution.py:508

commit v7 on v6

--- a/solution.py
+++ b/solution.py
@@ -23,6 +23,7 @@
 RAW = 40
 FIXED = RECORD - FIRST_AT
 BLOCK = 4
+LISTED = (7, 0, 6, 1, 2, 3, 4, 5)
 PARAMS = pltpu.CompilerParams(vmem_limit_bytes=32 * 2**20)
 FROM_HBM = pltpu.CompilerParams(vmem_limit_bytes=63 * 2**20)
 NT = (((1,), (1,)), ((), ()))
@@ -119,6 +120,12 @@
         out[pl.ds(2 * FIELDS + t, 1), :] = diag
 
 
+def place_of(block):
+    if isinstance(block, int):
+        return LISTED.index(block)
+    return sum(jnp.where(block == one, at, 0) for at, one in enumerate(LISTED))
+
+
 def second_part(stride):
     me = lax.axis_index("parts")
     member, kind = me // stride, me % stride
@@ -147,7 +154,7 @@
     step, exists = second_part(stride)
 
     def came_from(part):
-        return raw.at[(part + 2) % GROUP]
+        return raw.at[place_of(part)]
 
     def list_rows(part, level):
         rows = came_from(part)
@@ -157,20 +164,9 @@
         lists, others = list_rows(part, level), list_rows(part ^ apart, level)
         swapped(lists, others, own_state, other_state, out)
 
+    for r in range(GROUP):
+        level_step(0, r, 4, came_from(r), came_from(r ^ 4), once.at[r])
     second = (member + step + GROUP) % GROUP
-
-    def first_swap(half):
-        for i in range(GROUP // 2):
-            r = half + i
-            level_step(0, r, 4, came_from(r), came_from(r ^ 4), once.at[r])
-
-    near_half = member // 4 * 4
-    first_swap(near_half)
-
-    @pl.when(second // 4 * 4 != near_half)
-    def _():
-        first_swap(4 - near_half)
-
     for i, part in enumerate((member, member ^ 1, second, second ^ 1)):
         level_step(1, part, 2, once.at[part], once.at[part ^ 2], twice.at[i])
     for i, part in enumerate((member, second)):
@@ -462,7 +458,7 @@
         [pltpu.VMEM(one.shape, one.dtype) for one in inputs]
         + [pltpu.SemaphoreType.DMA((5,))],
     )
-    classes = [[r + stride * ((k - 2) % GROUP) for k in range(GROUP)] for r in range(stride)]
+    classes = [[r + stride * k for k in LISTED] for r in range(stride)]
     raw = lax.all_to_all(packed, "parts", 0, 0, axis_index_groups=classes)
 
     half = jax.ShapeDtypeStruct(delassus.shape, jnp.bfloat16)

time: 25.9 us -> 26 us (level)
  starting transfers between devices: 15.5 us -> 17.1 us
  waiting for transfers between devices: 2.84 us -> 1.46 us
    ppermute x1, starting transfers between devices: 1.06 us -> 2.01 us  [body(): other = send(here, perm=most)]
    all_to_all x1, starting transfers between devices: 8.35 us -> 9.3 us  [body(): raw = lax.all_to_all(packed, 'parts', 0, 0, axis_index_groups=classes)]
    ppermute x1, starting transfers between devices: 1.13 us -> 0.35 us  [body(): from_far = send(far, perm=[(i, i ^ 3) for i in range(parts)])]
    ppermute x1, waiting for transfers between devices: 0.68 us -> 0.01 us  [body(): other = send(here, perm=most)]
    all_to_all x1, waiting for transfers between devices: 2 us -> 1.44 us  [body(): raw = lax.all_to_all(packed, 'parts', 0, 0, axis_index_groups=classes)]
    ppermute x1, starting transfers between devices: 0.89 us -> 1.32 us  [body(): near = (mine, send(mine, perm=within), from_far)]
    ppermute x1, starting transfers between devices: 0.14 us -> 0.51 us  [body(): chip = send(here, perm=within)]
    ppermute x1, starting transfers between devices: 0.37 us -> 0.01 us  [body(): mid = send(here, perm=edge)]
  transfers between devices with their start and end apart: 9 -> 9, of which waited for: 3 -> 1; matrix products, arithmetic and copies ran while one was open for 0% -> 0% of each run, Pallas kernels for 11% -> 11%
where the time goes in v7:
time: 26 us; the launch traced here: 25.6 us
  starting transfers between devices  17.1 us (66%)
  Pallas kernels  5.35 us (21%)
  waiting for transfers between devices  1.46 us (6%)
  local copies, waits for them, and re-layouts  1.05 us (4%)
  between operations  0.7 us (3%)
    all_to_all x1, starting transfers between devices, body(): raw = lax.all_to_all(packed, 'parts', 0, 0, axis_index_groups=classes)  9.3 us
    pallas_call x7, Pallas kernels, call(): pl.pallas_call(kernel, out_shape=out_shape, in_specs=[pl.BlockSpec(memory...  5.35 us
    ppermute x2, starting transfers between devices, body(): came = (*near, send(low, perm=beyond), send(high, perm=beyond))  2.03 us
    ppermute x1, starting transfers between devices, body(): other = send(here, perm=most)  2.01 us
    ppermute x1, starting transfers between devices, body(): given = send(fixed, perm=second_parts(parts, stride))  1.54 us
    all_to_all x1, waiting for transfers between devices, body(): raw = lax.all_to_all(packed, 'parts', 0, 0, axis_index_groups=classes)  1.44 us
    ppermute x1, starting transfers between devices, body(): near = (mine, send(mine, perm=within), from_far)  1.32 us
    unnamed x4, local copies, waits for them, and re-layouts  1.05 us
  transfers between devices with their start and end apart: 9, of which 1 were waited for; matrix products, arithmetic and copies ran while one was open for 0% of the time, Pallas kernels for 11%

profile of v7, /device:TPU:0, one launch (start us, length us, event | category | flops | bytes accessed | tf_op | source)
XLA Modules:
  0.0 25.6 jit_solution(3057160036545345777)
XLA Ops:
  0.6 1.5 %pack.1 = f32[8,40,128]{2,1,0:T(8,128)} custom-call(f32[3,512]{1,0:T(4,128)} %refs_0_.1, f32[3,512]{1,0:T(4,128)} %refs_1_.1, f32[4,128]{1,0:T(4,128)} %bitcast.3, s32[3,256]{1,0:T(4,128)} %refs_3_.1, s32[1,128]{1,0:T(1,128)} %bitcast.4), custom_call_target="tpu_custom_call" | custom-call | tf_op jit(solution)/shard_map/pack/pallas_call | solution.py:392
  2.1 0.0 copy-start.1
  2.1 9.3 %all-to-all-start = ((f32[8,40,128]{2,1,0:T(8,128)}), f32[8,40,128]{2,1,0:T(8,128)S(1)}, u32[]{:S(2)}, u32[]{:S(2)}) async-start(f32[8,40,128]{2,1,0:T(8,128)} %pack.1), calls=%async_computation | async-start | bytes 327680 | tf_op jit(solution)/shard_map/all_to_all | solution.py:462
  11.4 0.0 copy-done.1
  11.4 0.0 copy-start
  11.4 1.0 %copy-done = f32[8,128,128]{2,1,0:T(8,128)S(1)} copy-done((f32[8,128,128]{2,1,0:T(8,128)S(1)}, f32[8,128,128]{2,1,0:T(8,128)}, u32[]{:S(2)}) %copy-start) | copy-done | bytes 524312
  12.5 0.2 fixed.1
  12.7 1.5 %collective-permute-start = (f32[24,128]{1,0:T(8,128)S(1)}, f32[24,128]{1,0:T(8,128)S(1)}, u32[]{:S(2)}, u32[]{:S(2)}) collective-permute-start(f32[24,128]{1,0:T(8,128)S(1)} %get-tuple-element.16.fixed), channel_id=1, source_target_pairs={{0,2},{1,3},{2,6},{3,7},{4,0},{5,1},{6,10},{7,11},{8,4},{9,5},{10,... | collective-permute-start | bytes 36872 | tf_op jit(solution)/shard_map/ppermute | solution.py:468
  14.2 1.4 %all-to-all-done.raw = f32[8,40,128]{2,1,0:T(8,128)S(1)} async-done(((f32[8,40,128]{2,1,0:T(8,128)}), f32[8,40,128]{2,1,0:T(8,128)S(1)}, u32[]{:S(2)}, u32[]{:S(2)}) %all-to-all-start) | async-done | bytes 163872 | tf_op jit(solution)/shard_map/all_to_all | solution.py:462
  15.7 0.9 %compose.1.states = f32[2,32,128]{2,1,0:T(8,128)S(1)} custom-call(f32[8,40,128]{2,1,0:T(8,128)S(1)} %all-to-all-done.raw), custom_call_target="tpu_custom_call" | custom-call | tf_op jit(solution)/shard_map/compose/pallas_call | solution.py:392
  16.5 0.0 collective-permute-done.given
  16.6 0.4 %collective-permute-start.2 = (f32[56,128]{1,0:T(8,128)S(1)}, f32[56,128]{1,0:T(8,128)S(1)}, u32[]{:S(2)}, u32[]{:S(2)}) collective-permute-start(f32[56,128]{1,0:T(8,128)S(1)} %get-tuple-element.18), channel_id=1, source_target_pairs={{0,3},{1,2},{2,1},{3,0},{4,7},{5,6},{6,5},{7,4},{8,11},{9,10},{10,... | collective-permute-start | bytes 86024 | tf_op jit(solution)/shard_map/ppermute | solution.py:486
  16.9 1.3 %collective-permute-start.1 = (f32[56,128]{1,0:T(8,128)S(1)}, f32[56,128]{1,0:T(8,128)S(1)}, u32[]{:S(2)}, u32[]{:S(2)}) collective-permute-start(f32[56,128]{1,0:T(8,128)S(1)} %get-tuple-element.17.refs_0_.mine), channel_id=1, source_target_pairs={{0,1},{1,0},{2,3},{3,2},{4,5},{5,4},{6,7},{7,6},{8,9},{9,8},{10,11... | collective-permute-start | bytes 86024 | tf_op jit(solution)/shard_map/ppermute | solution.py:487
  18.2 0.5 %collective-permute-start.3 = (f32[56,128]{1,0:T(8,128)S(1)}, f32[56,128]{1,0:T(8,128)S(1)}, u32[]{:S(2)}, u32[]{:S(2)}) collective-permute-start(f32[56,128]{1,0:T(8,128)S(1)} %get-tuple-element.19), channel_id=1, source_target_pairs={{0,2},{1,3},{2,0},{3,1},{4,6},{5,7},{6,4},{7,5},{8,10},{9,11},{10,... | collective-permute-start | bytes 86024 | tf_op jit(solution)/shard_map/ppermute | solution.py:489
  18.8 1.5 %collective-permute-start.4 = (f32[56,128]{1,0:T(8,128)S(1)}, f32[56,128]{1,0:T(8,128)S(1)}, u32[]{:S(2)}, u32[]{:S(2)}) collective-permute-start(f32[56,128]{1,0:T(8,128)S(1)} %get-tuple-element.20), channel_id=1, source_target_pairs={{0,2},{1,3},{2,0},{3,1},{4,6},{5,7},{6,4},{7,5},{8,10},{9,11},{10,... | collective-permute-start | bytes 86024 | tf_op jit(solution)/shard_map/ppermute | solution.py:489
  20.3 0.0 collective-permute-done.2.refs_2_
  20.3 0.0 collective-permute-done.1.refs_1_
  20.3 0.4 %near.1 = (f32[8,128]{1,0:T(8,128)S(1)}, f32[4,8,128]{2,1,0:T(8,128)S(1)}) custom-call(f32[56,128]{1,0:T(8,128)S(1)} %get-tuple-element.17.refs_0_.mine, f32[56,128]{1,0:T(8,128)S(1)} %collective-permute-done.1.refs_1_, f32[56,128]{1,0:T(8,128)S(1)} %collective-permute-done.2.refs_2_, bf16[8,128,128]{2,1,0:T(8,128)(2,1)S(1)} %get-tuple-element.21.refs_3_, ...), custom_call_target="tpu_custom_call" | custom-call | tf_op jit(solution)/shard_map/near/pallas_call | solution.py:392
  20.7 2.0 %collective-permute-start.7 = (f32[8,128]{1,0:T(8,128)S(1)}, f32[8,128]{1,0:T(8,128)S(1)}, u32[]{:S(2)}, u32[]{:S(2)}) collective-permute-start(f32[8,128]{1,0:T(8,128)S(1)} %get-tuple-element.26.here), channel_id=1, source_target_pairs={{0,4},{1,2},{2,1},{3,11},{4,0},{5,6},{6,5},{7,8},{8,7},{9,10},{10,... | collective-permute-start | bytes 12296 | tf_op jit(solution)/shard_map/ppermute | solution.py:503
  22.7 0.0 collective-permute-start.6
  22.7 0.5 %collective-permute-start.5 = (f32[8,128]{1,0:T(8,128)S(1)}, f32[8,128]{1,0:T(8,128)S(1)}, u32[]{:S(2)}, u32[]{:S(2)}) collective-permute-start(f32[8,128]{1,0:T(8,128)S(1)} %get-tuple-element.26.here), channel_id=1, source_target_pairs={{0,1},{1,0},{2,3},{3,2},{4,5},{5,4},{6,7},{7,6},{8,9},{9,8},{10,11... | collective-permute-start | bytes 12296 | tf_op jit(solution)/shard_map/ppermute | solution.py:504
  23.2 0.0 collective-permute-done.3.refs_3_
  23.2 0.0 collective-permute-done.4.refs_4_
  23.2 1.3 %middle.1 = (f32[3,5,8,128]{3,2,1,0:T(8,128)S(1)}, s32[8,128]{1,0:T(8,128)S(1)}, f32[3,24,128]{2,1,0:T(8,128)S(1)}) custom-call(f32[56,128]{1,0:T(8,128)S(1)} %get-tuple-element.17.refs_0_.mine, f32[56,128]{1,0:T(8,128)S(1)} %collective-permute-done.1.refs_1_, f32[56,128]{1,0:T(8,128)S(1)} %collective-permute-done.2.refs_2_, ...), custom_call_target="tpu_custom_call" | custom-call | tf_op jit(solution)/shard_map/middle/pallas_call | solution.py:392
  24.5 0.0 collective-permute-done.7.other
  24.5 0.0 collective-permute-done.6.mid
  24.5 0.0 collective-permute-done.5.chip
  24.5 1.1 %last.1 = (f32[3,512]{1,0:T(4,128)}, f32[8,128]{1,0:T(8,128)}) custom-call(f32[56,128]{1,0:T(8,128)S(1)} %get-tuple-element.17.refs_0_.mine, f32[3,5,8,128]{3,2,1,0:T(8,128)S(1)} %get-tuple-element.24.stage, s32[8,128]{1,0:T(8,128)S(1)} %get-tuple-element.25.back, f32[8,128]{1,0:T(8,128)S(1)} %get-tuple-element.26.here, ...), custom_call_target="tpu_custom_call" | custom-call | tf_op jit(solution)/shard_map/last/pallas_call | solution.py:392
  (1 shorter events, 0.0 us)
Async XLA Ops:
  2.1 9.3 %copy-start.1 = (s32[2,1024]{1,0:T(2,128)S(1)}, s32[2,1024]{1,0:T(2,128)}, u32[]{:S(2)}) copy-start(s32[2,1024]{1,0:T(2,128)} %pair.1) | copy-start | bytes 24580
  2.1 13.5 %all-to-all-start = ((f32[8,40,128]{2,1,0:T(8,128)}), f32[8,40,128]{2,1,0:T(8,128)S(1)}, u32[]{:S(2)}, u32[]{:S(2)}) async-start(f32[8,40,128]{2,1,0:T(8,128)} %pack.1), calls=%async_computation | async-start | bytes 327680 | tf_op jit(solution)/shard_map/all_to_all | solution.py:462
  11.4 1.0 %copy-start = (f32[8,128,128]{2,1,0:T(8,128)S(1)}, f32[8,128,128]{2,1,0:T(8,128)}, u32[]{:S(2)}) copy-start(f32[8,128,128]{2,1,0:T(8,128)} %tiles.1) | copy-start | bytes 1572868
  12.7 3.8 %collective-permute-start = (f32[24,128]{1,0:T(8,128)S(1)}, f32[24,128]{1,0:T(8,128)S(1)}, u32[]{:S(2)}, u32[]{:S(2)}) collective-permute-start(f32[24,128]{1,0:T(8,128)S(1)} %get-tuple-element.16.fixed), channel_id=1, source_target_pairs={{0,2},{1,3},{2,6},{3,7},{4,0},{5,1},{6,10},{7,11},{8,4},{9,5},{10,... | collective-permute-start | bytes 36872 | tf_op jit(solution)/shard_map/ppermute | solution.py:468
  16.6 3.7 %collective-permute-start.2 = (f32[56,128]{1,0:T(8,128)S(1)}, f32[56,128]{1,0:T(8,128)S(1)}, u32[]{:S(2)}, u32[]{:S(2)}) collective-permute-start(f32[56,128]{1,0:T(8,128)S(1)} %get-tuple-element.18), channel_id=1, source_target_pairs={{0,3},{1,2},{2,1},{3,0},{4,7},{5,6},{6,5},{7,4},{8,11},{9,10},{10,... | collective-permute-start | bytes 86024 | tf_op jit(solution)/shard_map/ppermute | solution.py:486
  16.9 3.4 %collective-permute-start.1 = (f32[56,128]{1,0:T(8,128)S(1)}, f32[56,128]{1,0:T(8,128)S(1)}, u32[]{:S(2)}, u32[]{:S(2)}) collective-permute-start(f32[56,128]{1,0:T(8,128)S(1)} %get-tuple-element.17.refs_0_.mine), channel_id=1, source_target_pairs={{0,1},{1,0},{2,3},{3,2},{4,5},{5,4},{6,7},{7,6},{8,9},{9,8},{10,11... | collective-permute-start | bytes 86024 | tf_op jit(solution)/shard_map/ppermute | solution.py:487
  18.2 5.0 %collective-permute-start.3 = (f32[56,128]{1,0:T(8,128)S(1)}, f32[56,128]{1,0:T(8,128)S(1)}, u32[]{:S(2)}, u32[]{:S(2)}) collective-permute-start(f32[56,128]{1,0:T(8,128)S(1)} %get-tuple-element.19), channel_id=1, source_target_pairs={{0,2},{1,3},{2,0},{3,1},{4,6},{5,7},{6,4},{7,5},{8,10},{9,11},{10,... | collective-permute-start | bytes 86024 | tf_op jit(solution)/shard_map/ppermute | solution.py:489
  18.8 4.5 %collective-permute-start.4 = (f32[56,128]{1,0:T(8,128)S(1)}, f32[56,128]{1,0:T(8,128)S(1)}, u32[]{:S(2)}, u32[]{:S(2)}) collective-permute-start(f32[56,128]{1,0:T(8,128)S(1)} %get-tuple-element.20), channel_id=1, source_target_pairs={{0,2},{1,3},{2,0},{3,1},{4,6},{5,7},{6,4},{7,5},{8,10},{9,11},{10,... | collective-permute-start | bytes 86024 | tf_op jit(solution)/shard_map/ppermute | solution.py:489
  20.7 3.8 %collective-permute-start.7 = (f32[8,128]{1,0:T(8,128)S(1)}, f32[8,128]{1,0:T(8,128)S(1)}, u32[]{:S(2)}, u32[]{:S(2)}) collective-permute-start(f32[8,128]{1,0:T(8,128)S(1)} %get-tuple-element.26.here), channel_id=1, source_target_pairs={{0,4},{1,2},{2,1},{3,11},{4,0},{5,6},{6,5},{7,8},{8,7},{9,10},{10,... | collective-permute-start | bytes 12296 | tf_op jit(solution)/shard_map/ppermute | solution.py:503
  22.7 1.8 %collective-permute-start.6 = (f32[8,128]{1,0:T(8,128)S(1)}, f32[8,128]{1,0:T(8,128)S(1)}, u32[]{:S(2)}, u32[]{:S(2)}) collective-permute-start(f32[8,128]{1,0:T(8,128)S(1)} %get-tuple-element.26.here), channel_id=1, source_target_pairs={{0,1},{1,0},{2,6},{3,4},{4,3},{5,7},{6,2},{7,5},{8,9},{9,8},{10,14... | collective-permute-start | bytes 12296 | tf_op jit(solution)/shard_map/ppermute | solution.py:505
  22.7 1.8 %collective-permute-start.5 = (f32[8,128]{1,0:T(8,128)S(1)}, f32[8,128]{1,0:T(8,128)S(1)}, u32[]{:S(2)}, u32[]{:S(2)}) collective-permute-start(f32[8,128]{1,0:T(8,128)S(1)} %get-tuple-element.26.here), channel_id=1, source_target_pairs={{0,1},{1,0},{2,3},{3,2},{4,5},{5,4},{6,7},{7,6},{8,9},{9,8},{10,11... | collective-permute-start | bytes 12296 | tf_op jit(solution)/shard_map/ppermute | solution.py:504

commit v8 on v7

--- a/solution.py
+++ b/solution.py
@@ -23,7 +23,7 @@
 RAW = 40
 FIXED = RECORD - FIRST_AT
 BLOCK = 4
-LISTED = (7, 0, 6, 1, 2, 3, 4, 5)
+LISTED = (2, 0, 1, 3, 4, 5, 6, 7)
 PARAMS = pltpu.CompilerParams(vmem_limit_bytes=32 * 2**20)
 FROM_HBM = pltpu.CompilerParams(vmem_limit_bytes=63 * 2**20)
 NT = (((1,), (1,)), ((), ()))

time: 26 us -> 26.6 us (1.023)
  waiting for transfers between devices: 1.46 us -> 4.72 us
  starting transfers between devices: 17.1 us -> 14.4 us
    all_to_all x1, waiting for transfers between devices: 1.44 us -> 3.65 us  [body(): raw = lax.all_to_all(packed, 'parts', 0, 0, axis_index_groups=classes)]
    all_to_all x1, starting transfers between devices: 9.3 us -> 7.85 us  [body(): raw = lax.all_to_all(packed, 'parts', 0, 0, axis_index_groups=classes)]
    ppermute x1, starting transfers between devices: 2.01 us -> 0.58 us  [body(): other = send(here, perm=most)]
    ppermute x1, starting transfers between devices: 0.01 us -> 0.75 us  [body(): mid = send(here, perm=edge)]
    ppermute x2, waiting for transfers between devices: 0.01 us -> 0.61 us  [body(): came = (*near, send(low, perm=beyond), send(high, perm=beyond))]
    ppermute x1, starting transfers between devices: 0.51 us -> 0.01 us  [body(): chip = send(here, perm=within)]
    ppermute x1, waiting for transfers between devices: 0.01 us -> 0.45 us  [body(): other = send(here, perm=most)]
    ppermute x1, starting transfers between devices: 0.35 us -> 0.07 us  [body(): from_far = send(far, perm=[(i, i ^ 3) for i in range(parts)])]
  transfers between devices with their start and end apart: 9 -> 9, of which waited for: 1 -> 4; matrix products, arithmetic and copies ran while one was open for 0% -> 0% of each run, Pallas kernels for 11% -> 11%
where the time goes in v8:
time: 26.6 us; the launch traced here: 26.2 us
  starting transfers between devices  14.4 us (54%)
  Pallas kernels  5.35 us (20%)
  waiting for transfers between devices  4.72 us (18%)
  local copies, waits for them, and re-layouts  1.05 us (4%)
  between operations  0.69 us (3%)
    all_to_all x1, starting transfers between devices, body(): raw = lax.all_to_all(packed, 'parts', 0, 0, axis_index_groups=classes)  7.85 us
    pallas_call x7, Pallas kernels, call(): pl.pallas_call(kernel, out_shape=out_shape, in_specs=[pl.BlockSpec(memory...  5.35 us
    all_to_all x1, waiting for transfers between devices, body(): raw = lax.all_to_all(packed, 'parts', 0, 0, axis_index_groups=classes)  3.65 us
    ppermute x2, starting transfers between devices, body(): came = (*near, send(low, perm=beyond), send(high, perm=beyond))  2.03 us
    ppermute x1, starting transfers between devices, body(): near = (mine, send(mine, perm=within), from_far)  1.59 us
    ppermute x1, starting transfers between devices, body(): given = send(fixed, perm=second_parts(parts, stride))  1.54 us
    unnamed x4, local copies, waits for them, and re-layouts  1.05 us
    ppermute x1, starting transfers between devices, body(): mid = send(here, perm=edge)  0.75 us
  transfers between devices with their start and end apart: 9, of which 4 were waited for; matrix products, arithmetic and copies ran while one was open for 0% of the time, Pallas kernels for 11%

profile of v8, /device:TPU:0, one launch (start us, length us, event | category | flops | bytes accessed | tf_op | source)
XLA Modules:
  0.0 26.2 jit_solution(5325939878947697854)
XLA Ops:
  0.6 1.5 %pack.1 = f32[8,40,128]{2,1,0:T(8,128)} custom-call(f32[3,512]{1,0:T(4,128)} %refs_0_.1, f32[3,512]{1,0:T(4,128)} %refs_1_.1, f32[4,128]{1,0:T(4,128)} %bitcast.3, s32[3,256]{1,0:T(4,128)} %refs_3_.1, s32[1,128]{1,0:T(1,128)} %bitcast.4), custom_call_target="tpu_custom_call" | custom-call | tf_op jit(solution)/shard_map/pack/pallas_call | solution.py:392
  2.1 0.0 copy-start.1
  2.1 7.9 %all-to-all-start = ((f32[8,40,128]{2,1,0:T(8,128)}), f32[8,40,128]{2,1,0:T(8,128)S(1)}, u32[]{:S(2)}, u32[]{:S(2)}) async-start(f32[8,40,128]{2,1,0:T(8,128)} %pack.1), calls=%async_computation | async-start | bytes 327680 | tf_op jit(solution)/shard_map/all_to_all | solution.py:462
  10.0 0.0 copy-done.1
  10.0 0.0 copy-start
  10.0 1.0 %copy-done = f32[8,128,128]{2,1,0:T(8,128)S(1)} copy-done((f32[8,128,128]{2,1,0:T(8,128)S(1)}, f32[8,128,128]{2,1,0:T(8,128)}, u32[]{:S(2)}) %copy-start) | copy-done | bytes 524312
  11.0 0.2 fixed.1
  11.2 1.5 %collective-permute-start = (f32[24,128]{1,0:T(8,128)S(1)}, f32[24,128]{1,0:T(8,128)S(1)}, u32[]{:S(2)}, u32[]{:S(2)}) collective-permute-start(f32[24,128]{1,0:T(8,128)S(1)} %get-tuple-element.16.fixed), channel_id=1, source_target_pairs={{0,2},{1,3},{2,6},{3,7},{4,0},{5,1},{6,10},{7,11},{8,4},{9,5},{10,... | collective-permute-start | bytes 36872 | tf_op jit(solution)/shard_map/ppermute | solution.py:468
  12.8 3.6 %all-to-all-done.raw = f32[8,40,128]{2,1,0:T(8,128)S(1)} async-done(((f32[8,40,128]{2,1,0:T(8,128)}), f32[8,40,128]{2,1,0:T(8,128)S(1)}, u32[]{:S(2)}, u32[]{:S(2)}) %all-to-all-start) | async-done | bytes 163872 | tf_op jit(solution)/shard_map/all_to_all | solution.py:462
  16.4 0.9 %compose.1.states = f32[2,32,128]{2,1,0:T(8,128)S(1)} custom-call(f32[8,40,128]{2,1,0:T(8,128)S(1)} %all-to-all-done.raw), custom_call_target="tpu_custom_call" | custom-call | tf_op jit(solution)/shard_map/compose/pallas_call | solution.py:392
  17.3 0.0 collective-permute-done.given
  17.3 0.1 collective-permute-start.2
  17.4 1.6 %collective-permute-start.1 = (f32[56,128]{1,0:T(8,128)S(1)}, f32[56,128]{1,0:T(8,128)S(1)}, u32[]{:S(2)}, u32[]{:S(2)}) collective-permute-start(f32[56,128]{1,0:T(8,128)S(1)} %get-tuple-element.17.refs_0_.mine), channel_id=1, source_target_pairs={{0,1},{1,0},{2,3},{3,2},{4,5},{5,4},{6,7},{7,6},{8,9},{9,8},{10,11... | collective-permute-start | bytes 86024 | tf_op jit(solution)/shard_map/ppermute | solution.py:487
  19.0 0.5 %collective-permute-start.3 = (f32[56,128]{1,0:T(8,128)S(1)}, f32[56,128]{1,0:T(8,128)S(1)}, u32[]{:S(2)}, u32[]{:S(2)}) collective-permute-start(f32[56,128]{1,0:T(8,128)S(1)} %get-tuple-element.19), channel_id=1, source_target_pairs={{0,2},{1,3},{2,0},{3,1},{4,6},{5,7},{6,4},{7,5},{8,10},{9,11},{10,... | collective-permute-start | bytes 86024 | tf_op jit(solution)/shard_map/ppermute | solution.py:489
  19.5 1.5 %collective-permute-start.4 = (f32[56,128]{1,0:T(8,128)S(1)}, f32[56,128]{1,0:T(8,128)S(1)}, u32[]{:S(2)}, u32[]{:S(2)}) collective-permute-start(f32[56,128]{1,0:T(8,128)S(1)} %get-tuple-element.20), channel_id=1, source_target_pairs={{0,2},{1,3},{2,0},{3,1},{4,6},{5,7},{6,4},{7,5},{8,10},{9,11},{10,... | collective-permute-start | bytes 86024 | tf_op jit(solution)/shard_map/ppermute | solution.py:489
  21.0 0.0 collective-permute-done.2.refs_2_
  21.0 0.0 collective-permute-done.1.refs_1_
  21.0 0.4 %near.1 = (f32[8,128]{1,0:T(8,128)S(1)}, f32[4,8,128]{2,1,0:T(8,128)S(1)}) custom-call(f32[56,128]{1,0:T(8,128)S(1)} %get-tuple-element.17.refs_0_.mine, f32[56,128]{1,0:T(8,128)S(1)} %collective-permute-done.1.refs_1_, f32[56,128]{1,0:T(8,128)S(1)} %collective-permute-done.2.refs_2_, bf16[8,128,128]{2,1,0:T(8,128)(2,1)S(1)} %get-tuple-element.21.refs_3_, ...), custom_call_target="tpu_custom_call" | custom-call | tf_op jit(solution)/shard_map/near/pallas_call | solution.py:392
  21.5 0.6 %collective-permute-start.7 = (f32[8,128]{1,0:T(8,128)S(1)}, f32[8,128]{1,0:T(8,128)S(1)}, u32[]{:S(2)}, u32[]{:S(2)}) collective-permute-start(f32[8,128]{1,0:T(8,128)S(1)} %get-tuple-element.26.here), channel_id=1, source_target_pairs={{0,4},{1,2},{2,1},{3,11},{4,0},{5,6},{6,5},{7,8},{8,7},{9,10},{10,... | collective-permute-start | bytes 12296 | tf_op jit(solution)/shard_map/ppermute | solution.py:503
  22.0 0.7 %collective-permute-start.6 = (f32[8,128]{1,0:T(8,128)S(1)}, f32[8,128]{1,0:T(8,128)S(1)}, u32[]{:S(2)}, u32[]{:S(2)}) collective-permute-start(f32[8,128]{1,0:T(8,128)S(1)} %get-tuple-element.26.here), channel_id=1, source_target_pairs={{0,1},{1,0},{2,6},{3,4},{4,3},{5,7},{6,2},{7,5},{8,9},{9,8},{10,14... | collective-permute-start | bytes 12296 | tf_op jit(solution)/shard_map/ppermute | solution.py:505
  22.8 0.0 collective-permute-start.5
  22.8 0.1 collective-permute-done.3.refs_3_
  22.9 0.5 %collective-permute-done.4.refs_4_ = f32[56,128]{1,0:T(8,128)S(1)} collective-permute-done((f32[56,128]{1,0:T(8,128)S(1)}, f32[56,128]{1,0:T(8,128)S(1)}, u32[]{:S(2)}, u32[]{:S(2)}) %collective-permute-start.4) | collective-permute-done | bytes 28704 | tf_op jit(solution)/shard_map/ppermute | solution.py:489
  23.4 1.3 %middle.1 = (f32[3,5,8,128]{3,2,1,0:T(8,128)S(1)}, s32[8,128]{1,0:T(8,128)S(1)}, f32[3,24,128]{2,1,0:T(8,128)S(1)}) custom-call(f32[56,128]{1,0:T(8,128)S(1)} %get-tuple-element.17.refs_0_.mine, f32[56,128]{1,0:T(8,128)S(1)} %collective-permute-done.1.refs_1_, f32[56,128]{1,0:T(8,128)S(1)} %collective-permute-done.2.refs_2_, ...), custom_call_target="tpu_custom_call" | custom-call | tf_op jit(solution)/shard_map/middle/pallas_call | solution.py:392
  24.7 0.5 %collective-permute-done.7.other = f32[8,128]{1,0:T(8,128)S(1)} collective-permute-done((f32[8,128]{1,0:T(8,128)S(1)}, f32[8,128]{1,0:T(8,128)S(1)}, u32[]{:S(2)}, u32[]{:S(2)}) %collective-permute-start.7) | collective-permute-done | bytes 4128 | tf_op jit(solution)/shard_map/ppermute | solution.py:503
  25.1 0.0 collective-permute-done.6.mid
  25.1 0.0 collective-permute-done.5.chip
  25.1 1.1 %last.1 = (f32[3,512]{1,0:T(4,128)}, f32[8,128]{1,0:T(8,128)}) custom-call(f32[56,128]{1,0:T(8,128)S(1)} %get-tuple-element.17.refs_0_.mine, f32[3,5,8,128]{3,2,1,0:T(8,128)S(1)} %get-tuple-element.24.stage, s32[8,128]{1,0:T(8,128)S(1)} %get-tuple-element.25.back, f32[8,128]{1,0:T(8,128)S(1)} %get-tuple-element.26.here, ...), custom_call_target="tpu_custom_call" | custom-call | tf_op jit(solution)/shard_map/last/pallas_call | solution.py:392
  (1 shorter events, 0.0 us)
Async XLA Ops:
  2.1 7.9 %copy-start.1 = (s32[2,1024]{1,0:T(2,128)S(1)}, s32[2,1024]{1,0:T(2,128)}, u32[]{:S(2)}) copy-start(s32[2,1024]{1,0:T(2,128)} %pair.1) | copy-start | bytes 24580
  2.1 14.3 %all-to-all-start = ((f32[8,40,128]{2,1,0:T(8,128)}), f32[8,40,128]{2,1,0:T(8,128)S(1)}, u32[]{:S(2)}, u32[]{:S(2)}) async-start(f32[8,40,128]{2,1,0:T(8,128)} %pack.1), calls=%async_computation | async-start | bytes 327680 | tf_op jit(solution)/shard_map/all_to_all | solution.py:462
  10.0 1.0 %copy-start = (f32[8,128,128]{2,1,0:T(8,128)S(1)}, f32[8,128,128]{2,1,0:T(8,128)}, u32[]{:S(2)}) copy-start(f32[8,128,128]{2,1,0:T(8,128)} %tiles.1) | copy-start | bytes 1572868
  11.2 6.1 %collective-permute-start = (f32[24,128]{1,0:T(8,128)S(1)}, f32[24,128]{1,0:T(8,128)S(1)}, u32[]{:S(2)}, u32[]{:S(2)}) collective-permute-start(f32[24,128]{1,0:T(8,128)S(1)} %get-tuple-element.16.fixed), channel_id=1, source_target_pairs={{0,2},{1,3},{2,6},{3,7},{4,0},{5,1},{6,10},{7,11},{8,4},{9,5},{10,... | collective-permute-start | bytes 36872 | tf_op jit(solution)/shard_map/ppermute | solution.py:468
  17.3 3.7 %collective-permute-start.2 = (f32[56,128]{1,0:T(8,128)S(1)}, f32[56,128]{1,0:T(8,128)S(1)}, u32[]{:S(2)}, u32[]{:S(2)}) collective-permute-start(f32[56,128]{1,0:T(8,128)S(1)} %get-tuple-element.18), channel_id=1, source_target_pairs={{0,3},{1,2},{2,1},{3,0},{4,7},{5,6},{6,5},{7,4},{8,11},{9,10},{10,... | collective-permute-start | bytes 86024 | tf_op jit(solution)/shard_map/ppermute | solution.py:486
  17.4 3.6 %collective-permute-start.1 = (f32[56,128]{1,0:T(8,128)S(1)}, f32[56,128]{1,0:T(8,128)S(1)}, u32[]{:S(2)}, u32[]{:S(2)}) collective-permute-start(f32[56,128]{1,0:T(8,128)S(1)} %get-tuple-element.17.refs_0_.mine), channel_id=1, source_target_pairs={{0,1},{1,0},{2,3},{3,2},{4,5},{5,4},{6,7},{7,6},{8,9},{9,8},{10,11... | collective-permute-start | bytes 86024 | tf_op jit(solution)/shard_map/ppermute | solution.py:487
  19.0 3.9 %collective-permute-start.3 = (f32[56,128]{1,0:T(8,128)S(1)}, f32[56,128]{1,0:T(8,128)S(1)}, u32[]{:S(2)}, u32[]{:S(2)}) collective-permute-start(f32[56,128]{1,0:T(8,128)S(1)} %get-tuple-element.19), channel_id=1, source_target_pairs={{0,2},{1,3},{2,0},{3,1},{4,6},{5,7},{6,4},{7,5},{8,10},{9,11},{10,... | collective-permute-start | bytes 86024 | tf_op jit(solution)/shard_map/ppermute | solution.py:489
  19.5 3.9 %collective-permute-start.4 = (f32[56,128]{1,0:T(8,128)S(1)}, f32[56,128]{1,0:T(8,128)S(1)}, u32[]{:S(2)}, u32[]{:S(2)}) collective-permute-start(f32[56,128]{1,0:T(8,128)S(1)} %get-tuple-element.20), channel_id=1, source_target_pairs={{0,2},{1,3},{2,0},{3,1},{4,6},{5,7},{6,4},{7,5},{8,10},{9,11},{10,... | collective-permute-start | bytes 86024 | tf_op jit(solution)/shard_map/ppermute | solution.py:489
  21.5 3.7 %collective-permute-start.7 = (f32[8,128]{1,0:T(8,128)S(1)}, f32[8,128]{1,0:T(8,128)S(1)}, u32[]{:S(2)}, u32[]{:S(2)}) collective-permute-start(f32[8,128]{1,0:T(8,128)S(1)} %get-tuple-element.26.here), channel_id=1, source_target_pairs={{0,4},{1,2},{2,1},{3,11},{4,0},{5,6},{6,5},{7,8},{8,7},{9,10},{10,... | collective-permute-start | bytes 12296 | tf_op jit(solution)/shard_map/ppermute | solution.py:503
  22.0 3.1 %collective-permute-start.6 = (f32[8,128]{1,0:T(8,128)S(1)}, f32[8,128]{1,0:T(8,128)S(1)}, u32[]{:S(2)}, u32[]{:S(2)}) collective-permute-start(f32[8,128]{1,0:T(8,128)S(1)} %get-tuple-element.26.here), channel_id=1, source_target_pairs={{0,1},{1,0},{2,6},{3,4},{4,3},{5,7},{6,2},{7,5},{8,9},{9,8},{10,14... | collective-permute-start | bytes 12296 | tf_op jit(solution)/shard_map/ppermute | solution.py:505
  22.8 2.3 %collective-permute-start.5 = (f32[8,128]{1,0:T(8,128)S(1)}, f32[8,128]{1,0:T(8,128)S(1)}, u32[]{:S(2)}, u32[]{:S(2)}) collective-permute-start(f32[8,128]{1,0:T(8,128)S(1)} %get-tuple-element.26.here), channel_id=1, source_target_pairs={{0,1},{1,0},{2,3},{3,2},{4,5},{5,4},{6,7},{7,6},{8,9},{9,8},{10,11... | collective-permute-start | bytes 12296 | tf_op jit(solution)/shard_map/ppermute | solution.py:504

commit v9 on v8

--- a/solution.py
+++ b/solution.py
@@ -23,7 +23,6 @@
 RAW = 40
 FIXED = RECORD - FIRST_AT
 BLOCK = 4
-LISTED = (2, 0, 1, 3, 4, 5, 6, 7)
 PARAMS = pltpu.CompilerParams(vmem_limit_bytes=32 * 2**20)
 FROM_HBM = pltpu.CompilerParams(vmem_limit_bytes=63 * 2**20)
 NT = (((1,), (1,)), ((), ()))
@@ -120,12 +119,6 @@
         out[pl.ds(2 * FIELDS + t, 1), :] = diag
 
 
-def place_of(block):
-    if isinstance(block, int):
-        return LISTED.index(block)
-    return sum(jnp.where(block == one, at, 0) for at, one in enumerate(LISTED))
-
-
 def second_part(stride):
     me = lax.axis_index("parts")
     member, kind = me // stride, me % stride
@@ -154,7 +147,7 @@
     step, exists = second_part(stride)
 
     def came_from(part):
-        return raw.at[place_of(part)]
+        return raw.at[(part + 3) % GROUP]
 
     def list_rows(part, level):
         rows = came_from(part)
@@ -458,7 +451,7 @@
         [pltpu.VMEM(one.shape, one.dtype) for one in inputs]
         + [pltpu.SemaphoreType.DMA((5,))],
     )
-    classes = [[r + stride * k for k in LISTED] for r in range(stride)]
+    classes = [[r + stride * ((k - 3) % GROUP) for k in range(GROUP)] for r in range(stride)]
     raw = lax.all_to_all(packed, "parts", 0, 0, axis_index_groups=classes)
 
     half = jax.ShapeDtypeStruct(delassus.shape, jnp.bfloat16)

time: 26.6 us -> 25.5 us (0.959)
  waiting for transfers between devices: 4.72 us -> 3.36 us
  starting transfers between devices: 14.4 us -> 14.7 us
    all_to_all x1, waiting for transfers between devices: 3.65 us -> 2.26 us  [body(): raw = lax.all_to_all(packed, 'parts', 0, 0, axis_index_groups=classes)]
    all_to_all x1, starting transfers between devices: 7.85 us -> 8.3 us  [body(): raw = lax.all_to_all(packed, 'parts', 0, 0, axis_index_groups=classes)]
where the time goes in v9:
time: 25.5 us; the launch traced here: 25.2 us
  starting transfers between devices  14.7 us (58%)
  Pallas kernels  5.35 us (21%)
  waiting for transfers between devices  3.36 us (13%)
  local copies, waits for them, and re-layouts  1.05 us (4%)
  between operations  0.69 us (3%)
    all_to_all x1, starting transfers between devices, body(): raw = lax.all_to_all(packed, 'parts', 0, 0, axis_index_groups=classes)  8.3 us
    pallas_call x7, Pallas kernels, call(): pl.pallas_call(kernel, out_shape=out_shape, in_specs=[pl.BlockSpec(memory...  5.35 us
    all_to_all x1, waiting for transfers between devices, body(): raw = lax.all_to_all(packed, 'parts', 0, 0, axis_index_groups=classes)  2.26 us
    ppermute x2, starting transfers between devices, body(): came = (*near, send(low, perm=beyond), send(high, perm=beyond))  2.03 us
    ppermute x1, starting transfers between devices, body(): given = send(fixed, perm=second_parts(parts, stride))  1.54 us
    ppermute x1, starting transfers between devices, body(): near = (mine, send(mine, perm=within), from_far)  1.44 us
    unnamed x4, local copies, waits for them, and re-layouts  1.05 us
    ppermute x2, waiting for transfers between devices, body(): came = (*near, send(low, perm=beyond), send(high, perm=beyond))  0.76 us
  transfers between devices with their start and end apart: 9, of which 4 were waited for; matrix products, arithmetic and copies ran while one was open for 0% of the time, Pallas kernels for 11%

profile of v9, /device:TPU:0, one launch (start us, length us, event | category | flops | bytes accessed | tf_op | source)
XLA Modules:
  0.0 25.2 jit_solution(8888190378665955734)
XLA Ops:
  0.6 1.5 %pack.1 = f32[8,40,128]{2,1,0:T(8,128)} custom-call(f32[3,512]{1,0:T(4,128)} %refs_0_.1, f32[3,512]{1,0:T(4,128)} %refs_1_.1, f32[4,128]{1,0:T(4,128)} %bitcast.3, s32[3,256]{1,0:T(4,128)} %refs_3_.1, s32[1,128]{1,0:T(1,128)} %bitcast.4), custom_call_target="tpu_custom_call" | custom-call | tf_op jit(solution)/shard_map/pack/pallas_call | solution.py:385
  2.1 0.0 copy-start.1
  2.1 8.3 %all-to-all-start = ((f32[8,40,128]{2,1,0:T(8,128)}), f32[8,40,128]{2,1,0:T(8,128)S(1)}, u32[]{:S(2)}, u32[]{:S(2)}) async-start(f32[8,40,128]{2,1,0:T(8,128)} %pack.1), calls=%async_computation | async-start | bytes 327680 | tf_op jit(solution)/shard_map/all_to_all | solution.py:455
  10.4 0.0 copy-done.1
  10.4 0.0 copy-start
  10.4 1.0 %copy-done = f32[8,128,128]{2,1,0:T(8,128)S(1)} copy-done((f32[8,128,128]{2,1,0:T(8,128)S(1)}, f32[8,128,128]{2,1,0:T(8,128)}, u32[]{:S(2)}) %copy-start) | copy-done | bytes 524312
  11.5 0.2 fixed.1
  11.7 1.5 %collective-permute-start = (f32[24,128]{1,0:T(8,128)S(1)}, f32[24,128]{1,0:T(8,128)S(1)}, u32[]{:S(2)}, u32[]{:S(2)}) collective-permute-start(f32[24,128]{1,0:T(8,128)S(1)} %get-tuple-element.16.fixed), channel_id=1, source_target_pairs={{0,2},{1,3},{2,6},{3,7},{4,0},{5,1},{6,10},{7,11},{8,4},{9,5},{10,... | collective-permute-start | bytes 36872 | tf_op jit(solution)/shard_map/ppermute | solution.py:461
  13.2 2.3 %all-to-all-done.raw = f32[8,40,128]{2,1,0:T(8,128)S(1)} async-done(((f32[8,40,128]{2,1,0:T(8,128)}), f32[8,40,128]{2,1,0:T(8,128)S(1)}, u32[]{:S(2)}, u32[]{:S(2)}) %all-to-all-start) | async-done | bytes 163872 | tf_op jit(solution)/shard_map/all_to_all | solution.py:455
  15.5 0.9 %compose.1.states = f32[2,32,128]{2,1,0:T(8,128)S(1)} custom-call(f32[8,40,128]{2,1,0:T(8,128)S(1)} %all-to-all-done.raw), custom_call_target="tpu_custom_call" | custom-call | tf_op jit(solution)/shard_map/compose/pallas_call | solution.py:385
  16.3 0.0 collective-permute-done.given
  16.4 0.1 collective-permute-start.2
  16.5 1.4 %collective-permute-start.1 = (f32[56,128]{1,0:T(8,128)S(1)}, f32[56,128]{1,0:T(8,128)S(1)}, u32[]{:S(2)}, u32[]{:S(2)}) collective-permute-start(f32[56,128]{1,0:T(8,128)S(1)} %get-tuple-element.17.refs_0_.mine), channel_id=1, source_target_pairs={{0,1},{1,0},{2,3},{3,2},{4,5},{5,4},{6,7},{7,6},{8,9},{9,8},{10,11... | collective-permute-start | bytes 86024 | tf_op jit(solution)/shard_map/ppermute | solution.py:480
  17.9 0.7 %collective-permute-start.3 = (f32[56,128]{1,0:T(8,128)S(1)}, f32[56,128]{1,0:T(8,128)S(1)}, u32[]{:S(2)}, u32[]{:S(2)}) collective-permute-start(f32[56,128]{1,0:T(8,128)S(1)} %get-tuple-element.19), channel_id=1, source_target_pairs={{0,2},{1,3},{2,0},{3,1},{4,6},{5,7},{6,4},{7,5},{8,10},{9,11},{10,... | collective-permute-start | bytes 86024 | tf_op jit(solution)/shard_map/ppermute | solution.py:482
  18.6 1.3 %collective-permute-start.4 = (f32[56,128]{1,0:T(8,128)S(1)}, f32[56,128]{1,0:T(8,128)S(1)}, u32[]{:S(2)}, u32[]{:S(2)}) collective-permute-start(f32[56,128]{1,0:T(8,128)S(1)} %get-tuple-element.20), channel_id=1, source_target_pairs={{0,2},{1,3},{2,0},{3,1},{4,6},{5,7},{6,4},{7,5},{8,10},{9,11},{10,... | collective-permute-start | bytes 86024 | tf_op jit(solution)/shard_map/ppermute | solution.py:482
  19.9 0.0 collective-permute-done.2.refs_2_
  20.0 0.0 collective-permute-done.1.refs_1_
  20.0 0.4 %near.1 = (f32[8,128]{1,0:T(8,128)S(1)}, f32[4,8,128]{2,1,0:T(8,128)S(1)}) custom-call(f32[56,128]{1,0:T(8,128)S(1)} %get-tuple-element.17.refs_0_.mine, f32[56,128]{1,0:T(8,128)S(1)} %collective-permute-done.1.refs_1_, f32[56,128]{1,0:T(8,128)S(1)} %collective-permute-done.2.refs_2_, bf16[8,128,128]{2,1,0:T(8,128)(2,1)S(1)} %get-tuple-element.21.refs_3_, ...), custom_call_target="tpu_custom_call" | custom-call | tf_op jit(solution)/shard_map/near/pallas_call | solution.py:385
  20.4 0.7 %collective-permute-start.7 = (f32[8,128]{1,0:T(8,128)S(1)}, f32[8,128]{1,0:T(8,128)S(1)}, u32[]{:S(2)}, u32[]{:S(2)}) collective-permute-start(f32[8,128]{1,0:T(8,128)S(1)} %get-tuple-element.26.here), channel_id=1, source_target_pairs={{0,4},{1,2},{2,1},{3,11},{4,0},{5,6},{6,5},{7,8},{8,7},{9,10},{10,... | collective-permute-start | bytes 12296 | tf_op jit(solution)/shard_map/ppermute | solution.py:496
  21.0 0.7 %collective-permute-start.6 = (f32[8,128]{1,0:T(8,128)S(1)}, f32[8,128]{1,0:T(8,128)S(1)}, u32[]{:S(2)}, u32[]{:S(2)}) collective-permute-start(f32[8,128]{1,0:T(8,128)S(1)} %get-tuple-element.26.here), channel_id=1, source_target_pairs={{0,1},{1,0},{2,6},{3,4},{4,3},{5,7},{6,2},{7,5},{8,9},{9,8},{10,14... | collective-permute-start | bytes 12296 | tf_op jit(solution)/shard_map/ppermute | solution.py:498
  21.7 0.0 collective-permute-start.5
  21.7 0.1 collective-permute-done.3.refs_3_
  21.8 0.7 %collective-permute-done.4.refs_4_ = f32[56,128]{1,0:T(8,128)S(1)} collective-permute-done((f32[56,128]{1,0:T(8,128)S(1)}, f32[56,128]{1,0:T(8,128)S(1)}, u32[]{:S(2)}, u32[]{:S(2)}) %collective-permute-start.4) | collective-permute-done | bytes 28704 | tf_op jit(solution)/shard_map/ppermute | solution.py:482
  22.5 1.3 %middle.1 = (f32[3,5,8,128]{3,2,1,0:T(8,128)S(1)}, s32[8,128]{1,0:T(8,128)S(1)}, f32[3,24,128]{2,1,0:T(8,128)S(1)}) custom-call(f32[56,128]{1,0:T(8,128)S(1)} %get-tuple-element.17.refs_0_.mine, f32[56,128]{1,0:T(8,128)S(1)} %collective-permute-done.1.refs_1_, f32[56,128]{1,0:T(8,128)S(1)} %collective-permute-done.2.refs_2_, ...), custom_call_target="tpu_custom_call" | custom-call | tf_op jit(solution)/shard_map/middle/pallas_call | solution.py:385
  23.7 0.3 %collective-permute-done.7.other = f32[8,128]{1,0:T(8,128)S(1)} collective-permute-done((f32[8,128]{1,0:T(8,128)S(1)}, f32[8,128]{1,0:T(8,128)S(1)}, u32[]{:S(2)}, u32[]{:S(2)}) %collective-permute-start.7) | collective-permute-done | bytes 4128 | tf_op jit(solution)/shard_map/ppermute | solution.py:496
  24.1 0.0 collective-permute-done.6.mid
  24.1 0.0 collective-permute-done.5.chip
  24.1 1.1 %last.1 = (f32[3,512]{1,0:T(4,128)}, f32[8,128]{1,0:T(8,128)}) custom-call(f32[56,128]{1,0:T(8,128)S(1)} %get-tuple-element.17.refs_0_.mine, f32[3,5,8,128]{3,2,1,0:T(8,128)S(1)} %get-tuple-element.24.stage, s32[8,128]{1,0:T(8,128)S(1)} %get-tuple-element.25.back, f32[8,128]{1,0:T(8,128)S(1)} %get-tuple-element.26.here, ...), custom_call_target="tpu_custom_call" | custom-call | tf_op jit(solution)/shard_map/last/pallas_call | solution.py:385
  (1 shorter events, 0.0 us)
Async XLA Ops:
  2.1 8.3 %copy-start.1 = (s32[2,1024]{1,0:T(2,128)S(1)}, s32[2,1024]{1,0:T(2,128)}, u32[]{:S(2)}) copy-start(s32[2,1024]{1,0:T(2,128)} %pair.1) | copy-start | bytes 24580
  2.1 13.4 %all-to-all-start = ((f32[8,40,128]{2,1,0:T(8,128)}), f32[8,40,128]{2,1,0:T(8,128)S(1)}, u32[]{:S(2)}, u32[]{:S(2)}) async-start(f32[8,40,128]{2,1,0:T(8,128)} %pack.1), calls=%async_computation | async-start | bytes 327680 | tf_op jit(solution)/shard_map/all_to_all | solution.py:455
  10.4 1.0 %copy-start = (f32[8,128,128]{2,1,0:T(8,128)S(1)}, f32[8,128,128]{2,1,0:T(8,128)}, u32[]{:S(2)}) copy-start(f32[8,128,128]{2,1,0:T(8,128)} %tiles.1) | copy-start | bytes 1572868
  11.7 4.7 %collective-permute-start = (f32[24,128]{1,0:T(8,128)S(1)}, f32[24,128]{1,0:T(8,128)S(1)}, u32[]{:S(2)}, u32[]{:S(2)}) collective-permute-start(f32[24,128]{1,0:T(8,128)S(1)} %get-tuple-element.16.fixed), channel_id=1, source_target_pairs={{0,2},{1,3},{2,6},{3,7},{4,0},{5,1},{6,10},{7,11},{8,4},{9,5},{10,... | collective-permute-start | bytes 36872 | tf_op jit(solution)/shard_map/ppermute | solution.py:461
  16.4 3.6 %collective-permute-start.2 = (f32[56,128]{1,0:T(8,128)S(1)}, f32[56,128]{1,0:T(8,128)S(1)}, u32[]{:S(2)}, u32[]{:S(2)}) collective-permute-start(f32[56,128]{1,0:T(8,128)S(1)} %get-tuple-element.18), channel_id=1, source_target_pairs={{0,3},{1,2},{2,1},{3,0},{4,7},{5,6},{6,5},{7,4},{8,11},{9,10},{10,... | collective-permute-start | bytes 86024 | tf_op jit(solution)/shard_map/ppermute | solution.py:479
  16.5 3.5 %collective-permute-start.1 = (f32[56,128]{1,0:T(8,128)S(1)}, f32[56,128]{1,0:T(8,128)S(1)}, u32[]{:S(2)}, u32[]{:S(2)}) collective-permute-start(f32[56,128]{1,0:T(8,128)S(1)} %get-tuple-element.17.refs_0_.mine), channel_id=1, source_target_pairs={{0,1},{1,0},{2,3},{3,2},{4,5},{5,4},{6,7},{7,6},{8,9},{9,8},{10,11... | collective-permute-start | bytes 86024 | tf_op jit(solution)/shard_map/ppermute | solution.py:480
  17.9 3.9 %collective-permute-start.3 = (f32[56,128]{1,0:T(8,128)S(1)}, f32[56,128]{1,0:T(8,128)S(1)}, u32[]{:S(2)}, u32[]{:S(2)}) collective-permute-start(f32[56,128]{1,0:T(8,128)S(1)} %get-tuple-element.19), channel_id=1, source_target_pairs={{0,2},{1,3},{2,0},{3,1},{4,6},{5,7},{6,4},{7,5},{8,10},{9,11},{10,... | collective-permute-start | bytes 86024 | tf_op jit(solution)/shard_map/ppermute | solution.py:482
  18.6 3.9 %collective-permute-start.4 = (f32[56,128]{1,0:T(8,128)S(1)}, f32[56,128]{1,0:T(8,128)S(1)}, u32[]{:S(2)}, u32[]{:S(2)}) collective-permute-start(f32[56,128]{1,0:T(8,128)S(1)} %get-tuple-element.20), channel_id=1, source_target_pairs={{0,2},{1,3},{2,0},{3,1},{4,6},{5,7},{6,4},{7,5},{8,10},{9,11},{10,... | collective-permute-start | bytes 86024 | tf_op jit(solution)/shard_map/ppermute | solution.py:482
  20.4 3.7 %collective-permute-start.7 = (f32[8,128]{1,0:T(8,128)S(1)}, f32[8,128]{1,0:T(8,128)S(1)}, u32[]{:S(2)}, u32[]{:S(2)}) collective-permute-start(f32[8,128]{1,0:T(8,128)S(1)} %get-tuple-element.26.here), channel_id=1, source_target_pairs={{0,4},{1,2},{2,1},{3,11},{4,0},{5,6},{6,5},{7,8},{8,7},{9,10},{10,... | collective-permute-start | bytes 12296 | tf_op jit(solution)/shard_map/ppermute | solution.py:496
  21.0 3.0 %collective-permute-start.6 = (f32[8,128]{1,0:T(8,128)S(1)}, f32[8,128]{1,0:T(8,128)S(1)}, u32[]{:S(2)}, u32[]{:S(2)}) collective-permute-start(f32[8,128]{1,0:T(8,128)S(1)} %get-tuple-element.26.here), channel_id=1, source_target_pairs={{0,1},{1,0},{2,6},{3,4},{4,3},{5,7},{6,2},{7,5},{8,9},{9,8},{10,14... | collective-permute-start | bytes 12296 | tf_op jit(solution)/shard_map/ppermute | solution.py:498
  21.7 2.4 %collective-permute-start.5 = (f32[8,128]{1,0:T(8,128)S(1)}, f32[8,128]{1,0:T(8,128)S(1)}, u32[]{:S(2)}, u32[]{:S(2)}) collective-permute-start(f32[8,128]{1,0:T(8,128)S(1)} %get-tuple-element.26.here), channel_id=1, source_target_pairs={{0,1},{1,0},{2,3},{3,2},{4,5},{5,4},{6,7},{7,6},{8,9},{9,8},{10,11... | collective-permute-start | bytes 12296 | tf_op jit(solution)/shard_map/ppermute | solution.py:497
